TPU v7x, 32 devices: a whole 2x2x4 slice. The times are simulated.
32 devices in a mesh: row: 8 (over z, x), col: 4 (over y, core).
Axes of the slice: x: 2, y: 2, z: 4, core: 2. Of those that a mesh axis runs over, the one named last changes fastest.
Arguments:
- features: bfloat16 [4, 1024, 256], P('col', 'row'), may hold values from -6 to 6
- weight: bfloat16 [256, 256], replicated, may hold values from -0.375 to 0.375
- tile_values: bfloat16 [8, 4, 32, 128, 128], P('row', 'col'), may hold values from -0.125 to 0.125
- tile_slots: int32 [8, 4, 32], P('row', 'col'), may hold values from 0 to 31, as said below
- tile_counts: int32 [8, 4], P('row', 'col'), may hold values from 1 to 32, as said below
- cotangent: bfloat16 [8, 512, 256], P('row', 'col'), may hold values from -6 to 6
Outputs:
- layer_out: bfloat16 [8, 512, 256], P('row', 'col')
- feature_grad: bfloat16 [4, 1024, 256], P('col', 'row')
- weight_grad: float32 [256, 256], replicated
Inputs may be any that keep to these rules, and one draw needn't show every extreme that they name: `tile_slots`: within one grid block the 32 slot positions are distinct; slots from tile_counts on carry no edges. `tile_counts`: some grid block uses all 32 slots.
All inputs are finite; a program needn't handle non-finite values.
Results may differ from a plain program's by a relative error of at most 0.022.
Values may be sent and summed in bfloat16 or wider, within the bound.
No kernel may reach another device: no remote copies, remote signals or barrier semaphores. Data moves between devices by JAX's collectives and lax.ppermute only.
A program may use at most 64 MiB of HBM per device.

v0:
```python
import math

import jax
import jax.numpy as jnp
from jax import lax
from jax.experimental import pallas as pl
from jax.experimental.pallas import tpu as pltpu
from jax.sharding import PartitionSpec as P

F32 = jnp.float32
BF16 = jnp.bfloat16
VMEM = pl.BlockSpec(memory_space=pltpu.VMEM)
SMEM = pl.BlockSpec(memory_space=pltpu.SMEM)
ANY = pl.BlockSpec(memory_space=pl.ANY)


def hint(microseconds):
    return pl.CostEstimate(
        flops=int(microseconds * 1e9), bytes_accessed=int(microseconds * 3.6e6), transcendentals=0
    )


def shape(*dims, dtype=BF16):
    return jax.ShapeDtypeStruct(dims, dtype)


def rows_of(index, slab):
    return pl.ds(pl.multiple_of(index * slab, slab), slab)


def summed(refs):
    total = refs[0][...].astype(F32)
    for ref in refs[1:]:
        total = total + ref[...].astype(F32)
    return total


def dense_kernel(slots_ref, count_ref, tiles_ref, adj_ref, sems):
    slot_count, tile, _ = tiles_ref.shape
    col_tiles = adj_ref.shape[1] // tile
    live = jnp.minimum(count_ref[0], slot_count)
    adj_ref[...] = jnp.zeros_like(adj_ref)

    def copy(k):
        slot = slots_ref[k]
        row = pl.multiple_of((slot // col_tiles) * tile, tile)
        col = pl.multiple_of((slot % col_tiles) * tile, tile)
        place = adj_ref.at[pl.ds(row, tile), pl.ds(col, tile)]
        return pltpu.make_async_copy(tiles_ref.at[k], place, sems.at[k])

    def start(k, carry):
        copy(k).start()
        return carry

    def wait(k, carry):
        copy(k).wait()
        return carry

    lax.fori_loop(0, live, start, 0)
    lax.fori_loop(0, live, wait, 0)


def stack_kernel(*refs):
    out_ref = refs[-1]
    for k in range(out_ref.shape[0]):
        out_ref[k] = refs[k][...]


def place_cots(me_ref, near_ref, other_ref, out_ref):
    slab = near_ref.shape[1]
    for k in range(near_ref.shape[0]):
        out_ref[rows_of(me_ref[1] ^ (2 * k), slab), :] = near_ref[k]
        out_ref[rows_of(me_ref[1] ^ (2 * k + 1), slab), :] = other_ref[k]


def forward_kernel(me_ref, adj_ref, near_ref, other_ref, *refs, half):
    pair_refs, (*out_refs, both_ref, column, cots, part, grad) = refs[:half], refs[half:]
    slab = near_ref.shape[1]
    others = len(out_refs) // 2
    piece = both_ref.shape[0] - slab
    place_cots(me_ref, near_ref, other_ref, cots)
    for k, ref in enumerate(pair_refs[::-1]):
        column[rows_of(me_ref[0] ^ k, slab), :] = ref[0]
        column[rows_of(me_ref[0] ^ k ^ half, slab), :] = ref[1]
    product = jnp.dot(adj_ref[...], column[...], preferred_element_type=F32).astype(BF16)
    part[...] = product
    grad[...] = lax.dot_general(
        product, cots[...], (((0,), (0,)), ((), ())), preferred_element_type=F32
    ).astype(BF16)
    for n in range(others):
        k = n + 1 if n else 0
        out_refs[n][...] = part[rows_of(me_ref[1] ^ k, slab), :]
        out_refs[others + n][...] = grad[rows_of(me_ref[1] ^ k, piece), :]
    both_ref[:slab, :] = part[rows_of(me_ref[1] ^ 1, slab), :]
    both_ref[slab:, :] = grad[rows_of(me_ref[1] ^ 1, piece), :]


def backward_kernel(me_ref, adj_ref, near_ref, other_ref, *refs):
    *pair_refs, cots, total = refs
    half, slab = len(pair_refs), pair_refs[0].shape[1]
    place_cots(me_ref, near_ref, other_ref, cots)
    total[...] = lax.dot_general(
        adj_ref[...], cots[...], (((0,), (0,)), ((), ())), preferred_element_type=F32
    ).astype(BF16)
    for k, ref in enumerate(pair_refs):
        ref[0] = total[rows_of(me_ref[0] ^ k, slab), :]
        ref[1] = total[rows_of(me_ref[0] ^ k ^ half, slab), :]


def pair_sum_kernel(*refs):
    *pair_refs, keep_ref, send_ref = refs
    total = summed(pair_refs)
    keep_ref[...] = total[0]
    send_ref[...] = total[1].astype(BF16)


def weighted(weight_ref, term_refs, contract):
    return lax.dot_general(
        summed(term_refs).astype(BF16),
        weight_ref[...],
        (((1,), (contract,)), ((), ())),
        preferred_element_type=F32,
    ).astype(BF16)


def output_kernel(weight_ref, first_ref, *refs):
    *term_refs, out_ref = refs
    first_ref = first_ref.at[: out_ref.shape[0], :]
    out_ref[...] = weighted(weight_ref, [first_ref, *term_refs], 0)


def col_kernel(first_ref, *refs, terms):
    out_ref = refs[-1]
    first_ref = first_ref.at[first_ref.shape[0] - out_ref.shape[0] :, :]
    out_ref[...] = summed([first_ref, *refs[:terms]]).astype(BF16)


def hold_kernel(*refs):
    count = len(refs) // 2
    for src_ref, dst_ref in zip(refs[:count], refs[count + 1 :]):
        dst_ref[...] = src_ref[...]


def near_kernel(send_ref, *refs, terms):
    slab = send_ref.shape[0]
    refs[-1][:slab, :] = send_ref[...]
    refs[-1][slab:, :] = summed(refs[:terms]).astype(BF16)


def row_kernel(held_ref, got_ref, out_ref):
    slab = held_ref.shape[0] - out_ref.shape[0]
    out_ref[...] = summed([held_ref.at[slab:, :], got_ref.at[slab:, :]]).astype(BF16)


def finish_kernel(me_ref, weight_ref, keep_ref, got_ref, *refs, scale):
    *piece_refs, feature_ref, grad_ref = refs
    got_ref = got_ref.at[: feature_ref.shape[0], :]
    piece = piece_refs[0].shape[0]
    for k, ref in enumerate(piece_refs):
        grad_ref[rows_of(me_ref[1] ^ k, piece), :] = ref[...].astype(F32) * scale
    feature_ref[...] = weighted(weight_ref, [keep_ref, got_ref], 1)


def swap(array, axis, distance):
    pairs = [(i, i ^ distance) for i in range(lax.axis_size(axis))]
    return lax.ppermute(array, axis, pairs)


def exchange(chunks, axis, stride=1):
    return [chunks[0]] + [swap(chunks[k], axis, k * stride) for k in range(1, len(chunks))]


def body(features, weight, tile_values, tile_slots, tile_counts, cotangent):
    row_devices = lax.axis_size("row")
    col_devices = lax.axis_size("col")
    half = row_devices // 2
    slots, tile = tile_values.shape[2:4]
    slab, width = features.shape[1:]
    rows, cols = col_devices * slab, row_devices * slab
    piece = width // col_devices
    me = jnp.stack([lax.axis_index("row"), lax.axis_index("col")]).astype(jnp.int32)

    def call(kernel, name, out_shape, in_specs, args, scratch=(), micros=None):
        many = isinstance(out_shape, list)
        return pl.pallas_call(
            kernel,
            out_shape=out_shape,
            in_specs=in_specs,
            out_specs=[VMEM] * len(out_shape) if many else VMEM,
            scratch_shapes=scratch,
            compiler_params=pltpu.CompilerParams(
                vmem_limit_bytes=min(8 * 2**20 + 6 * rows * cols, 56 * 2**20)
            ),
            cost_estimate=None if micros is None else hint(micros),
            name=name,
        )(*args)

    own = features[0]
    far = swap(own, "row", half)
    adj = call(
        dense_kernel, "dense", shape(rows, cols), [SMEM, SMEM, ANY],
        (tile_slots[0, 0], tile_counts[0], tile_values[0, 0]),
        scratch=[pltpu.SemaphoreType.DMA((slots,))],
    )

    def hold(arrays, after, name):
        return call(
            hold_kernel, name, [shape(slab, width)] * len(arrays),
            [VMEM] * len(arrays) + [ANY], (*arrays, after),
        )

    def stack(arrays, name, after=()):
        return call(
            stack_kernel, name, shape(len(arrays), slab, width),
            [VMEM] * len(arrays) + [ANY] * len(after), (*arrays, *after), micros=3,
        )

    kept = hold([own, cotangent[0]], tile_counts, "own")
    pair = stack([kept[0], far], "pair")
    features_got = exchange([pair] * half, "row")
    cot_near = stack(
        [kept[1]] + exchange([cotangent[0]] * (col_devices // 2), "col", 2)[1:], "cot_near"
    )
    cot_other = swap(cot_near, "col", 1)

    outs = call(
        lambda *refs: forward_kernel(*refs, half=half), "forward",
        [shape(slab, width)] * (col_devices - 1)
        + [shape(piece, width)] * (col_devices - 1)
        + [shape(slab + piece, width)],
        [SMEM] + [VMEM] * (3 + half), (me, adj, cot_near, cot_other, *features_got[::-1]),
        scratch=[
            pltpu.VMEM((cols, width), BF16),
            pltpu.VMEM((rows, width), BF16),
            pltpu.VMEM((rows, width), BF16),
            pltpu.VMEM((width, width), BF16),
        ],
    )
    column_pairs = call(
        backward_kernel, "backward", [shape(2, slab, width)] * half,
        [SMEM] + [VMEM] * 3, (me, adj, cot_near, cot_other),
        scratch=[pltpu.VMEM((rows, width), BF16), pltpu.VMEM((cols, width), BF16)],
    )
    column_keep, column_send = call(
        pair_sum_kernel, "pair_sum", [shape(slab, width, dtype=F32), shape(slab, width)],
        [VMEM] * half, exchange(column_pairs, "row")[::-1], micros=5,
    )
    chunks, pieces = outs[: col_devices - 1], outs[col_devices - 1 : -1]
    first = swap(outs[-1], "col", 1)

    def fetch(arrays):
        return [arrays[0]] + [swap(arrays[k - 1], "col", k) for k in range(2, col_devices)]

    grad_col = call(
        lambda *refs: col_kernel(*refs, terms=col_devices - 1), "grad_col", shape(piece, width),
        [VMEM] * col_devices + [ANY], (first, *fetch(pieces), column_send),
    )
    near_terms = exchange([grad_col] * half, "row")
    row_got = fetch([chunks[0], *hold(chunks[1:], near_terms[3], "hold_chunks")])
    both = call(
        lambda *refs: near_kernel(*refs, terms=half), "grad_near", shape(slab + piece, width),
        [VMEM] * (1 + half), (column_send, *near_terms),
    )
    both_far = swap(both, "row", half)
    grad_row = call(
        row_kernel, "grad_row", shape(piece, width), [VMEM] * 2, (both, both_far)
    )
    scale = 1.0 / math.sqrt(row_devices * col_devices * slab)
    layer_out = call(
        output_kernel, "layer_out", shape(slab, width),
        [VMEM] * (1 + col_devices), (weight, first, *row_got),
    )
    feature_grad, weight_grad = call(
        lambda *refs: finish_kernel(*refs, scale=scale), "finish",
        [shape(slab, width), shape(width, width, dtype=F32)],
        [SMEM] + [VMEM] * (3 + col_devices),
        (me, weight, column_keep, both_far, *exchange([grad_row] * col_devices, "col")),
    )
    return (layer_out[None], feature_grad[None], weight_grad)


def solution(mesh):
    placed = (
        P("col", "row", None),
        P(),
        P("row", "col", None, None, None),
        P("row", "col", None),
        P("row", "col"),
        P("row", "col", None),
    )
    return jax.shard_map(
        body,
        mesh=mesh,
        in_specs=placed,
        out_specs=(P("row", "col", None), P("col", "row", None), P()),
        check_vma=False,
    )
```

profile of v0, /device:TPU:0, one launch (start us, length us, event | category | flops | bytes accessed | tf_op | source)
XLA Modules:
  0.0 45.7 jit_solution(13017066188027335111)
XLA Ops:
  0.6 3.0 %collective-permute-start = (bf16[128,256]{1,0:T(8,128)(2,1)}, bf16[128,256]{1,0:T(8,128)(2,1)S(1)}, u32[]{:S(2)}, u32[]{:S(2)}) collective-permute-start(bf16[128,256]{1,0:T(8,128)(2,1)} %bitcast.11), channel_id=1, source_target_pairs={{0,2},{1,3},{2,0},{3,1},{4,6},{5,7},{6,4},{7,5},{8,10},{9,11},{10,... | collective-permute-start | bytes 196616 | tf_op jit(solution)/shard_map/ppermute | solution.py:166
  3.7 2.6 %collective-permute-start.2 = (bf16[128,256]{1,0:T(8,128)(2,1)}, bf16[128,256]{1,0:T(8,128)(2,1)S(1)}, u32[]{:S(2)}, u32[]{:S(2)}) collective-permute-start(bf16[128,256]{1,0:T(8,128)(2,1)} %bitcast.13), channel_id=1, source_target_pairs={{0,16},{4,20},{8,24},{12,28},{16,0},{20,4},{24,8},{28,12},{1,17},{... | collective-permute-start | bytes 196616 | tf_op jit(solution)/shard_map/ppermute | solution.py:166
  6.9 0.8 %copy-done.2 = bf16[1,128,256]{2,1,0:T(8,128)(2,1)S(1)} copy-done((bf16[1,128,256]{2,1,0:T(8,128)(2,1)S(1)}, bf16[1,128,256]{2,1,0:T(8,128)(2,1)}, u32[]{:S(2)}) %copy-start.2) | copy-done | bytes 65560
  7.7 0.8 %copy-done.3 = bf16[1,128,256]{2,1,0:T(8,128)(2,1)S(1)} copy-done((bf16[1,128,256]{2,1,0:T(8,128)(2,1)S(1)}, bf16[1,128,256]{2,1,0:T(8,128)(2,1)}, u32[]{:S(2)}) %copy-start.3) | copy-done | bytes 65560
  8.6 0.0 collective-permute-done.refs_1_
  8.6 0.1 collective-permute-start.1
  8.7 0.6 %collective-permute-done.2.refs_1_ = bf16[128,256]{1,0:T(8,128)(2,1)S(1)} collective-permute-done((bf16[128,256]{1,0:T(8,128)(2,1)}, bf16[128,256]{1,0:T(8,128)(2,1)S(1)}, u32[]{:S(2)}, u32[]{:S(2)}) %collective-permute-start.2) | collective-permute-done | bytes 65568 | tf_op jit(solution)/shard_map/ppermute | solution.py:166
  9.4 2.3 %collective-permute-start.3 = (bf16[2,128,256]{2,1,0:T(8,128)(2,1)S(1)}, bf16[2,128,256]{2,1,0:T(8,128)(2,1)S(1)}, u32[]{:S(2)}, u32[]{:S(2)}) collective-permute-start(bf16[2,128,256]{2,1,0:T(8,128)(2,1)S(1)} %pair.1.refs_7_), channel_id=1, source_target_pairs={{0,12},{4,8},{8,4},{12,0},{16,28},{20,24},{24,20},{28,16},{1,13},{... | collective-permute-start | bytes 393224 | tf_op jit(solution)/shard_map/ppermute | solution.py:166
  11.6 0.1 pad_add_fusion.refs_0_.me_ref
  11.7 0.7 %collective-permute-start.4 = (bf16[2,128,256]{2,1,0:T(8,128)(2,1)S(1)}, bf16[2,128,256]{2,1,0:T(8,128)(2,1)S(1)}, u32[]{:S(2)}, u32[]{:S(2)}) collective-permute-start(bf16[2,128,256]{2,1,0:T(8,128)(2,1)S(1)} %pair.1.refs_7_), channel_id=1, source_target_pairs={{0,8},{4,12},{8,0},{12,4},{16,24},{20,28},{24,16},{28,20},{1,9},{5... | collective-permute-start | bytes 393224 | tf_op jit(solution)/shard_map/ppermute | solution.py:166
  12.4 0.5 %collective-permute-start.5 = (bf16[2,128,256]{2,1,0:T(8,128)(2,1)S(1)}, bf16[2,128,256]{2,1,0:T(8,128)(2,1)S(1)}, u32[]{:S(2)}, u32[]{:S(2)}) collective-permute-start(bf16[2,128,256]{2,1,0:T(8,128)(2,1)S(1)} %pair.1.refs_7_), channel_id=1, source_target_pairs={{0,4},{4,0},{8,12},{12,8},{16,20},{20,16},{24,28},{28,24},{1,5},{5... | collective-permute-start | bytes 393224 | tf_op jit(solution)/shard_map/ppermute | solution.py:166
  13.0 0.7 %copy-done.4 = s32[1,1,32]{2,1,0:T(1,128)S(1)} copy-done((s32[1,1,32]{2,1,0:T(1,128)S(1)}, s32[1,1,32]{2,1,0:T(1,128)}, u32[]{:S(2)}) %copy-start.4) | copy-done | bytes 152
  13.6 1.5 %dense.1.refs_1_.adj_ref = bf16[512,1024]{1,0:T(8,128)(2,1)S(1)} custom-call(s32[32]{0:T(128)S(1)} %bitcast.15, s32[1]{0:T(128)} %bitcast.9.count_ref, bf16[32,128,128]{2,1,0:T(8,128)(2,1)S(1)} %bitcast.10), custom_call_target="tpu_custom_call" | custom-call | tf_op jit(solution)/shard_map/dense/pallas_call | solution.py:185
  15.1 0.0 collective-permute-done.1.refs_3_.other_ref
  15.1 1.1 %backward.1 = (bf16[2,128,256]{2,1,0:T(8,128)(2,1)S(1)}, bf16[2,128,256]{2,1,0:T(8,128)(2,1)S(1)}, bf16[2,128,256]{2,1,0:T(8,128)(2,1)S(1)}, bf16[2,128,256]{2,1,0:T(8,128)(2,1)S(1)}) custom-call(s32[2]{0:T(128)S(1)} %pad_add_fusion.refs_0_.me_ref, bf16[512,1024]{1,0:T(8,128)(2,1)S(1)} %dense.1.refs_1_.adj_ref, ...), custom_call_target="tpu_custom_call" | custom-call | tf_op jit(solution)/shard_map/backward/pallas_call | solution.py:185
  16.2 2.0 %collective-permute-start.9 = (bf16[2,128,256]{2,1,0:T(8,128)(2,1)S(1)}, bf16[2,128,256]{2,1,0:T(8,128)(2,1)S(1)}, u32[]{:S(2)}, u32[]{:S(2)}) collective-permute-start(bf16[2,128,256]{2,1,0:T(8,128)(2,1)S(1)} %get-tuple-element.31), channel_id=1, source_target_pairs={{0,12},{4,8},{8,4},{12,0},{16,28},{20,24},{24,20},{28,16},{1,13},{... | collective-permute-start | bytes 393224 | tf_op jit(solution)/shard_map/ppermute | solution.py:166
  18.2 1.1 %collective-permute-start.10 = (bf16[2,128,256]{2,1,0:T(8,128)(2,1)S(1)}, bf16[2,128,256]{2,1,0:T(8,128)(2,1)S(1)}, u32[]{:S(2)}, u32[]{:S(2)}) collective-permute-start(bf16[2,128,256]{2,1,0:T(8,128)(2,1)S(1)} %get-tuple-element.32), channel_id=1, source_target_pairs={{0,8},{4,12},{8,0},{12,4},{16,24},{20,28},{24,16},{28,20},{1,9},{5... | collective-permute-start | bytes 393224 | tf_op jit(solution)/shard_map/ppermute | solution.py:166
  19.3 0.0 collective-permute-done.3.refs_4_
  19.3 0.5 %collective-permute-start.11 = (bf16[2,128,256]{2,1,0:T(8,128)(2,1)S(1)}, bf16[2,128,256]{2,1,0:T(8,128)(2,1)S(1)}, u32[]{:S(2)}, u32[]{:S(2)}) collective-permute-start(bf16[2,128,256]{2,1,0:T(8,128)(2,1)S(1)} %get-tuple-element.33), channel_id=1, source_target_pairs={{0,4},{4,0},{8,12},{12,8},{16,20},{20,16},{24,28},{28,24},{1,5},{5... | collective-permute-start | bytes 393224 | tf_op jit(solution)/shard_map/ppermute | solution.py:166
  19.8 1.3 %forward.1 = (bf16[128,256]{1,0:T(8,128)(2,1)S(1)}, bf16[128,256]{1,0:T(8,128)(2,1)S(1)}, bf16[128,256]{1,0:T(8,128)(2,1)S(1)}, bf16[64,256]{1,0:T(8,128)(2,1)S(...) custom-call(s32[2]{0:T(128)S(1)} %pad_add_fusion.refs_0_.me_ref, ...), custom_call_target="tpu_custom_call" | custom-call | tf_op jit(solution)/shard_map/forward/pallas_call | solution.py:185
  21.1 0.1 collective-permute-start.6
  21.2 0.4 collective-permute-start.7
  21.6 1.2 %collective-permute-done.9.refs_0_ = bf16[2,128,256]{2,1,0:T(8,128)(2,1)S(1)} collective-permute-done((bf16[2,128,256]{2,1,0:T(8,128)(2,1)S(1)}, bf16[2,128,256]{2,1,0:T(8,128)(2,1)S(1)}, u32[]{:S(2)}, u32[]{:S(2)}) %collective-permute-start.9) | collective-permute-done | bytes 131104 | tf_op jit(solution)/shard_map/ppermute | solution.py:166
  22.8 0.2 collective-permute-start.8
  23.1 1.1 %collective-permute-done.10.refs_1_ = bf16[2,128,256]{2,1,0:T(8,128)(2,1)S(1)} collective-permute-done((bf16[2,128,256]{2,1,0:T(8,128)(2,1)S(1)}, bf16[2,128,256]{2,1,0:T(8,128)(2,1)S(1)}, u32[]{:S(2)}, u32[]{:S(2)}) %collective-permute-start.10) | collective-permute-done | bytes 131104 | tf_op jit(solution)/shard_map/ppermute | solution.py:166
  24.2 0.1 collective-permute-done.11.refs_2_
  24.3 0.1 pair_sum.1
  24.4 0.8 %collective-permute-done.7.refs_2_ = bf16[64,256]{1,0:T(8,128)(2,1)S(1)} collective-permute-done((bf16[64,256]{1,0:T(8,128)(2,1)S(1)}, bf16[64,256]{1,0:T(8,128)(2,1)S(1)}, u32[]{:S(2)}, u32[]{:S(2)}) %collective-permute-start.7) | collective-permute-done | bytes 32800 | tf_op jit(solution)/shard_map/ppermute | solution.py:166
  25.2 1.0 %collective-permute-done.8.refs_3_ = bf16[64,256]{1,0:T(8,128)(2,1)S(1)} collective-permute-done((bf16[64,256]{1,0:T(8,128)(2,1)S(1)}, bf16[64,256]{1,0:T(8,128)(2,1)S(1)}, u32[]{:S(2)}, u32[]{:S(2)}) %collective-permute-start.8) | collective-permute-done | bytes 32800 | tf_op jit(solution)/shard_map/ppermute | solution.py:166
  26.2 2.5 %collective-permute-start.12 = (bf16[64,256]{1,0:T(8,128)(2,1)S(1)}, bf16[64,256]{1,0:T(8,128)(2,1)S(1)}, u32[]{:S(2)}, u32[]{:S(2)}) collective-permute-start(bf16[64,256]{1,0:T(8,128)(2,1)S(1)} %grad_col.1.refs_1_), channel_id=1, source_target_pairs={{0,12},{4,8},{8,4},{12,0},{16,28},{20,24},{24,20},{28,16},{1,13},{... | collective-permute-start | bytes 98312 | tf_op jit(solution)/shard_map/ppermute | solution.py:166
  28.6 0.6 %collective-permute-start.15 = (bf16[64,256]{1,0:T(8,128)(2,1)S(1)}, bf16[64,256]{1,0:T(8,128)(2,1)S(1)}, u32[]{:S(2)}, u32[]{:S(2)}) collective-permute-start(bf16[64,256]{1,0:T(8,128)(2,1)S(1)} %grad_col.1.refs_1_), channel_id=1, source_target_pairs={{0,4},{4,0},{8,12},{12,8},{16,20},{20,16},{24,28},{28,24},{1,5},{5... | collective-permute-start | bytes 98312 | tf_op jit(solution)/shard_map/ppermute | solution.py:166
  29.2 0.5 %collective-permute-start.16 = (bf16[64,256]{1,0:T(8,128)(2,1)S(1)}, bf16[64,256]{1,0:T(8,128)(2,1)S(1)}, u32[]{:S(2)}, u32[]{:S(2)}) collective-permute-start(bf16[64,256]{1,0:T(8,128)(2,1)S(1)} %grad_col.1.refs_1_), channel_id=1, source_target_pairs={{0,8},{4,12},{8,0},{12,4},{16,24},{20,28},{24,16},{28,20},{1,9},{5... | collective-permute-start | bytes 98312 | tf_op jit(solution)/shard_map/ppermute | solution.py:166
  29.7 1.3 %collective-permute-done.12.refs_2_.refs_4_ = bf16[64,256]{1,0:T(8,128)(2,1)S(1)} collective-permute-done((bf16[64,256]{1,0:T(8,128)(2,1)S(1)}, bf16[64,256]{1,0:T(8,128)(2,1)S(1)}, u32[]{:S(2)}, u32[]{:S(2)}) %collective-permute-start.12) | collective-permute-done | bytes 32800 | tf_op jit(solution)/shard_map/ppermute | solution.py:166
  31.1 1.5 %collective-permute-done.15.refs_2_ = bf16[64,256]{1,0:T(8,128)(2,1)S(1)} collective-permute-done((bf16[64,256]{1,0:T(8,128)(2,1)S(1)}, bf16[64,256]{1,0:T(8,128)(2,1)S(1)}, u32[]{:S(2)}, u32[]{:S(2)}) %collective-permute-start.15) | collective-permute-done | bytes 32800 | tf_op jit(solution)/shard_map/ppermute | solution.py:166
  32.6 0.6 %collective-permute-done.16.refs_3_ = bf16[64,256]{1,0:T(8,128)(2,1)S(1)} collective-permute-done((bf16[64,256]{1,0:T(8,128)(2,1)S(1)}, bf16[64,256]{1,0:T(8,128)(2,1)S(1)}, u32[]{:S(2)}, u32[]{:S(2)}) %collective-permute-start.16) | collective-permute-done | bytes 32800 | tf_op jit(solution)/shard_map/ppermute | solution.py:166
  33.2 2.8 %collective-permute-start.17 = (bf16[192,256]{1,0:T(8,128)(2,1)S(1)}, bf16[192,256]{1,0:T(8,128)(2,1)S(1)}, u32[]{:S(2)}, u32[]{:S(2)}) collective-permute-start(bf16[192,256]{1,0:T(8,128)(2,1)S(1)} %grad_near.1.held_ref), channel_id=1, source_target_pairs={{0,16},{4,20},{8,24},{12,28},{16,0},{20,4},{24,8},{28,12},{1,17},{... | collective-permute-start | bytes 294920 | tf_op jit(solution)/shard_map/ppermute | solution.py:166
  36.0 0.0 copy-start.1
  36.0 0.8 %collective-permute-start.13 = (bf16[128,256]{1,0:T(8,128)(2,1)S(1)}, bf16[128,256]{1,0:T(8,128)(2,1)S(1)}, u32[]{:S(2)}, u32[]{:S(2)}) collective-permute-start(bf16[128,256]{1,0:T(8,128)(2,1)S(1)} %get-tuple-element.36), channel_id=1, source_target_pairs={{0,2},{1,3},{2,0},{3,1},{4,6},{5,7},{6,4},{7,5},{8,10},{9,11},{10,... | collective-permute-start | bytes 196616 | tf_op jit(solution)/shard_map/ppermute | solution.py:166
  36.8 0.0 collective-permute-start.14
  36.8 2.9 %collective-permute-done.17.got_ref.refs_3_ = bf16[192,256]{1,0:T(8,128)(2,1)S(1)} collective-permute-done((bf16[192,256]{1,0:T(8,128)(2,1)S(1)}, bf16[192,256]{1,0:T(8,128)(2,1)S(1)}, u32[]{:S(2)}, u32[]{:S(2)}) %collective-permute-start.17) | collective-permute-done | bytes 98336 | tf_op jit(solution)/shard_map/ppermute | solution.py:166
  39.8 0.1 collective-permute-start.18
  39.8 0.9 %collective-permute-start.19 = (bf16[64,256]{1,0:T(8,128)(2,1)S(1)}, bf16[64,256]{1,0:T(8,128)(2,1)S(1)}, u32[]{:S(2)}, u32[]{:S(2)}) collective-permute-start(bf16[64,256]{1,0:T(8,128)(2,1)S(1)} %grad_row.1.refs_4_), channel_id=1, source_target_pairs={{0,2},{1,3},{2,0},{3,1},{4,6},{5,7},{6,4},{7,5},{8,10},{9,11},{10,... | collective-permute-start | bytes 98312 | tf_op jit(solution)/shard_map/ppermute | solution.py:166
  40.7 1.0 %collective-permute-start.20 = (bf16[64,256]{1,0:T(8,128)(2,1)S(1)}, bf16[64,256]{1,0:T(8,128)(2,1)S(1)}, u32[]{:S(2)}, u32[]{:S(2)}) collective-permute-start(bf16[64,256]{1,0:T(8,128)(2,1)S(1)} %grad_row.1.refs_4_), channel_id=1, source_target_pairs={{0,3},{1,2},{2,1},{3,0},{4,7},{5,6},{6,5},{7,4},{8,11},{9,10},{10,... | collective-permute-start | bytes 98312 | tf_op jit(solution)/shard_map/ppermute | solution.py:166
  41.7 0.8 %layer_out.1 = bf16[128,256]{1,0:T(8,128)(2,1)} custom-call(bf16[256,256]{1,0:T(8,128)(2,1)S(1)} %copy-done.1, bf16[192,256]{1,0:T(8,128)(2,1)S(1)} %collective-permute-done.6.refs_0_.first_ref, bf16[128,256]{1,0:T(8,128)(2,1)S(1)} %get-tuple-element.25.refs_0_, bf16[128,256]{1,0:T(8,128)(2,1)S(1)} %collective-permute-done.13.refs_1_, ...), custom_call_target="tpu_custom_call" | custom-call | tf_op jit(solution)/shard_map/layer_out/pallas_call | solution.py:185
  42.5 0.0 collective-permute-done.18.refs_5_
  42.5 1.4 %collective-permute-done.19.refs_6_ = bf16[64,256]{1,0:T(8,128)(2,1)S(1)} collective-permute-done((bf16[64,256]{1,0:T(8,128)(2,1)S(1)}, bf16[64,256]{1,0:T(8,128)(2,1)S(1)}, u32[]{:S(2)}, u32[]{:S(2)}) %collective-permute-start.19) | collective-permute-done | bytes 32800 | tf_op jit(solution)/shard_map/ppermute | solution.py:166
  44.0 0.4 collective-permute-done.20.refs_7_
  44.3 1.4 %finish.1 = (bf16[128,256]{1,0:T(8,128)(2,1)}, f32[256,256]{1,0:T(8,128)}) custom-call(s32[2]{0:T(128)S(1)} %pad_add_fusion.refs_0_.me_ref, bf16[256,256]{1,0:T(8,128)(2,1)S(1)} %copy-done.1, f32[128,256]{1,0:T(8,128)S(1)} %get-tuple-element.38.refs_2_, bf16[192,256]{1,0:T(8,128)(2,1)S(1)} %collective-permute-done.17.got_ref.refs_3_, ...), custom_call_target="tpu_custom_call" | custom-call | tf_op jit(solution)/shard_map/finish/pallas_call | solution.py:185
  (18 shorter events, 0.1 us)
Async XLA Ops:
  0.6 8.0 %collective-permute-start = (bf16[128,256]{1,0:T(8,128)(2,1)}, bf16[128,256]{1,0:T(8,128)(2,1)S(1)}, u32[]{:S(2)}, u32[]{:S(2)}) collective-permute-start(bf16[128,256]{1,0:T(8,128)(2,1)} %bitcast.11), channel_id=1, source_target_pairs={{0,2},{1,3},{2,0},{3,1},{4,6},{5,7},{6,4},{7,5},{8,10},{9,11},{10,... | collective-permute-start | bytes 196616 | tf_op jit(solution)/shard_map/ppermute | solution.py:166
  3.7 5.7 %collective-permute-start.2 = (bf16[128,256]{1,0:T(8,128)(2,1)}, bf16[128,256]{1,0:T(8,128)(2,1)S(1)}, u32[]{:S(2)}, u32[]{:S(2)}) collective-permute-start(bf16[128,256]{1,0:T(8,128)(2,1)} %bitcast.13), channel_id=1, source_target_pairs={{0,16},{4,20},{8,24},{12,28},{16,0},{20,4},{24,8},{28,12},{1,17},{... | collective-permute-start | bytes 196616 | tf_op jit(solution)/shard_map/ppermute | solution.py:166
  6.9 0.8 %copy-start.2 = (bf16[1,128,256]{2,1,0:T(8,128)(2,1)S(1)}, bf16[1,128,256]{2,1,0:T(8,128)(2,1)}, u32[]{:S(2)}) copy-start(bf16[1,128,256]{2,1,0:T(8,128)(2,1)} %param.11) | copy-start | bytes 196612
  7.7 0.8 %copy-start.3 = (bf16[1,128,256]{2,1,0:T(8,128)(2,1)S(1)}, bf16[1,128,256]{2,1,0:T(8,128)(2,1)}, u32[]{:S(2)}) copy-start(bf16[1,128,256]{2,1,0:T(8,128)(2,1)} %param.6) | copy-start | bytes 196612
  8.6 6.5 %collective-permute-start.1 = (bf16[2,128,256]{2,1,0:T(8,128)(2,1)S(1)}, bf16[2,128,256]{2,1,0:T(8,128)(2,1)S(1)}, u32[]{:S(2)}, u32[]{:S(2)}) collective-permute-start(bf16[2,128,256]{2,1,0:T(8,128)(2,1)S(1)} %cot_near.1.refs_2_.near_ref), channel_id=1, source_target_pairs={{0,1},{1,0},{2,3},{3,2},{4,5},{5,4},{6,7},{7,6},{8,9},{9,8},{10,11... | collective-permute-start | bytes 393224 | tf_op jit(solution)/shard_map/ppermute | solution.py:166
  9.3 3.6 %copy-start = (bf16[1,1,32,128,128]{4,3,2,1,0:T(8,128)(2,1)S(1)}, bf16[1,1,32,128,128]{4,3,2,1,0:T(8,128)(2,1)}, u32[]{:S(2)}) copy-start(bf16[1,1,32,128,128]{4,3,2,1,0:T(8,128)(2,1)} %param.8) | copy-start | bytes 3145732
  9.4 10.0 %collective-permute-start.3 = (bf16[2,128,256]{2,1,0:T(8,128)(2,1)S(1)}, bf16[2,128,256]{2,1,0:T(8,128)(2,1)S(1)}, u32[]{:S(2)}, u32[]{:S(2)}) collective-permute-start(bf16[2,128,256]{2,1,0:T(8,128)(2,1)S(1)} %pair.1.refs_7_), channel_id=1, source_target_pairs={{0,12},{4,8},{8,4},{12,0},{16,28},{20,24},{24,20},{28,16},{1,13},{... | collective-permute-start | bytes 393224 | tf_op jit(solution)/shard_map/ppermute | solution.py:166
  11.7 8.1 %collective-permute-start.4 = (bf16[2,128,256]{2,1,0:T(8,128)(2,1)S(1)}, bf16[2,128,256]{2,1,0:T(8,128)(2,1)S(1)}, u32[]{:S(2)}, u32[]{:S(2)}) collective-permute-start(bf16[2,128,256]{2,1,0:T(8,128)(2,1)S(1)} %pair.1.refs_7_), channel_id=1, source_target_pairs={{0,8},{4,12},{8,0},{12,4},{16,24},{20,28},{24,16},{28,20},{1,9},{5... | collective-permute-start | bytes 393224 | tf_op jit(solution)/shard_map/ppermute | solution.py:166
  12.4 7.4 %collective-permute-start.5 = (bf16[2,128,256]{2,1,0:T(8,128)(2,1)S(1)}, bf16[2,128,256]{2,1,0:T(8,128)(2,1)S(1)}, u32[]{:S(2)}, u32[]{:S(2)}) collective-permute-start(bf16[2,128,256]{2,1,0:T(8,128)(2,1)S(1)} %pair.1.refs_7_), channel_id=1, source_target_pairs={{0,4},{4,0},{8,12},{12,8},{16,20},{20,16},{24,28},{28,24},{1,5},{5... | collective-permute-start | bytes 393224 | tf_op jit(solution)/shard_map/ppermute | solution.py:166
  13.0 0.7 %copy-start.4 = (s32[1,1,32]{2,1,0:T(1,128)S(1)}, s32[1,1,32]{2,1,0:T(1,128)}, u32[]{:S(2)}) copy-start(s32[1,1,32]{2,1,0:T(1,128)} %param.9) | copy-start | bytes 388
  16.2 6.6 %collective-permute-start.9 = (bf16[2,128,256]{2,1,0:T(8,128)(2,1)S(1)}, bf16[2,128,256]{2,1,0:T(8,128)(2,1)S(1)}, u32[]{:S(2)}, u32[]{:S(2)}) collective-permute-start(bf16[2,128,256]{2,1,0:T(8,128)(2,1)S(1)} %get-tuple-element.31), channel_id=1, source_target_pairs={{0,12},{4,8},{8,4},{12,0},{16,28},{20,24},{24,20},{28,16},{1,13},{... | collective-permute-start | bytes 393224 | tf_op jit(solution)/shard_map/ppermute | solution.py:166
  18.2 6.0 %collective-permute-start.10 = (bf16[2,128,256]{2,1,0:T(8,128)(2,1)S(1)}, bf16[2,128,256]{2,1,0:T(8,128)(2,1)S(1)}, u32[]{:S(2)}, u32[]{:S(2)}) collective-permute-start(bf16[2,128,256]{2,1,0:T(8,128)(2,1)S(1)} %get-tuple-element.32), channel_id=1, source_target_pairs={{0,8},{4,12},{8,0},{12,4},{16,24},{20,28},{24,16},{28,20},{1,9},{5... | collective-permute-start | bytes 393224 | tf_op jit(solution)/shard_map/ppermute | solution.py:166
  19.3 5.0 %collective-permute-start.11 = (bf16[2,128,256]{2,1,0:T(8,128)(2,1)S(1)}, bf16[2,128,256]{2,1,0:T(8,128)(2,1)S(1)}, u32[]{:S(2)}, u32[]{:S(2)}) collective-permute-start(bf16[2,128,256]{2,1,0:T(8,128)(2,1)S(1)} %get-tuple-element.33), channel_id=1, source_target_pairs={{0,4},{4,0},{8,12},{12,8},{16,20},{20,16},{24,28},{28,24},{1,5},{5... | collective-permute-start | bytes 393224 | tf_op jit(solution)/shard_map/ppermute | solution.py:166
  21.1 5.0 %collective-permute-start.6 = (bf16[192,256]{1,0:T(8,128)(2,1)S(1)}, bf16[192,256]{1,0:T(8,128)(2,1)S(1)}, u32[]{:S(2)}, u32[]{:S(2)}) collective-permute-start(bf16[192,256]{1,0:T(8,128)(2,1)S(1)} %get-tuple-element.24), channel_id=1, source_target_pairs={{0,1},{1,0},{2,3},{3,2},{4,5},{5,4},{6,7},{7,6},{8,9},{9,8},{10,11... | collective-permute-start | bytes 294920 | tf_op jit(solution)/shard_map/ppermute | solution.py:166
  21.2 4.0 %collective-permute-start.7 = (bf16[64,256]{1,0:T(8,128)(2,1)S(1)}, bf16[64,256]{1,0:T(8,128)(2,1)S(1)}, u32[]{:S(2)}, u32[]{:S(2)}) collective-permute-start(bf16[64,256]{1,0:T(8,128)(2,1)S(1)} %get-tuple-element.29), channel_id=1, source_target_pairs={{0,2},{1,3},{2,0},{3,1},{4,6},{5,7},{6,4},{7,5},{8,10},{9,11},{10,... | collective-permute-start | bytes 98312 | tf_op jit(solution)/shard_map/ppermute | solution.py:166
  22.8 3.3 %collective-permute-start.8 = (bf16[64,256]{1,0:T(8,128)(2,1)S(1)}, bf16[64,256]{1,0:T(8,128)(2,1)S(1)}, u32[]{:S(2)}, u32[]{:S(2)}) collective-permute-start(bf16[64,256]{1,0:T(8,128)(2,1)S(1)} %get-tuple-element.30), channel_id=1, source_target_pairs={{0,3},{1,2},{2,1},{3,0},{4,7},{5,6},{6,5},{7,4},{8,11},{9,10},{10,... | collective-permute-start | bytes 98312 | tf_op jit(solution)/shard_map/ppermute | solution.py:166
  26.2 4.9 %collective-permute-start.12 = (bf16[64,256]{1,0:T(8,128)(2,1)S(1)}, bf16[64,256]{1,0:T(8,128)(2,1)S(1)}, u32[]{:S(2)}, u32[]{:S(2)}) collective-permute-start(bf16[64,256]{1,0:T(8,128)(2,1)S(1)} %grad_col.1.refs_1_), channel_id=1, source_target_pairs={{0,12},{4,8},{8,4},{12,0},{16,28},{20,24},{24,20},{28,16},{1,13},{... | collective-permute-start | bytes 98312 | tf_op jit(solution)/shard_map/ppermute | solution.py:166
  28.6 3.9 %collective-permute-start.15 = (bf16[64,256]{1,0:T(8,128)(2,1)S(1)}, bf16[64,256]{1,0:T(8,128)(2,1)S(1)}, u32[]{:S(2)}, u32[]{:S(2)}) collective-permute-start(bf16[64,256]{1,0:T(8,128)(2,1)S(1)} %grad_col.1.refs_1_), channel_id=1, source_target_pairs={{0,4},{4,0},{8,12},{12,8},{16,20},{20,16},{24,28},{28,24},{1,5},{5... | collective-permute-start | bytes 98312 | tf_op jit(solution)/shard_map/ppermute | solution.py:166
  29.2 3.9 %collective-permute-start.16 = (bf16[64,256]{1,0:T(8,128)(2,1)S(1)}, bf16[64,256]{1,0:T(8,128)(2,1)S(1)}, u32[]{:S(2)}, u32[]{:S(2)}) collective-permute-start(bf16[64,256]{1,0:T(8,128)(2,1)S(1)} %grad_col.1.refs_1_), channel_id=1, source_target_pairs={{0,8},{4,12},{8,0},{12,4},{16,24},{20,28},{24,16},{28,20},{1,9},{5... | collective-permute-start | bytes 98312 | tf_op jit(solution)/shard_map/ppermute | solution.py:166
  33.2 6.6 %collective-permute-start.17 = (bf16[192,256]{1,0:T(8,128)(2,1)S(1)}, bf16[192,256]{1,0:T(8,128)(2,1)S(1)}, u32[]{:S(2)}, u32[]{:S(2)}) collective-permute-start(bf16[192,256]{1,0:T(8,128)(2,1)S(1)} %grad_near.1.held_ref), channel_id=1, source_target_pairs={{0,16},{4,20},{8,24},{12,28},{16,0},{20,4},{24,8},{28,12},{1,17},{... | collective-permute-start | bytes 294920 | tf_op jit(solution)/shard_map/ppermute | solution.py:166
  36.0 5.8 %copy-start.1 = (bf16[256,256]{1,0:T(8,128)(2,1)S(1)}, bf16[256,256]{1,0:T(8,128)(2,1)}, u32[]{:S(2)}) copy-start(bf16[256,256]{1,0:T(8,128)(2,1)} %refs_1_.1) | copy-start | bytes 393220
  36.0 5.7 %collective-permute-start.13 = (bf16[128,256]{1,0:T(8,128)(2,1)S(1)}, bf16[128,256]{1,0:T(8,128)(2,1)S(1)}, u32[]{:S(2)}, u32[]{:S(2)}) collective-permute-start(bf16[128,256]{1,0:T(8,128)(2,1)S(1)} %get-tuple-element.36), channel_id=1, source_target_pairs={{0,2},{1,3},{2,0},{3,1},{4,6},{5,7},{6,4},{7,5},{8,10},{9,11},{10,... | collective-permute-start | bytes 196616 | tf_op jit(solution)/shard_map/ppermute | solution.py:166
  36.8 4.9 %collective-permute-start.14 = (bf16[128,256]{1,0:T(8,128)(2,1)S(1)}, bf16[128,256]{1,0:T(8,128)(2,1)S(1)}, u32[]{:S(2)}, u32[]{:S(2)}) collective-permute-start(bf16[128,256]{1,0:T(8,128)(2,1)S(1)} %get-tuple-element.37), channel_id=1, source_target_pairs={{0,3},{1,2},{2,1},{3,0},{4,7},{5,6},{6,5},{7,4},{8,11},{9,10},{10,... | collective-permute-start | bytes 196616 | tf_op jit(solution)/shard_map/ppermute | solution.py:166
  39.8 2.8 %collective-permute-start.18 = (bf16[64,256]{1,0:T(8,128)(2,1)S(1)}, bf16[64,256]{1,0:T(8,128)(2,1)S(1)}, u32[]{:S(2)}, u32[]{:S(2)}) collective-permute-start(bf16[64,256]{1,0:T(8,128)(2,1)S(1)} %grad_row.1.refs_4_), channel_id=1, source_target_pairs={{0,1},{1,0},{2,3},{3,2},{4,5},{5,4},{6,7},{7,6},{8,9},{9,8},{10,11... | collective-permute-start | bytes 98312 | tf_op jit(solution)/shard_map/ppermute | solution.py:166
  39.8 4.1 %collective-permute-start.19 = (bf16[64,256]{1,0:T(8,128)(2,1)S(1)}, bf16[64,256]{1,0:T(8,128)(2,1)S(1)}, u32[]{:S(2)}, u32[]{:S(2)}) collective-permute-start(bf16[64,256]{1,0:T(8,128)(2,1)S(1)} %grad_row.1.refs_4_), channel_id=1, source_target_pairs={{0,2},{1,3},{2,0},{3,1},{4,6},{5,7},{6,4},{7,5},{8,10},{9,11},{10,... | collective-permute-start | bytes 98312 | tf_op jit(solution)/shard_map/ppermute | solution.py:166
  40.7 3.6 %collective-permute-start.20 = (bf16[64,256]{1,0:T(8,128)(2,1)S(1)}, bf16[64,256]{1,0:T(8,128)(2,1)S(1)}, u32[]{:S(2)}, u32[]{:S(2)}) collective-permute-start(bf16[64,256]{1,0:T(8,128)(2,1)S(1)} %grad_row.1.refs_4_), channel_id=1, source_target_pairs={{0,3},{1,2},{2,1},{3,0},{4,7},{5,6},{6,5},{7,4},{8,11},{9,10},{10,... | collective-permute-start | bytes 98312 | tf_op jit(solution)/shard_map/ppermute | solution.py:166
where the time goes:
time: 45.9 us; the launch traced here: 45.7 us
  starting transfers between devices  22.6 us (49%)
  waiting for transfers between devices  13.1 us (29%)
  Pallas kernels  6.22 us (14%)
  local copies, waits for them, and re-layouts  2.33 us (5%)
  between operations  1.42 us (3%)
    ppermute x21, starting transfers between devices, swap(): return lax.ppermute(array, axis, pairs)  22.6 us
    ppermute x21, waiting for transfers between devices, swap(): return lax.ppermute(array, axis, pairs)  13.1 us
    pallas_call x13, Pallas kernels, call(): pl.pallas_call(kernel, out_shape=out_shape, in_specs=in_specs, out_specs=...  6.22 us
    unnamed x10, local copies, waits for them, and re-layouts  2.33 us
  transfers between devices with their start and end apart: 21, of which 12 were waited for; matrix products, arithmetic and copies ran while one was open for 0% of the time, Pallas kernels for 10%

commit v1 on v0

--- a/solution.py
+++ b/solution.py
@@ -35,14 +35,14 @@
     return total
 
 
-def dense_kernel(slots_ref, count_ref, tiles_ref, adj_ref, sems):
+def dense_kernel(meta_ref, tiles_ref, adj_ref, sems):
     slot_count, tile, _ = tiles_ref.shape
     col_tiles = adj_ref.shape[1] // tile
-    live = jnp.minimum(count_ref[0], slot_count)
+    live = jnp.minimum(meta_ref[2], slot_count)
     adj_ref[...] = jnp.zeros_like(adj_ref)
 
     def copy(k):
-        slot = slots_ref[k]
+        slot = meta_ref[3 + k]
         row = pl.multiple_of((slot // col_tiles) * tile, tile)
         col = pl.multiple_of((slot % col_tiles) * tile, tile)
         place = adj_ref.at[pl.ds(row, tile), pl.ds(col, tile)]
@@ -66,22 +66,22 @@
         out_ref[k] = refs[k][...]
 
 
-def place_cots(me_ref, near_ref, other_ref, out_ref):
+def place_cots(meta_ref, near_ref, other_ref, out_ref):
     slab = near_ref.shape[1]
     for k in range(near_ref.shape[0]):
-        out_ref[rows_of(me_ref[1] ^ (2 * k), slab), :] = near_ref[k]
-        out_ref[rows_of(me_ref[1] ^ (2 * k + 1), slab), :] = other_ref[k]
-
-
-def forward_kernel(me_ref, adj_ref, near_ref, other_ref, *refs, half):
+        out_ref[rows_of(meta_ref[1] ^ (2 * k), slab), :] = near_ref[k]
+        out_ref[rows_of(meta_ref[1] ^ (2 * k + 1), slab), :] = other_ref[k]
+
+
+def forward_kernel(meta_ref, adj_ref, near_ref, other_ref, *refs, half):
     pair_refs, (*out_refs, both_ref, column, cots, part, grad) = refs[:half], refs[half:]
     slab = near_ref.shape[1]
     others = len(out_refs) // 2
     piece = both_ref.shape[0] - slab
-    place_cots(me_ref, near_ref, other_ref, cots)
+    place_cots(meta_ref, near_ref, other_ref, cots)
     for k, ref in enumerate(pair_refs[::-1]):
-        column[rows_of(me_ref[0] ^ k, slab), :] = ref[0]
-        column[rows_of(me_ref[0] ^ k ^ half, slab), :] = ref[1]
+        column[rows_of(meta_ref[0] ^ k, slab), :] = ref[0]
+        column[rows_of(meta_ref[0] ^ k ^ half, slab), :] = ref[1]
     product = jnp.dot(adj_ref[...], column[...], preferred_element_type=F32).astype(BF16)
     part[...] = product
     grad[...] = lax.dot_general(
@@ -89,22 +89,22 @@
     ).astype(BF16)
     for n in range(others):
         k = n + 1 if n else 0
-        out_refs[n][...] = part[rows_of(me_ref[1] ^ k, slab), :]
-        out_refs[others + n][...] = grad[rows_of(me_ref[1] ^ k, piece), :]
-    both_ref[:slab, :] = part[rows_of(me_ref[1] ^ 1, slab), :]
-    both_ref[slab:, :] = grad[rows_of(me_ref[1] ^ 1, piece), :]
-
-
-def backward_kernel(me_ref, adj_ref, near_ref, other_ref, *refs):
+        out_refs[n][...] = part[rows_of(meta_ref[1] ^ k, slab), :]
+        out_refs[others + n][...] = grad[rows_of(meta_ref[1] ^ k, piece), :]
+    both_ref[:slab, :] = part[rows_of(meta_ref[1] ^ 1, slab), :]
+    both_ref[slab:, :] = grad[rows_of(meta_ref[1] ^ 1, piece), :]
+
+
+def backward_kernel(meta_ref, adj_ref, near_ref, other_ref, *refs):
     *pair_refs, cots, total = refs
     half, slab = len(pair_refs), pair_refs[0].shape[1]
-    place_cots(me_ref, near_ref, other_ref, cots)
+    place_cots(meta_ref, near_ref, other_ref, cots)
     total[...] = lax.dot_general(
         adj_ref[...], cots[...], (((0,), (0,)), ((), ())), preferred_element_type=F32
     ).astype(BF16)
     for k, ref in enumerate(pair_refs):
-        ref[0] = total[rows_of(me_ref[0] ^ k, slab), :]
-        ref[1] = total[rows_of(me_ref[0] ^ k ^ half, slab), :]
+        ref[0] = total[rows_of(meta_ref[0] ^ k, slab), :]
+        ref[1] = total[rows_of(meta_ref[0] ^ k ^ half, slab), :]
 
 
 def pair_sum_kernel(*refs):
@@ -123,10 +123,11 @@
     ).astype(BF16)
 
 
-def output_kernel(weight_ref, first_ref, *refs):
-    *term_refs, out_ref = refs
-    first_ref = first_ref.at[: out_ref.shape[0], :]
-    out_ref[...] = weighted(weight_ref, [first_ref, *term_refs], 0)
+def output_kernel(weight_ref, keep_ref, far_ref, first_ref, *refs):
+    *chunk_refs, layer_ref, feature_ref = refs
+    slab = layer_ref.shape[0]
+    layer_ref[...] = weighted(weight_ref, [first_ref.at[:slab, :], *chunk_refs], 0)
+    feature_ref[...] = weighted(weight_ref, [keep_ref, far_ref.at[:slab, :]], 1)
 
 
 def col_kernel(first_ref, *refs, terms):
@@ -152,13 +153,11 @@
     out_ref[...] = summed([held_ref.at[slab:, :], got_ref.at[slab:, :]]).astype(BF16)
 
 
-def finish_kernel(me_ref, weight_ref, keep_ref, got_ref, *refs, scale):
-    *piece_refs, feature_ref, grad_ref = refs
-    got_ref = got_ref.at[: feature_ref.shape[0], :]
+def gather_kernel(meta_ref, *refs):
+    *piece_refs, out_ref = refs
     piece = piece_refs[0].shape[0]
     for k, ref in enumerate(piece_refs):
-        grad_ref[rows_of(me_ref[1] ^ k, piece), :] = ref[...].astype(F32) * scale
-    feature_ref[...] = weighted(weight_ref, [keep_ref, got_ref], 1)
+        out_ref[rows_of(meta_ref[1] ^ k, piece), :] = ref[...]
 
 
 def swap(array, axis, distance):
@@ -178,7 +177,8 @@
     slab, width = features.shape[1:]
     rows, cols = col_devices * slab, row_devices * slab
     piece = width // col_devices
-    me = jnp.stack([lax.axis_index("row"), lax.axis_index("col")]).astype(jnp.int32)
+    place = jnp.stack([lax.axis_index("row"), lax.axis_index("col")]).astype(jnp.int32)
+    me = jnp.concatenate([place, tile_counts[0], tile_slots[0, 0]])
 
     def call(kernel, name, out_shape, in_specs, args, scratch=(), micros=None):
         many = isinstance(out_shape, list)
@@ -198,14 +198,13 @@
     own = features[0]
     far = swap(own, "row", half)
     adj = call(
-        dense_kernel, "dense", shape(rows, cols), [SMEM, SMEM, ANY],
-        (tile_slots[0, 0], tile_counts[0], tile_values[0, 0]),
+        dense_kernel, "dense", shape(rows, cols), [SMEM, ANY], (me, tile_values[0, 0]),
         scratch=[pltpu.SemaphoreType.DMA((slots,))],
     )
 
     def hold(arrays, after, name):
         return call(
-            hold_kernel, name, [shape(slab, width)] * len(arrays),
+            hold_kernel, name, [shape(*array.shape) for array in arrays],
             [VMEM] * len(arrays) + [ANY], (*arrays, after),
         )
 
@@ -241,13 +240,13 @@
         [SMEM] + [VMEM] * 3, (me, adj, cot_near, cot_other),
         scratch=[pltpu.VMEM((rows, width), BF16), pltpu.VMEM((cols, width), BF16)],
     )
+    chunks, pieces = outs[: col_devices - 1], outs[col_devices - 1 : -1]
+    first = swap(outs[-1], "col", 1)
+
     column_keep, column_send = call(
         pair_sum_kernel, "pair_sum", [shape(slab, width, dtype=F32), shape(slab, width)],
         [VMEM] * half, exchange(column_pairs, "row")[::-1], micros=5,
     )
-    chunks, pieces = outs[: col_devices - 1], outs[col_devices - 1 : -1]
-    first = swap(outs[-1], "col", 1)
-
     def fetch(arrays):
         return [arrays[0]] + [swap(arrays[k - 1], "col", k) for k in range(2, col_devices)]
 
@@ -265,17 +264,15 @@
     grad_row = call(
         row_kernel, "grad_row", shape(piece, width), [VMEM] * 2, (both, both_far)
     )
-    scale = 1.0 / math.sqrt(row_devices * col_devices * slab)
-    layer_out = call(
-        output_kernel, "layer_out", shape(slab, width),
-        [VMEM] * (1 + col_devices), (weight, first, *row_got),
-    )
-    feature_grad, weight_grad = call(
-        lambda *refs: finish_kernel(*refs, scale=scale), "finish",
-        [shape(slab, width), shape(width, width, dtype=F32)],
-        [SMEM] + [VMEM] * (3 + col_devices),
-        (me, weight, column_keep, both_far, *exchange([grad_row] * col_devices, "col")),
-    )
+    layer_out, feature_grad = call(
+        output_kernel, "outputs", [shape(slab, width)] * 2, [VMEM] * (3 + col_devices),
+        (weight, column_keep, both_far, first, *row_got),
+    )
+    gathered = call(
+        gather_kernel, "weight_grad", shape(width, width), [SMEM] + [VMEM] * col_devices,
+        (me, *exchange([grad_row] * col_devices, "col")),
+    )
+    weight_grad = gathered.astype(F32) * (1.0 / math.sqrt(row_devices * col_devices * slab))
     return (layer_out[None], feature_grad[None], weight_grad)
 
 

time: 45.9 us -> 43.8 us (0.954)
  waiting for transfers between devices: 13.1 us -> 11.1 us
  Pallas kernels: 6.22 us -> 4.98 us
  other arithmetic: 0.07 us -> 0.8 us
    ppermute x21, waiting for transfers between devices: 13.1 us -> 11.1 us  [swap(): return lax.ppermute(array, axis, pairs)]
    pallas_call x13, Pallas kernels: 6.22 us -> 4.98 us  [call(): pl.pallas_call(kernel, out_shape=out_shape, in_specs=in_specs, out_specs=...]
    mul x0 -> x1, other arithmetic: none -> 0.72 us  [body(): gathered.astype(F32) * (1.0 / math.sqrt(row_devices * col_devices * slab))]
where the time goes in v1:
time: 43.8 us; the launch traced here: 43.7 us
  starting transfers between devices  23 us (53%)
  waiting for transfers between devices  11.1 us (25%)
  Pallas kernels  4.98 us (11%)
  local copies, waits for them, and re-layouts  2.34 us (5%)
  between operations  1.42 us (3%)
  other arithmetic  0.8 us (2%)
    ppermute x21, starting transfers between devices, swap(): return lax.ppermute(array, axis, pairs)  23 us
    ppermute x21, waiting for transfers between devices, swap(): return lax.ppermute(array, axis, pairs)  11.1 us
    pallas_call x13, Pallas kernels, call(): pl.pallas_call(kernel, out_shape=out_shape, in_specs=in_specs, out_specs=...  4.98 us
    unnamed x10, local copies, waits for them, and re-layouts  2.34 us
  transfers between devices with their start and end apart: 21, of which 12 were waited for; matrix products, arithmetic and copies ran while one was open for 0% of the time, Pallas kernels for 10%

profile of v1, /device:TPU:0, one launch (start us, length us, event | category | flops | bytes accessed | tf_op | source)
XLA Modules:
  0.0 43.7 jit_solution(15234205185095847444)
XLA Ops:
  0.6 3.0 %collective-permute-start = (bf16[128,256]{1,0:T(8,128)(2,1)}, bf16[128,256]{1,0:T(8,128)(2,1)S(1)}, u32[]{:S(2)}, u32[]{:S(2)}) collective-permute-start(bf16[128,256]{1,0:T(8,128)(2,1)} %bitcast.11), channel_id=1, source_target_pairs={{0,2},{1,3},{2,0},{3,1},{4,6},{5,7},{6,4},{7,5},{8,10},{9,11},{10,... | collective-permute-start | bytes 196616 | tf_op jit(solution)/shard_map/ppermute | solution.py:165
  3.7 2.6 %collective-permute-start.5 = (bf16[128,256]{1,0:T(8,128)(2,1)}, bf16[128,256]{1,0:T(8,128)(2,1)S(1)}, u32[]{:S(2)}, u32[]{:S(2)}) collective-permute-start(bf16[128,256]{1,0:T(8,128)(2,1)} %bitcast.13), channel_id=1, source_target_pairs={{0,16},{4,20},{8,24},{12,28},{16,0},{20,4},{24,8},{28,12},{1,17},{... | collective-permute-start | bytes 196616 | tf_op jit(solution)/shard_map/ppermute | solution.py:165
  6.9 0.8 %copy-done.2 = bf16[1,128,256]{2,1,0:T(8,128)(2,1)S(1)} copy-done((bf16[1,128,256]{2,1,0:T(8,128)(2,1)S(1)}, bf16[1,128,256]{2,1,0:T(8,128)(2,1)}, u32[]{:S(2)}) %copy-start.2) | copy-done | bytes 65560
  7.7 0.8 %copy-done.3 = bf16[1,128,256]{2,1,0:T(8,128)(2,1)S(1)} copy-done((bf16[1,128,256]{2,1,0:T(8,128)(2,1)S(1)}, bf16[1,128,256]{2,1,0:T(8,128)(2,1)}, u32[]{:S(2)}) %copy-start.3) | copy-done | bytes 65560
  8.6 0.0 collective-permute-done.refs_1_
  8.6 0.1 collective-permute-start.1
  8.7 0.6 %collective-permute-done.5.refs_1_ = bf16[128,256]{1,0:T(8,128)(2,1)S(1)} collective-permute-done((bf16[128,256]{1,0:T(8,128)(2,1)}, bf16[128,256]{1,0:T(8,128)(2,1)S(1)}, u32[]{:S(2)}, u32[]{:S(2)}) %collective-permute-start.5) | collective-permute-done | bytes 65568 | tf_op jit(solution)/shard_map/ppermute | solution.py:165
  9.4 1.6 %collective-permute-start.8 = (bf16[2,128,256]{2,1,0:T(8,128)(2,1)S(1)}, bf16[2,128,256]{2,1,0:T(8,128)(2,1)S(1)}, u32[]{:S(2)}, u32[]{:S(2)}) collective-permute-start(bf16[2,128,256]{2,1,0:T(8,128)(2,1)S(1)} %pair.1.refs_7_), channel_id=1, source_target_pairs={{0,4},{4,0},{8,12},{12,8},{16,20},{20,16},{24,28},{28,24},{1,5},{5... | collective-permute-start | bytes 393224 | tf_op jit(solution)/shard_map/ppermute | solution.py:165
  10.9 0.7 %copy-done.4 = s32[1,1,32]{2,1,0:T(1,128)S(1)} copy-done((s32[1,1,32]{2,1,0:T(1,128)S(1)}, s32[1,1,32]{2,1,0:T(1,128)}, u32[]{:S(2)}) %copy-start.4) | copy-done | bytes 152
  11.6 0.1 pad_add_fusion.meta_ref.refs_0_
  11.6 1.3 %collective-permute-start.7 = (bf16[2,128,256]{2,1,0:T(8,128)(2,1)S(1)}, bf16[2,128,256]{2,1,0:T(8,128)(2,1)S(1)}, u32[]{:S(2)}, u32[]{:S(2)}) collective-permute-start(bf16[2,128,256]{2,1,0:T(8,128)(2,1)S(1)} %pair.1.refs_7_), channel_id=1, source_target_pairs={{0,8},{4,12},{8,0},{12,4},{16,24},{20,28},{24,16},{28,20},{1,9},{5... | collective-permute-start | bytes 393224 | tf_op jit(solution)/shard_map/ppermute | solution.py:165
  12.9 0.7 %collective-permute-start.6 = (bf16[2,128,256]{2,1,0:T(8,128)(2,1)S(1)}, bf16[2,128,256]{2,1,0:T(8,128)(2,1)S(1)}, u32[]{:S(2)}, u32[]{:S(2)}) collective-permute-start(bf16[2,128,256]{2,1,0:T(8,128)(2,1)S(1)} %pair.1.refs_7_), channel_id=1, source_target_pairs={{0,12},{4,8},{8,4},{12,0},{16,28},{20,24},{24,20},{28,16},{1,13},{... | collective-permute-start | bytes 393224 | tf_op jit(solution)/shard_map/ppermute | solution.py:165
  13.6 1.0 %dense.1.adj_ref.refs_1_ = bf16[512,1024]{1,0:T(8,128)(2,1)S(1)} custom-call(s32[35]{0:T(128)S(1)} %pad_add_fusion.meta_ref.refs_0_, bf16[32,128,128]{2,1,0:T(8,128)(2,1)S(1)} %bitcast.10), custom_call_target="tpu_custom_call" | custom-call | tf_op jit(solution)/shard_map/dense/pallas_call | solution.py:185
  14.7 0.0 collective-permute-done.1.other_ref.refs_3_
  14.7 1.1 %backward.1 = (bf16[2,128,256]{2,1,0:T(8,128)(2,1)S(1)}, bf16[2,128,256]{2,1,0:T(8,128)(2,1)S(1)}, bf16[2,128,256]{2,1,0:T(8,128)(2,1)S(1)}, bf16[2,128,256]{2,1,0:T(8,128)(2,1)S(1)}) custom-call(s32[35]{0:T(128)S(1)} %pad_add_fusion.meta_ref.refs_0_, bf16[512,1024]{1,0:T(8,128)(2,1)S(1)} %dense.1.adj_ref.refs_1_, ...), custom_call_target="tpu_custom_call" | custom-call | tf_op jit(solution)/shard_map/backward/pallas_call | solution.py:185
  15.8 2.3 %collective-permute-start.2 = (bf16[2,128,256]{2,1,0:T(8,128)(2,1)S(1)}, bf16[2,128,256]{2,1,0:T(8,128)(2,1)S(1)}, u32[]{:S(2)}, u32[]{:S(2)}) collective-permute-start(bf16[2,128,256]{2,1,0:T(8,128)(2,1)S(1)} %get-tuple-element.23), channel_id=1, source_target_pairs={{0,12},{4,8},{8,4},{12,0},{16,28},{20,24},{24,20},{28,16},{1,13},{... | collective-permute-start | bytes 393224 | tf_op jit(solution)/shard_map/ppermute | solution.py:165
  18.1 0.8 %collective-permute-start.3 = (bf16[2,128,256]{2,1,0:T(8,128)(2,1)S(1)}, bf16[2,128,256]{2,1,0:T(8,128)(2,1)S(1)}, u32[]{:S(2)}, u32[]{:S(2)}) collective-permute-start(bf16[2,128,256]{2,1,0:T(8,128)(2,1)S(1)} %get-tuple-element.24), channel_id=1, source_target_pairs={{0,8},{4,12},{8,0},{12,4},{16,24},{20,28},{24,16},{28,20},{1,9},{5... | collective-permute-start | bytes 393224 | tf_op jit(solution)/shard_map/ppermute | solution.py:165
  18.9 0.0 collective-permute-done.8.refs_6_
  18.9 0.5 %collective-permute-start.4 = (bf16[2,128,256]{2,1,0:T(8,128)(2,1)S(1)}, bf16[2,128,256]{2,1,0:T(8,128)(2,1)S(1)}, u32[]{:S(2)}, u32[]{:S(2)}) collective-permute-start(bf16[2,128,256]{2,1,0:T(8,128)(2,1)S(1)} %get-tuple-element.25), channel_id=1, source_target_pairs={{0,4},{4,0},{8,12},{12,8},{16,20},{20,16},{24,28},{28,24},{1,5},{5... | collective-permute-start | bytes 393224 | tf_op jit(solution)/shard_map/ppermute | solution.py:165
  19.4 0.9 %collective-permute-done.6.refs_4_ = bf16[2,128,256]{2,1,0:T(8,128)(2,1)S(1)} collective-permute-done((bf16[2,128,256]{2,1,0:T(8,128)(2,1)S(1)}, bf16[2,128,256]{2,1,0:T(8,128)(2,1)S(1)}, u32[]{:S(2)}, u32[]{:S(2)}) %collective-permute-start.6) | collective-permute-done | bytes 131104 | tf_op jit(solution)/shard_map/ppermute | solution.py:165
  20.3 1.3 %forward.1 = (bf16[128,256]{1,0:T(8,128)(2,1)S(1)}, bf16[128,256]{1,0:T(8,128)(2,1)S(1)}, bf16[128,256]{1,0:T(8,128)(2,1)S(1)}, bf16[64,256]{1,0:T(8,128)(2,1)S(...) custom-call(s32[35]{0:T(128)S(1)} %pad_add_fusion.meta_ref.refs_0_, ...), custom_call_target="tpu_custom_call" | custom-call | tf_op jit(solution)/shard_map/forward/pallas_call | solution.py:185
  21.6 0.5 %collective-permute-start.10 = (bf16[64,256]{1,0:T(8,128)(2,1)S(1)}, bf16[64,256]{1,0:T(8,128)(2,1)S(1)}, u32[]{:S(2)}, u32[]{:S(2)}) collective-permute-start(bf16[64,256]{1,0:T(8,128)(2,1)S(1)} %get-tuple-element.32), channel_id=1, source_target_pairs={{0,2},{1,3},{2,0},{3,1},{4,6},{5,7},{6,4},{7,5},{8,10},{9,11},{10,... | collective-permute-start | bytes 98312 | tf_op jit(solution)/shard_map/ppermute | solution.py:165
  22.1 0.0 collective-permute-start.11
  22.1 1.1 %collective-permute-done.2.refs_0_ = bf16[2,128,256]{2,1,0:T(8,128)(2,1)S(1)} collective-permute-done((bf16[2,128,256]{2,1,0:T(8,128)(2,1)S(1)}, bf16[2,128,256]{2,1,0:T(8,128)(2,1)S(1)}, u32[]{:S(2)}, u32[]{:S(2)}) %collective-permute-start.2) | collective-permute-done | bytes 131104 | tf_op jit(solution)/shard_map/ppermute | solution.py:165
  23.2 0.6 %collective-permute-start.9 = (bf16[192,256]{1,0:T(8,128)(2,1)S(1)}, bf16[192,256]{1,0:T(8,128)(2,1)S(1)}, u32[]{:S(2)}, u32[]{:S(2)}) collective-permute-start(bf16[192,256]{1,0:T(8,128)(2,1)S(1)} %get-tuple-element.30), channel_id=1, source_target_pairs={{0,1},{1,0},{2,3},{3,2},{4,5},{5,4},{6,7},{7,6},{8,9},{9,8},{10,11... | collective-permute-start | bytes 294920 | tf_op jit(solution)/shard_map/ppermute | solution.py:165
  23.8 1.3 %collective-permute-done.3.refs_1_ = bf16[2,128,256]{2,1,0:T(8,128)(2,1)S(1)} collective-permute-done((bf16[2,128,256]{2,1,0:T(8,128)(2,1)S(1)}, bf16[2,128,256]{2,1,0:T(8,128)(2,1)S(1)}, u32[]{:S(2)}, u32[]{:S(2)}) %collective-permute-start.3) | collective-permute-done | bytes 131104 | tf_op jit(solution)/shard_map/ppermute | solution.py:165
  25.1 0.0 collective-permute-done.4.refs_2_
  25.1 0.1 pair_sum.1
  25.2 0.6 %collective-permute-done.10.refs_2_ = bf16[64,256]{1,0:T(8,128)(2,1)S(1)} collective-permute-done((bf16[64,256]{1,0:T(8,128)(2,1)S(1)}, bf16[64,256]{1,0:T(8,128)(2,1)S(1)}, u32[]{:S(2)}, u32[]{:S(2)}) %collective-permute-start.10) | collective-permute-done | bytes 32800 | tf_op jit(solution)/shard_map/ppermute | solution.py:165
  25.8 2.8 %collective-permute-start.14 = (bf16[64,256]{1,0:T(8,128)(2,1)S(1)}, bf16[64,256]{1,0:T(8,128)(2,1)S(1)}, u32[]{:S(2)}, u32[]{:S(2)}) collective-permute-start(bf16[64,256]{1,0:T(8,128)(2,1)S(1)} %grad_col.1.refs_1_), channel_id=1, source_target_pairs={{0,12},{4,8},{8,4},{12,0},{16,28},{20,24},{24,20},{28,16},{1,13},{... | collective-permute-start | bytes 98312 | tf_op jit(solution)/shard_map/ppermute | solution.py:165
  28.6 0.1 collective-permute-start.13
  28.7 0.7 %collective-permute-start.12 = (bf16[64,256]{1,0:T(8,128)(2,1)S(1)}, bf16[64,256]{1,0:T(8,128)(2,1)S(1)}, u32[]{:S(2)}, u32[]{:S(2)}) collective-permute-start(bf16[64,256]{1,0:T(8,128)(2,1)S(1)} %grad_col.1.refs_1_), channel_id=1, source_target_pairs={{0,4},{4,0},{8,12},{12,8},{16,20},{20,16},{24,28},{28,24},{1,5},{5... | collective-permute-start | bytes 98312 | tf_op jit(solution)/shard_map/ppermute | solution.py:165
  29.4 1.3 %collective-permute-done.14.refs_4_.refs_2_ = bf16[64,256]{1,0:T(8,128)(2,1)S(1)} collective-permute-done((bf16[64,256]{1,0:T(8,128)(2,1)S(1)}, bf16[64,256]{1,0:T(8,128)(2,1)S(1)}, u32[]{:S(2)}, u32[]{:S(2)}) %collective-permute-start.14) | collective-permute-done | bytes 32800 | tf_op jit(solution)/shard_map/ppermute | solution.py:165
  30.7 1.8 %collective-permute-done.13.refs_3_ = bf16[64,256]{1,0:T(8,128)(2,1)S(1)} collective-permute-done((bf16[64,256]{1,0:T(8,128)(2,1)S(1)}, bf16[64,256]{1,0:T(8,128)(2,1)S(1)}, u32[]{:S(2)}, u32[]{:S(2)}) %collective-permute-start.13) | collective-permute-done | bytes 32800 | tf_op jit(solution)/shard_map/ppermute | solution.py:165
  32.5 0.1 collective-permute-done.12.refs_2_
  32.7 2.5 %collective-permute-start.15 = (bf16[192,256]{1,0:T(8,128)(2,1)S(1)}, bf16[192,256]{1,0:T(8,128)(2,1)S(1)}, u32[]{:S(2)}, u32[]{:S(2)}) collective-permute-start(bf16[192,256]{1,0:T(8,128)(2,1)S(1)} %grad_near.1.held_ref), channel_id=1, source_target_pairs={{0,16},{4,20},{8,24},{12,28},{16,0},{20,4},{24,8},{28,12},{1,17},{... | collective-permute-start | bytes 294920 | tf_op jit(solution)/shard_map/ppermute | solution.py:165
  35.2 0.0 copy-start.1
  35.2 1.1 %collective-permute-start.16 = (bf16[128,256]{1,0:T(8,128)(2,1)S(1)}, bf16[128,256]{1,0:T(8,128)(2,1)S(1)}, u32[]{:S(2)}, u32[]{:S(2)}) collective-permute-start(bf16[128,256]{1,0:T(8,128)(2,1)S(1)} %get-tuple-element.37), channel_id=1, source_target_pairs={{0,2},{1,3},{2,0},{3,1},{4,6},{5,7},{6,4},{7,5},{8,10},{9,11},{10,... | collective-permute-start | bytes 196616 | tf_op jit(solution)/shard_map/ppermute | solution.py:165
  36.3 2.0 %collective-permute-done.15.far_ref.got_ref = bf16[192,256]{1,0:T(8,128)(2,1)S(1)} collective-permute-done((bf16[192,256]{1,0:T(8,128)(2,1)S(1)}, bf16[192,256]{1,0:T(8,128)(2,1)S(1)}, u32[]{:S(2)}, u32[]{:S(2)}) %collective-permute-start.15) | collective-permute-done | bytes 98336 | tf_op jit(solution)/shard_map/ppermute | solution.py:165
  38.3 0.1 collective-permute-start.20
  38.3 1.5 %collective-permute-start.19 = (bf16[64,256]{1,0:T(8,128)(2,1)S(1)}, bf16[64,256]{1,0:T(8,128)(2,1)S(1)}, u32[]{:S(2)}, u32[]{:S(2)}) collective-permute-start(bf16[64,256]{1,0:T(8,128)(2,1)S(1)} %grad_row.1.refs_0_), channel_id=1, source_target_pairs={{0,2},{1,3},{2,0},{3,1},{4,6},{5,7},{6,4},{7,5},{8,10},{9,11},{10,... | collective-permute-start | bytes 98312 | tf_op jit(solution)/shard_map/ppermute | solution.py:165
  39.9 0.3 collective-permute-start.18
  40.2 0.4 collective-permute-done.17.refs_2_
  40.6 0.8 %outputs.1 = (bf16[128,256]{1,0:T(8,128)(2,1)}, bf16[128,256]{1,0:T(8,128)(2,1)}) custom-call(bf16[256,256]{1,0:T(8,128)(2,1)S(1)} %copy-done.1, f32[128,256]{1,0:T(8,128)S(1)} %get-tuple-element.27.keep_ref, bf16[192,256]{1,0:T(8,128)(2,1)S(1)} %collective-permute-done.15.far_ref.got_ref, bf16[192,256]{1,0:T(8,128)(2,1)S(1)} %collective-permute-done.9.refs_0_.first_ref, ...), custom_call_target="tpu_custom_call" | custom-call | tf_op jit(solution)/shard_map/outputs/pallas_call | solution.py:185
  41.4 0.6 %collective-permute-done.20.refs_3_ = bf16[64,256]{1,0:T(8,128)(2,1)S(1)} collective-permute-done((bf16[64,256]{1,0:T(8,128)(2,1)S(1)}, bf16[64,256]{1,0:T(8,128)(2,1)S(1)}, u32[]{:S(2)}, u32[]{:S(2)}) %collective-permute-start.20) | collective-permute-done | bytes 32800 | tf_op jit(solution)/shard_map/ppermute | solution.py:165
  42.0 0.4 collective-permute-done.19.refs_2_
  42.4 0.6 %weight_grad.1 = bf16[256,256]{1,0:T(8,128)(2,1)S(1)} custom-call(s32[35]{0:T(128)S(1)} %pad_add_fusion.meta_ref.refs_0_, bf16[64,256]{1,0:T(8,128)(2,1)S(1)} %grad_row.1.refs_0_, bf16[64,256]{1,0:T(8,128)(2,1)S(1)} %collective-permute-done.18.refs_1_, bf16[64,256]{1,0:T(8,128)(2,1)S(1)} %collective-permute-done.19.refs_2_, ...), custom_call_target="tpu_custom_call" | custom-call | tf_op jit(solution)/shard_map/weight_grad/pallas_call | solution.py:185
  42.9 0.7 %convert_multiply_fusion = f32[256,256]{1,0:T(8,128)} fusion(bf16[256,256]{1,0:T(8,128)(2,1)S(1)} %weight_grad.1), kind=kLoop, calls=%fused_computation | loop fusion | flops 131072 | bytes 393216 | tf_op jit(solution)/shard_map/mul | solution.py:275
  (19 shorter events, 0.1 us)
Async XLA Ops:
  0.6 8.0 %collective-permute-start = (bf16[128,256]{1,0:T(8,128)(2,1)}, bf16[128,256]{1,0:T(8,128)(2,1)S(1)}, u32[]{:S(2)}, u32[]{:S(2)}) collective-permute-start(bf16[128,256]{1,0:T(8,128)(2,1)} %bitcast.11), channel_id=1, source_target_pairs={{0,2},{1,3},{2,0},{3,1},{4,6},{5,7},{6,4},{7,5},{8,10},{9,11},{10,... | collective-permute-start | bytes 196616 | tf_op jit(solution)/shard_map/ppermute | solution.py:165
  3.7 5.7 %collective-permute-start.5 = (bf16[128,256]{1,0:T(8,128)(2,1)}, bf16[128,256]{1,0:T(8,128)(2,1)S(1)}, u32[]{:S(2)}, u32[]{:S(2)}) collective-permute-start(bf16[128,256]{1,0:T(8,128)(2,1)} %bitcast.13), channel_id=1, source_target_pairs={{0,16},{4,20},{8,24},{12,28},{16,0},{20,4},{24,8},{28,12},{1,17},{... | collective-permute-start | bytes 196616 | tf_op jit(solution)/shard_map/ppermute | solution.py:165
  6.9 0.8 %copy-start.2 = (bf16[1,128,256]{2,1,0:T(8,128)(2,1)S(1)}, bf16[1,128,256]{2,1,0:T(8,128)(2,1)}, u32[]{:S(2)}) copy-start(bf16[1,128,256]{2,1,0:T(8,128)(2,1)} %param.11) | copy-start | bytes 196612
  7.7 0.8 %copy-start.3 = (bf16[1,128,256]{2,1,0:T(8,128)(2,1)S(1)}, bf16[1,128,256]{2,1,0:T(8,128)(2,1)}, u32[]{:S(2)}) copy-start(bf16[1,128,256]{2,1,0:T(8,128)(2,1)} %param.6) | copy-start | bytes 196612
  8.6 6.0 %collective-permute-start.1 = (bf16[2,128,256]{2,1,0:T(8,128)(2,1)S(1)}, bf16[2,128,256]{2,1,0:T(8,128)(2,1)S(1)}, u32[]{:S(2)}, u32[]{:S(2)}) collective-permute-start(bf16[2,128,256]{2,1,0:T(8,128)(2,1)S(1)} %cot_near.1.near_ref.refs_2_), channel_id=1, source_target_pairs={{0,1},{1,0},{2,3},{3,2},{4,5},{5,4},{6,7},{7,6},{8,9},{9,8},{10,11... | collective-permute-start | bytes 393224 | tf_op jit(solution)/shard_map/ppermute | solution.py:165
  9.3 4.3 %copy-start = (bf16[1,1,32,128,128]{4,3,2,1,0:T(8,128)(2,1)S(1)}, bf16[1,1,32,128,128]{4,3,2,1,0:T(8,128)(2,1)}, u32[]{:S(2)}) copy-start(bf16[1,1,32,128,128]{4,3,2,1,0:T(8,128)(2,1)} %param.8) | copy-start | bytes 3145732
  9.4 9.5 %collective-permute-start.8 = (bf16[2,128,256]{2,1,0:T(8,128)(2,1)S(1)}, bf16[2,128,256]{2,1,0:T(8,128)(2,1)S(1)}, u32[]{:S(2)}, u32[]{:S(2)}) collective-permute-start(bf16[2,128,256]{2,1,0:T(8,128)(2,1)S(1)} %pair.1.refs_7_), channel_id=1, source_target_pairs={{0,4},{4,0},{8,12},{12,8},{16,20},{20,16},{24,28},{28,24},{1,5},{5... | collective-permute-start | bytes 393224 | tf_op jit(solution)/shard_map/ppermute | solution.py:165
  10.9 0.7 %copy-start.4 = (s32[1,1,32]{2,1,0:T(1,128)S(1)}, s32[1,1,32]{2,1,0:T(1,128)}, u32[]{:S(2)}) copy-start(s32[1,1,32]{2,1,0:T(1,128)} %param.9) | copy-start | bytes 388
  11.6 7.7 %collective-permute-start.7 = (bf16[2,128,256]{2,1,0:T(8,128)(2,1)S(1)}, bf16[2,128,256]{2,1,0:T(8,128)(2,1)S(1)}, u32[]{:S(2)}, u32[]{:S(2)}) collective-permute-start(bf16[2,128,256]{2,1,0:T(8,128)(2,1)S(1)} %pair.1.refs_7_), channel_id=1, source_target_pairs={{0,8},{4,12},{8,0},{12,4},{16,24},{20,28},{24,16},{28,20},{1,9},{5... | collective-permute-start | bytes 393224 | tf_op jit(solution)/shard_map/ppermute | solution.py:165
  12.9 7.3 %collective-permute-start.6 = (bf16[2,128,256]{2,1,0:T(8,128)(2,1)S(1)}, bf16[2,128,256]{2,1,0:T(8,128)(2,1)S(1)}, u32[]{:S(2)}, u32[]{:S(2)}) collective-permute-start(bf16[2,128,256]{2,1,0:T(8,128)(2,1)S(1)} %pair.1.refs_7_), channel_id=1, source_target_pairs={{0,12},{4,8},{8,4},{12,0},{16,28},{20,24},{24,20},{28,16},{1,13},{... | collective-permute-start | bytes 393224 | tf_op jit(solution)/shard_map/ppermute | solution.py:165
  15.8 7.4 %collective-permute-start.2 = (bf16[2,128,256]{2,1,0:T(8,128)(2,1)S(1)}, bf16[2,128,256]{2,1,0:T(8,128)(2,1)S(1)}, u32[]{:S(2)}, u32[]{:S(2)}) collective-permute-start(bf16[2,128,256]{2,1,0:T(8,128)(2,1)S(1)} %get-tuple-element.23), channel_id=1, source_target_pairs={{0,12},{4,8},{8,4},{12,0},{16,28},{20,24},{24,20},{28,16},{1,13},{... | collective-permute-start | bytes 393224 | tf_op jit(solution)/shard_map/ppermute | solution.py:165
  18.1 7.1 %collective-permute-start.3 = (bf16[2,128,256]{2,1,0:T(8,128)(2,1)S(1)}, bf16[2,128,256]{2,1,0:T(8,128)(2,1)S(1)}, u32[]{:S(2)}, u32[]{:S(2)}) collective-permute-start(bf16[2,128,256]{2,1,0:T(8,128)(2,1)S(1)} %get-tuple-element.24), channel_id=1, source_target_pairs={{0,8},{4,12},{8,0},{12,4},{16,24},{20,28},{24,16},{28,20},{1,9},{5... | collective-permute-start | bytes 393224 | tf_op jit(solution)/shard_map/ppermute | solution.py:165
  18.9 6.2 %collective-permute-start.4 = (bf16[2,128,256]{2,1,0:T(8,128)(2,1)S(1)}, bf16[2,128,256]{2,1,0:T(8,128)(2,1)S(1)}, u32[]{:S(2)}, u32[]{:S(2)}) collective-permute-start(bf16[2,128,256]{2,1,0:T(8,128)(2,1)S(1)} %get-tuple-element.25), channel_id=1, source_target_pairs={{0,4},{4,0},{8,12},{12,8},{16,20},{20,16},{24,28},{28,24},{1,5},{5... | collective-permute-start | bytes 393224 | tf_op jit(solution)/shard_map/ppermute | solution.py:165
  21.6 4.2 %collective-permute-start.10 = (bf16[64,256]{1,0:T(8,128)(2,1)S(1)}, bf16[64,256]{1,0:T(8,128)(2,1)S(1)}, u32[]{:S(2)}, u32[]{:S(2)}) collective-permute-start(bf16[64,256]{1,0:T(8,128)(2,1)S(1)} %get-tuple-element.32), channel_id=1, source_target_pairs={{0,2},{1,3},{2,0},{3,1},{4,6},{5,7},{6,4},{7,5},{8,10},{9,11},{10,... | collective-permute-start | bytes 98312 | tf_op jit(solution)/shard_map/ppermute | solution.py:165
  22.1 3.7 %collective-permute-start.11 = (bf16[64,256]{1,0:T(8,128)(2,1)S(1)}, bf16[64,256]{1,0:T(8,128)(2,1)S(1)}, u32[]{:S(2)}, u32[]{:S(2)}) collective-permute-start(bf16[64,256]{1,0:T(8,128)(2,1)S(1)} %get-tuple-element.33), channel_id=1, source_target_pairs={{0,3},{1,2},{2,1},{3,0},{4,7},{5,6},{6,5},{7,4},{8,11},{9,10},{10,... | collective-permute-start | bytes 98312 | tf_op jit(solution)/shard_map/ppermute | solution.py:165
  23.2 2.6 %collective-permute-start.9 = (bf16[192,256]{1,0:T(8,128)(2,1)S(1)}, bf16[192,256]{1,0:T(8,128)(2,1)S(1)}, u32[]{:S(2)}, u32[]{:S(2)}) collective-permute-start(bf16[192,256]{1,0:T(8,128)(2,1)S(1)} %get-tuple-element.30), channel_id=1, source_target_pairs={{0,1},{1,0},{2,3},{3,2},{4,5},{5,4},{6,7},{7,6},{8,9},{9,8},{10,11... | collective-permute-start | bytes 294920 | tf_op jit(solution)/shard_map/ppermute | solution.py:165
  25.8 4.9 %collective-permute-start.14 = (bf16[64,256]{1,0:T(8,128)(2,1)S(1)}, bf16[64,256]{1,0:T(8,128)(2,1)S(1)}, u32[]{:S(2)}, u32[]{:S(2)}) collective-permute-start(bf16[64,256]{1,0:T(8,128)(2,1)S(1)} %grad_col.1.refs_1_), channel_id=1, source_target_pairs={{0,12},{4,8},{8,4},{12,0},{16,28},{20,24},{24,20},{28,16},{1,13},{... | collective-permute-start | bytes 98312 | tf_op jit(solution)/shard_map/ppermute | solution.py:165
  28.6 3.9 %collective-permute-start.13 = (bf16[64,256]{1,0:T(8,128)(2,1)S(1)}, bf16[64,256]{1,0:T(8,128)(2,1)S(1)}, u32[]{:S(2)}, u32[]{:S(2)}) collective-permute-start(bf16[64,256]{1,0:T(8,128)(2,1)S(1)} %grad_col.1.refs_1_), channel_id=1, source_target_pairs={{0,8},{4,12},{8,0},{12,4},{16,24},{20,28},{24,16},{28,20},{1,9},{5... | collective-permute-start | bytes 98312 | tf_op jit(solution)/shard_map/ppermute | solution.py:165
  28.7 3.9 %collective-permute-start.12 = (bf16[64,256]{1,0:T(8,128)(2,1)S(1)}, bf16[64,256]{1,0:T(8,128)(2,1)S(1)}, u32[]{:S(2)}, u32[]{:S(2)}) collective-permute-start(bf16[64,256]{1,0:T(8,128)(2,1)S(1)} %grad_col.1.refs_1_), channel_id=1, source_target_pairs={{0,4},{4,0},{8,12},{12,8},{16,20},{20,16},{24,28},{28,24},{1,5},{5... | collective-permute-start | bytes 98312 | tf_op jit(solution)/shard_map/ppermute | solution.py:165
  32.7 5.6 %collective-permute-start.15 = (bf16[192,256]{1,0:T(8,128)(2,1)S(1)}, bf16[192,256]{1,0:T(8,128)(2,1)S(1)}, u32[]{:S(2)}, u32[]{:S(2)}) collective-permute-start(bf16[192,256]{1,0:T(8,128)(2,1)S(1)} %grad_near.1.held_ref), channel_id=1, source_target_pairs={{0,16},{4,20},{8,24},{12,28},{16,0},{20,4},{24,8},{28,12},{1,17},{... | collective-permute-start | bytes 294920 | tf_op jit(solution)/shard_map/ppermute | solution.py:165
  35.2 5.4 %copy-start.1 = (bf16[256,256]{1,0:T(8,128)(2,1)S(1)}, bf16[256,256]{1,0:T(8,128)(2,1)}, u32[]{:S(2)}) copy-start(bf16[256,256]{1,0:T(8,128)(2,1)} %weight_ref.1) | copy-start | bytes 393220
  35.2 5.0 %collective-permute-start.16 = (bf16[128,256]{1,0:T(8,128)(2,1)S(1)}, bf16[128,256]{1,0:T(8,128)(2,1)S(1)}, u32[]{:S(2)}, u32[]{:S(2)}) collective-permute-start(bf16[128,256]{1,0:T(8,128)(2,1)S(1)} %get-tuple-element.37), channel_id=1, source_target_pairs={{0,2},{1,3},{2,0},{3,1},{4,6},{5,7},{6,4},{7,5},{8,10},{9,11},{10,... | collective-permute-start | bytes 196616 | tf_op jit(solution)/shard_map/ppermute | solution.py:165
  36.3 4.3 %collective-permute-start.17 = (bf16[128,256]{1,0:T(8,128)(2,1)S(1)}, bf16[128,256]{1,0:T(8,128)(2,1)S(1)}, u32[]{:S(2)}, u32[]{:S(2)}) collective-permute-start(bf16[128,256]{1,0:T(8,128)(2,1)S(1)} %get-tuple-element.38), channel_id=1, source_target_pairs={{0,3},{1,2},{2,1},{3,0},{4,7},{5,6},{6,5},{7,4},{8,11},{9,10},{10,... | collective-permute-start | bytes 196616 | tf_op jit(solution)/shard_map/ppermute | solution.py:165
  38.3 3.7 %collective-permute-start.20 = (bf16[64,256]{1,0:T(8,128)(2,1)S(1)}, bf16[64,256]{1,0:T(8,128)(2,1)S(1)}, u32[]{:S(2)}, u32[]{:S(2)}) collective-permute-start(bf16[64,256]{1,0:T(8,128)(2,1)S(1)} %grad_row.1.refs_0_), channel_id=1, source_target_pairs={{0,3},{1,2},{2,1},{3,0},{4,7},{5,6},{6,5},{7,4},{8,11},{9,10},{10,... | collective-permute-start | bytes 98312 | tf_op jit(solution)/shard_map/ppermute | solution.py:165
  38.3 4.0 %collective-permute-start.19 = (bf16[64,256]{1,0:T(8,128)(2,1)S(1)}, bf16[64,256]{1,0:T(8,128)(2,1)S(1)}, u32[]{:S(2)}, u32[]{:S(2)}) collective-permute-start(bf16[64,256]{1,0:T(8,128)(2,1)S(1)} %grad_row.1.refs_0_), channel_id=1, source_target_pairs={{0,2},{1,3},{2,0},{3,1},{4,6},{5,7},{6,4},{7,5},{8,10},{9,11},{10,... | collective-permute-start | bytes 98312 | tf_op jit(solution)/shard_map/ppermute | solution.py:165
  39.9 2.5 %collective-permute-start.18 = (bf16[64,256]{1,0:T(8,128)(2,1)S(1)}, bf16[64,256]{1,0:T(8,128)(2,1)S(1)}, u32[]{:S(2)}, u32[]{:S(2)}) collective-permute-start(bf16[64,256]{1,0:T(8,128)(2,1)S(1)} %grad_row.1.refs_0_), channel_id=1, source_target_pairs={{0,1},{1,0},{2,3},{3,2},{4,5},{5,4},{6,7},{7,6},{8,9},{9,8},{10,11... | collective-permute-start | bytes 98312 | tf_op jit(solution)/shard_map/ppermute | solution.py:165

commit v2 on v1

--- a/solution.py
+++ b/solution.py
@@ -214,7 +214,7 @@
             [VMEM] * len(arrays) + [ANY] * len(after), (*arrays, *after), micros=3,
         )
 
-    kept = hold([own, cotangent[0]], tile_counts, "own")
+    kept = hold([own, cotangent[0]], me, "own")
     pair = stack([kept[0], far], "pair")
     features_got = exchange([pair] * half, "row")
     cot_near = stack(

time: 43.8 us -> 45.3 us (1.034)
  waiting for transfers between devices: 11.1 us -> 13.7 us
  starting transfers between devices: 23 us -> 22 us
    ppermute x21, waiting for transfers between devices: 11.1 us -> 13.7 us  [swap(): return lax.ppermute(array, axis, pairs)]
    ppermute x21, starting transfers between devices: 23 us -> 22 us  [swap(): return lax.ppermute(array, axis, pairs)]
  transfers between devices with their start and end apart: 21 -> 21, of which waited for: 12 -> 10; matrix products, arithmetic and copies ran while one was open for 0% -> 0% of each run, Pallas kernels for 10% -> 10%
where the time goes in v2:
time: 45.3 us; the launch traced here: 45.6 us
  starting transfers between devices  22 us (49%)
  waiting for transfers between devices  13.7 us (30%)
  Pallas kernels  5.29 us (12%)
  local copies, waits for them, and re-layouts  2.34 us (5%)
  between operations  1.45 us (3%)
  other arithmetic  0.8 us (2%)
    ppermute x21, starting transfers between devices, swap(): return lax.ppermute(array, axis, pairs)  22 us
    ppermute x21, waiting for transfers between devices, swap(): return lax.ppermute(array, axis, pairs)  13.7 us
    pallas_call x13, Pallas kernels, call(): pl.pallas_call(kernel, out_shape=out_shape, in_specs=in_specs, out_specs=...  5.29 us
    unnamed x10, local copies, waits for them, and re-layouts  2.34 us
  transfers between devices with their start and end apart: 21, of which 10 were waited for; matrix products, arithmetic and copies ran while one was open for 0% of the time, Pallas kernels for 10%

profile of v2, /device:TPU:0, one launch (start us, length us, event | category | flops | bytes accessed | tf_op | source)
XLA Modules:
  0.0 45.6 jit_solution(7116608202406903284)
XLA Ops:
  0.6 4.1 %collective-permute-start.5 = (bf16[128,256]{1,0:T(8,128)(2,1)}, bf16[128,256]{1,0:T(8,128)(2,1)S(1)}, u32[]{:S(2)}, u32[]{:S(2)}) collective-permute-start(bf16[128,256]{1,0:T(8,128)(2,1)} %bitcast.13), channel_id=1, source_target_pairs={{0,16},{4,20},{8,24},{12,28},{16,0},{20,4},{24,8},{28,12},{1,17},{... | collective-permute-start | bytes 196616 | tf_op jit(solution)/shard_map/ppermute | solution.py:165
  4.7 1.5 %collective-permute-start = (bf16[128,256]{1,0:T(8,128)(2,1)}, bf16[128,256]{1,0:T(8,128)(2,1)S(1)}, u32[]{:S(2)}, u32[]{:S(2)}) collective-permute-start(bf16[128,256]{1,0:T(8,128)(2,1)} %bitcast.11), channel_id=1, source_target_pairs={{0,2},{1,3},{2,0},{3,1},{4,6},{5,7},{6,4},{7,5},{8,10},{9,11},{10,... | collective-permute-start | bytes 196616 | tf_op jit(solution)/shard_map/ppermute | solution.py:165
  6.9 0.6 %copy-done.4 = s32[1,1,32]{2,1,0:T(1,128)S(1)} copy-done((s32[1,1,32]{2,1,0:T(1,128)S(1)}, s32[1,1,32]{2,1,0:T(1,128)}, u32[]{:S(2)}) %copy-start.4) | copy-done | bytes 152
  7.6 0.1 pad_add_fusion.meta_ref.refs_2_.refs_0_
  7.6 0.8 %copy-done.2 = bf16[1,128,256]{2,1,0:T(8,128)(2,1)S(1)} copy-done((bf16[1,128,256]{2,1,0:T(8,128)(2,1)S(1)}, bf16[1,128,256]{2,1,0:T(8,128)(2,1)}, u32[]{:S(2)}) %copy-start.2) | copy-done | bytes 65560
  8.5 0.8 %copy-done.3 = bf16[1,128,256]{2,1,0:T(8,128)(2,1)S(1)} copy-done((bf16[1,128,256]{2,1,0:T(8,128)(2,1)S(1)}, bf16[1,128,256]{2,1,0:T(8,128)(2,1)}, u32[]{:S(2)}) %copy-start.3) | copy-done | bytes 65560
  9.4 0.1 collective-permute-start.1
  9.4 0.0 copy-start
  9.5 1.6 %collective-permute-start.8 = (bf16[2,128,256]{2,1,0:T(8,128)(2,1)S(1)}, bf16[2,128,256]{2,1,0:T(8,128)(2,1)S(1)}, u32[]{:S(2)}, u32[]{:S(2)}) collective-permute-start(bf16[2,128,256]{2,1,0:T(8,128)(2,1)S(1)} %pair.1.refs_7_), channel_id=1, source_target_pairs={{0,4},{4,0},{8,12},{12,8},{16,20},{20,16},{24,28},{28,24},{1,5},{5... | collective-permute-start | bytes 393224 | tf_op jit(solution)/shard_map/ppermute | solution.py:165
  11.0 1.6 %collective-permute-start.7 = (bf16[2,128,256]{2,1,0:T(8,128)(2,1)S(1)}, bf16[2,128,256]{2,1,0:T(8,128)(2,1)S(1)}, u32[]{:S(2)}, u32[]{:S(2)}) collective-permute-start(bf16[2,128,256]{2,1,0:T(8,128)(2,1)S(1)} %pair.1.refs_7_), channel_id=1, source_target_pairs={{0,8},{4,12},{8,0},{12,4},{16,24},{20,28},{24,16},{28,20},{1,9},{5... | collective-permute-start | bytes 393224 | tf_op jit(solution)/shard_map/ppermute | solution.py:165
  12.6 0.4 collective-permute-start.6
  13.0 1.3 %dense.1.adj_ref.refs_1_ = bf16[512,1024]{1,0:T(8,128)(2,1)S(1)} custom-call(s32[35]{0:T(128)S(1)} %pad_add_fusion.meta_ref.refs_2_.refs_0_, bf16[32,128,128]{2,1,0:T(8,128)(2,1)S(1)} %bitcast.10), custom_call_target="tpu_custom_call" | custom-call | tf_op jit(solution)/shard_map/dense/pallas_call | solution.py:185
  14.4 0.0 collective-permute-done.1.other_ref.refs_3_
  14.4 1.1 %backward.1 = (bf16[2,128,256]{2,1,0:T(8,128)(2,1)S(1)}, bf16[2,128,256]{2,1,0:T(8,128)(2,1)S(1)}, bf16[2,128,256]{2,1,0:T(8,128)(2,1)S(1)}, bf16[2,128,256]{2,1,0:T(8,128)(2,1)S(1)}) custom-call(s32[35]{0:T(128)S(1)} %pad_add_fusion.meta_ref.refs_2_.refs_0_, bf16[512,1024]{1,0:T(8,128)(2,1)S(1)} %dense.1.adj_ref.refs_1_, ...), custom_call_target="tpu_custom_call" | custom-call | tf_op jit(solution)/shard_map/backward/pallas_call | solution.py:185
  15.5 2.3 %collective-permute-start.2 = (bf16[2,128,256]{2,1,0:T(8,128)(2,1)S(1)}, bf16[2,128,256]{2,1,0:T(8,128)(2,1)S(1)}, u32[]{:S(2)}, u32[]{:S(2)}) collective-permute-start(bf16[2,128,256]{2,1,0:T(8,128)(2,1)S(1)} %get-tuple-element.23), channel_id=1, source_target_pairs={{0,12},{4,8},{8,4},{12,0},{16,28},{20,24},{24,20},{28,16},{1,13},{... | collective-permute-start | bytes 393224 | tf_op jit(solution)/shard_map/ppermute | solution.py:165
  17.8 0.4 collective-permute-start.3
  18.2 0.8 %collective-permute-start.4 = (bf16[2,128,256]{2,1,0:T(8,128)(2,1)S(1)}, bf16[2,128,256]{2,1,0:T(8,128)(2,1)S(1)}, u32[]{:S(2)}, u32[]{:S(2)}) collective-permute-start(bf16[2,128,256]{2,1,0:T(8,128)(2,1)S(1)} %get-tuple-element.25), channel_id=1, source_target_pairs={{0,4},{4,0},{8,12},{12,8},{16,20},{20,16},{24,28},{28,24},{1,5},{5... | collective-permute-start | bytes 393224 | tf_op jit(solution)/shard_map/ppermute | solution.py:165
  19.0 0.0 collective-permute-done.7.refs_5_
  19.0 0.8 %collective-permute-done.6.refs_4_ = bf16[2,128,256]{2,1,0:T(8,128)(2,1)S(1)} collective-permute-done((bf16[2,128,256]{2,1,0:T(8,128)(2,1)S(1)}, bf16[2,128,256]{2,1,0:T(8,128)(2,1)S(1)}, u32[]{:S(2)}, u32[]{:S(2)}) %collective-permute-start.6) | collective-permute-done | bytes 131104 | tf_op jit(solution)/shard_map/ppermute | solution.py:165
  19.9 1.3 %forward.1 = (bf16[128,256]{1,0:T(8,128)(2,1)S(1)}, bf16[128,256]{1,0:T(8,128)(2,1)S(1)}, bf16[128,256]{1,0:T(8,128)(2,1)S(1)}, bf16[64,256]{1,0:T(8,128)(2,1)S(...) custom-call(s32[35]{0:T(128)S(1)} %pad_add_fusion.meta_ref.refs_2_.refs_0_, ...), custom_call_target="tpu_custom_call" | custom-call | tf_op jit(solution)/shard_map/forward/pallas_call | solution.py:185
  21.2 1.3 %collective-permute-start.10 = (bf16[64,256]{1,0:T(8,128)(2,1)S(1)}, bf16[64,256]{1,0:T(8,128)(2,1)S(1)}, u32[]{:S(2)}, u32[]{:S(2)}) collective-permute-start(bf16[64,256]{1,0:T(8,128)(2,1)S(1)} %get-tuple-element.32), channel_id=1, source_target_pairs={{0,2},{1,3},{2,0},{3,1},{4,6},{5,7},{6,4},{7,5},{8,10},{9,11},{10,... | collective-permute-start | bytes 98312 | tf_op jit(solution)/shard_map/ppermute | solution.py:165
  22.5 0.0 collective-permute-start.11
  22.5 0.4 collective-permute-done.2.refs_0_
  22.9 0.5 %collective-permute-start.9 = (bf16[192,256]{1,0:T(8,128)(2,1)S(1)}, bf16[192,256]{1,0:T(8,128)(2,1)S(1)}, u32[]{:S(2)}, u32[]{:S(2)}) collective-permute-start(bf16[192,256]{1,0:T(8,128)(2,1)S(1)} %get-tuple-element.30), channel_id=1, source_target_pairs={{0,1},{1,0},{2,3},{3,2},{4,5},{5,4},{6,7},{7,6},{8,9},{9,8},{10,11... | collective-permute-start | bytes 294920 | tf_op jit(solution)/shard_map/ppermute | solution.py:165
  23.4 1.7 %collective-permute-done.3.refs_1_ = bf16[2,128,256]{2,1,0:T(8,128)(2,1)S(1)} collective-permute-done((bf16[2,128,256]{2,1,0:T(8,128)(2,1)S(1)}, bf16[2,128,256]{2,1,0:T(8,128)(2,1)S(1)}, u32[]{:S(2)}, u32[]{:S(2)}) %collective-permute-start.3) | collective-permute-done | bytes 131104 | tf_op jit(solution)/shard_map/ppermute | solution.py:165
  25.1 0.0 collective-permute-done.4.refs_2_
  25.1 0.1 pair_sum.1
  25.2 0.7 %collective-permute-done.11.refs_3_ = bf16[64,256]{1,0:T(8,128)(2,1)S(1)} collective-permute-done((bf16[64,256]{1,0:T(8,128)(2,1)S(1)}, bf16[64,256]{1,0:T(8,128)(2,1)S(1)}, u32[]{:S(2)}, u32[]{:S(2)}) %collective-permute-start.11) | collective-permute-done | bytes 32800 | tf_op jit(solution)/shard_map/ppermute | solution.py:165
  25.9 0.0 collective-permute-done.9.refs_0_.first_ref
  25.9 2.8 %collective-permute-start.14 = (bf16[64,256]{1,0:T(8,128)(2,1)S(1)}, bf16[64,256]{1,0:T(8,128)(2,1)S(1)}, u32[]{:S(2)}, u32[]{:S(2)}) collective-permute-start(bf16[64,256]{1,0:T(8,128)(2,1)S(1)} %grad_col.1.refs_1_), channel_id=1, source_target_pairs={{0,12},{4,8},{8,4},{12,0},{16,28},{20,24},{24,20},{28,16},{1,13},{... | collective-permute-start | bytes 98312 | tf_op jit(solution)/shard_map/ppermute | solution.py:165
  28.7 0.7 %collective-permute-start.13 = (bf16[64,256]{1,0:T(8,128)(2,1)S(1)}, bf16[64,256]{1,0:T(8,128)(2,1)S(1)}, u32[]{:S(2)}, u32[]{:S(2)}) collective-permute-start(bf16[64,256]{1,0:T(8,128)(2,1)S(1)} %grad_col.1.refs_1_), channel_id=1, source_target_pairs={{0,8},{4,12},{8,0},{12,4},{16,24},{20,28},{24,16},{28,20},{1,9},{5... | collective-permute-start | bytes 98312 | tf_op jit(solution)/shard_map/ppermute | solution.py:165
  29.4 0.1 collective-permute-start.12
  29.4 1.3 %collective-permute-done.14.refs_4_.refs_2_ = bf16[64,256]{1,0:T(8,128)(2,1)S(1)} collective-permute-done((bf16[64,256]{1,0:T(8,128)(2,1)S(1)}, bf16[64,256]{1,0:T(8,128)(2,1)S(1)}, u32[]{:S(2)}, u32[]{:S(2)}) %collective-permute-start.14) | collective-permute-done | bytes 32800 | tf_op jit(solution)/shard_map/ppermute | solution.py:165
  30.8 1.8 %collective-permute-done.13.refs_3_ = bf16[64,256]{1,0:T(8,128)(2,1)S(1)} collective-permute-done((bf16[64,256]{1,0:T(8,128)(2,1)S(1)}, bf16[64,256]{1,0:T(8,128)(2,1)S(1)}, u32[]{:S(2)}, u32[]{:S(2)}) %collective-permute-start.13) | collective-permute-done | bytes 32800 | tf_op jit(solution)/shard_map/ppermute | solution.py:165
  32.6 0.7 %collective-permute-done.12.refs_2_ = bf16[64,256]{1,0:T(8,128)(2,1)S(1)} collective-permute-done((bf16[64,256]{1,0:T(8,128)(2,1)S(1)}, bf16[64,256]{1,0:T(8,128)(2,1)S(1)}, u32[]{:S(2)}, u32[]{:S(2)}) %collective-permute-start.12) | collective-permute-done | bytes 32800 | tf_op jit(solution)/shard_map/ppermute | solution.py:165
  33.3 0.7 %collective-permute-start.15 = (bf16[192,256]{1,0:T(8,128)(2,1)S(1)}, bf16[192,256]{1,0:T(8,128)(2,1)S(1)}, u32[]{:S(2)}, u32[]{:S(2)}) collective-permute-start(bf16[192,256]{1,0:T(8,128)(2,1)S(1)} %grad_near.1.held_ref), channel_id=1, source_target_pairs={{0,16},{4,20},{8,24},{12,28},{16,0},{20,4},{24,8},{28,12},{1,17},{... | collective-permute-start | bytes 294920 | tf_op jit(solution)/shard_map/ppermute | solution.py:165
  34.1 0.0 copy-start.1
  34.1 1.2 %collective-permute-start.16 = (bf16[128,256]{1,0:T(8,128)(2,1)S(1)}, bf16[128,256]{1,0:T(8,128)(2,1)S(1)}, u32[]{:S(2)}, u32[]{:S(2)}) collective-permute-start(bf16[128,256]{1,0:T(8,128)(2,1)S(1)} %get-tuple-element.37), channel_id=1, source_target_pairs={{0,2},{1,3},{2,0},{3,1},{4,6},{5,7},{6,4},{7,5},{8,10},{9,11},{10,... | collective-permute-start | bytes 196616 | tf_op jit(solution)/shard_map/ppermute | solution.py:165
  35.2 4.7 %collective-permute-done.15.far_ref.got_ref = bf16[192,256]{1,0:T(8,128)(2,1)S(1)} collective-permute-done((bf16[192,256]{1,0:T(8,128)(2,1)S(1)}, bf16[192,256]{1,0:T(8,128)(2,1)S(1)}, u32[]{:S(2)}, u32[]{:S(2)}) %collective-permute-start.15) | collective-permute-done | bytes 98336 | tf_op jit(solution)/shard_map/ppermute | solution.py:165
  39.9 0.1 collective-permute-start.20
  40.0 1.1 %collective-permute-start.19 = (bf16[64,256]{1,0:T(8,128)(2,1)S(1)}, bf16[64,256]{1,0:T(8,128)(2,1)S(1)}, u32[]{:S(2)}, u32[]{:S(2)}) collective-permute-start(bf16[64,256]{1,0:T(8,128)(2,1)S(1)} %grad_row.1.refs_0_), channel_id=1, source_target_pairs={{0,2},{1,3},{2,0},{3,1},{4,6},{5,7},{6,4},{7,5},{8,10},{9,11},{10,... | collective-permute-start | bytes 98312 | tf_op jit(solution)/shard_map/ppermute | solution.py:165
  41.1 0.8 %collective-permute-start.18 = (bf16[64,256]{1,0:T(8,128)(2,1)S(1)}, bf16[64,256]{1,0:T(8,128)(2,1)S(1)}, u32[]{:S(2)}, u32[]{:S(2)}) collective-permute-start(bf16[64,256]{1,0:T(8,128)(2,1)S(1)} %grad_row.1.refs_0_), channel_id=1, source_target_pairs={{0,1},{1,0},{2,3},{3,2},{4,5},{5,4},{6,7},{7,6},{8,9},{9,8},{10,11... | collective-permute-start | bytes 98312 | tf_op jit(solution)/shard_map/ppermute | solution.py:165
  41.9 0.0 collective-permute-done.16.refs_1_
  41.9 0.8 %outputs.1 = (bf16[128,256]{1,0:T(8,128)(2,1)}, bf16[128,256]{1,0:T(8,128)(2,1)}) custom-call(bf16[256,256]{1,0:T(8,128)(2,1)S(1)} %copy-done.1, f32[128,256]{1,0:T(8,128)S(1)} %get-tuple-element.27.keep_ref, bf16[192,256]{1,0:T(8,128)(2,1)S(1)} %collective-permute-done.15.far_ref.got_ref, bf16[192,256]{1,0:T(8,128)(2,1)S(1)} %collective-permute-done.9.refs_0_.first_ref, ...), custom_call_target="tpu_custom_call" | custom-call | tf_op jit(solution)/shard_map/outputs/pallas_call | solution.py:185
  42.7 0.6 %collective-permute-done.20.refs_3_ = bf16[64,256]{1,0:T(8,128)(2,1)S(1)} collective-permute-done((bf16[64,256]{1,0:T(8,128)(2,1)S(1)}, bf16[64,256]{1,0:T(8,128)(2,1)S(1)}, u32[]{:S(2)}, u32[]{:S(2)}) %collective-permute-start.20) | collective-permute-done | bytes 32800 | tf_op jit(solution)/shard_map/ppermute | solution.py:165
  43.4 0.9 %collective-permute-done.19.refs_2_ = bf16[64,256]{1,0:T(8,128)(2,1)S(1)} collective-permute-done((bf16[64,256]{1,0:T(8,128)(2,1)S(1)}, bf16[64,256]{1,0:T(8,128)(2,1)S(1)}, u32[]{:S(2)}, u32[]{:S(2)}) %collective-permute-start.19) | collective-permute-done | bytes 32800 | tf_op jit(solution)/shard_map/ppermute | solution.py:165
  44.3 0.6 %weight_grad.1 = bf16[256,256]{1,0:T(8,128)(2,1)S(1)} custom-call(s32[35]{0:T(128)S(1)} %pad_add_fusion.meta_ref.refs_2_.refs_0_, bf16[64,256]{1,0:T(8,128)(2,1)S(1)} %grad_row.1.refs_0_, bf16[64,256]{1,0:T(8,128)(2,1)S(1)} %collective-permute-done.18.refs_1_, bf16[64,256]{1,0:T(8,128)(2,1)S(1)} %collective-permute-done.19.refs_2_, ...), custom_call_target="tpu_custom_call" | custom-call | tf_op jit(solution)/shard_map/weight_grad/pallas_call | solution.py:185
  44.8 0.7 %convert_multiply_fusion = f32[256,256]{1,0:T(8,128)} fusion(bf16[256,256]{1,0:T(8,128)(2,1)S(1)} %weight_grad.1), kind=kLoop, calls=%fused_computation | loop fusion | flops 131072 | bytes 393216 | tf_op jit(solution)/shard_map/mul | solution.py:275
  (19 shorter events, 0.1 us)
Async XLA Ops:
  0.6 8.8 %collective-permute-start.5 = (bf16[128,256]{1,0:T(8,128)(2,1)}, bf16[128,256]{1,0:T(8,128)(2,1)S(1)}, u32[]{:S(2)}, u32[]{:S(2)}) collective-permute-start(bf16[128,256]{1,0:T(8,128)(2,1)} %bitcast.13), channel_id=1, source_target_pairs={{0,16},{4,20},{8,24},{12,28},{16,0},{20,4},{24,8},{28,12},{1,17},{... | collective-permute-start | bytes 196616 | tf_op jit(solution)/shard_map/ppermute | solution.py:165
  4.7 4.6 %collective-permute-start = (bf16[128,256]{1,0:T(8,128)(2,1)}, bf16[128,256]{1,0:T(8,128)(2,1)S(1)}, u32[]{:S(2)}, u32[]{:S(2)}) collective-permute-start(bf16[128,256]{1,0:T(8,128)(2,1)} %bitcast.11), channel_id=1, source_target_pairs={{0,2},{1,3},{2,0},{3,1},{4,6},{5,7},{6,4},{7,5},{8,10},{9,11},{10,... | collective-permute-start | bytes 196616 | tf_op jit(solution)/shard_map/ppermute | solution.py:165
  6.9 0.7 %copy-start.4 = (s32[1,1,32]{2,1,0:T(1,128)S(1)}, s32[1,1,32]{2,1,0:T(1,128)}, u32[]{:S(2)}) copy-start(s32[1,1,32]{2,1,0:T(1,128)} %param.9) | copy-start | bytes 388
  7.6 0.8 %copy-start.2 = (bf16[1,128,256]{2,1,0:T(8,128)(2,1)S(1)}, bf16[1,128,256]{2,1,0:T(8,128)(2,1)}, u32[]{:S(2)}) copy-start(bf16[1,128,256]{2,1,0:T(8,128)(2,1)} %param.11) | copy-start | bytes 196612
  8.5 0.8 %copy-start.3 = (bf16[1,128,256]{2,1,0:T(8,128)(2,1)S(1)}, bf16[1,128,256]{2,1,0:T(8,128)(2,1)}, u32[]{:S(2)}) copy-start(bf16[1,128,256]{2,1,0:T(8,128)(2,1)} %param.6) | copy-start | bytes 196612
  9.4 5.0 %collective-permute-start.1 = (bf16[2,128,256]{2,1,0:T(8,128)(2,1)S(1)}, bf16[2,128,256]{2,1,0:T(8,128)(2,1)S(1)}, u32[]{:S(2)}, u32[]{:S(2)}) collective-permute-start(bf16[2,128,256]{2,1,0:T(8,128)(2,1)S(1)} %cot_near.1.near_ref.refs_2_), channel_id=1, source_target_pairs={{0,1},{1,0},{2,3},{3,2},{4,5},{5,4},{6,7},{7,6},{8,9},{9,8},{10,11... | collective-permute-start | bytes 393224 | tf_op jit(solution)/shard_map/ppermute | solution.py:165
  9.4 3.6 %copy-start = (bf16[1,1,32,128,128]{4,3,2,1,0:T(8,128)(2,1)S(1)}, bf16[1,1,32,128,128]{4,3,2,1,0:T(8,128)(2,1)}, u32[]{:S(2)}) copy-start(bf16[1,1,32,128,128]{4,3,2,1,0:T(8,128)(2,1)} %param.8) | copy-start | bytes 3145732
  9.5 8.7 %collective-permute-start.8 = (bf16[2,128,256]{2,1,0:T(8,128)(2,1)S(1)}, bf16[2,128,256]{2,1,0:T(8,128)(2,1)S(1)}, u32[]{:S(2)}, u32[]{:S(2)}) collective-permute-start(bf16[2,128,256]{2,1,0:T(8,128)(2,1)S(1)} %pair.1.refs_7_), channel_id=1, source_target_pairs={{0,4},{4,0},{8,12},{12,8},{16,20},{20,16},{24,28},{28,24},{1,5},{5... | collective-permute-start | bytes 393224 | tf_op jit(solution)/shard_map/ppermute | solution.py:165
  11.0 8.0 %collective-permute-start.7 = (bf16[2,128,256]{2,1,0:T(8,128)(2,1)S(1)}, bf16[2,128,256]{2,1,0:T(8,128)(2,1)S(1)}, u32[]{:S(2)}, u32[]{:S(2)}) collective-permute-start(bf16[2,128,256]{2,1,0:T(8,128)(2,1)S(1)} %pair.1.refs_7_), channel_id=1, source_target_pairs={{0,8},{4,12},{8,0},{12,4},{16,24},{20,28},{24,16},{28,20},{1,9},{5... | collective-permute-start | bytes 393224 | tf_op jit(solution)/shard_map/ppermute | solution.py:165
  12.6 7.3 %collective-permute-start.6 = (bf16[2,128,256]{2,1,0:T(8,128)(2,1)S(1)}, bf16[2,128,256]{2,1,0:T(8,128)(2,1)S(1)}, u32[]{:S(2)}, u32[]{:S(2)}) collective-permute-start(bf16[2,128,256]{2,1,0:T(8,128)(2,1)S(1)} %pair.1.refs_7_), channel_id=1, source_target_pairs={{0,12},{4,8},{8,4},{12,0},{16,28},{20,24},{24,20},{28,16},{1,13},{... | collective-permute-start | bytes 393224 | tf_op jit(solution)/shard_map/ppermute | solution.py:165
  15.5 7.4 %collective-permute-start.2 = (bf16[2,128,256]{2,1,0:T(8,128)(2,1)S(1)}, bf16[2,128,256]{2,1,0:T(8,128)(2,1)S(1)}, u32[]{:S(2)}, u32[]{:S(2)}) collective-permute-start(bf16[2,128,256]{2,1,0:T(8,128)(2,1)S(1)} %get-tuple-element.23), channel_id=1, source_target_pairs={{0,12},{4,8},{8,4},{12,0},{16,28},{20,24},{24,20},{28,16},{1,13},{... | collective-permute-start | bytes 393224 | tf_op jit(solution)/shard_map/ppermute | solution.py:165
  17.8 7.3 %collective-permute-start.3 = (bf16[2,128,256]{2,1,0:T(8,128)(2,1)S(1)}, bf16[2,128,256]{2,1,0:T(8,128)(2,1)S(1)}, u32[]{:S(2)}, u32[]{:S(2)}) collective-permute-start(bf16[2,128,256]{2,1,0:T(8,128)(2,1)S(1)} %get-tuple-element.24), channel_id=1, source_target_pairs={{0,8},{4,12},{8,0},{12,4},{16,24},{20,28},{24,16},{28,20},{1,9},{5... | collective-permute-start | bytes 393224 | tf_op jit(solution)/shard_map/ppermute | solution.py:165
  18.2 6.9 %collective-permute-start.4 = (bf16[2,128,256]{2,1,0:T(8,128)(2,1)S(1)}, bf16[2,128,256]{2,1,0:T(8,128)(2,1)S(1)}, u32[]{:S(2)}, u32[]{:S(2)}) collective-permute-start(bf16[2,128,256]{2,1,0:T(8,128)(2,1)S(1)} %get-tuple-element.25), channel_id=1, source_target_pairs={{0,4},{4,0},{8,12},{12,8},{16,20},{20,16},{24,28},{28,24},{1,5},{5... | collective-permute-start | bytes 393224 | tf_op jit(solution)/shard_map/ppermute | solution.py:165
  21.2 4.0 %collective-permute-start.10 = (bf16[64,256]{1,0:T(8,128)(2,1)S(1)}, bf16[64,256]{1,0:T(8,128)(2,1)S(1)}, u32[]{:S(2)}, u32[]{:S(2)}) collective-permute-start(bf16[64,256]{1,0:T(8,128)(2,1)S(1)} %get-tuple-element.32), channel_id=1, source_target_pairs={{0,2},{1,3},{2,0},{3,1},{4,6},{5,7},{6,4},{7,5},{8,10},{9,11},{10,... | collective-permute-start | bytes 98312 | tf_op jit(solution)/shard_map/ppermute | solution.py:165
  22.5 3.4 %collective-permute-start.11 = (bf16[64,256]{1,0:T(8,128)(2,1)S(1)}, bf16[64,256]{1,0:T(8,128)(2,1)S(1)}, u32[]{:S(2)}, u32[]{:S(2)}) collective-permute-start(bf16[64,256]{1,0:T(8,128)(2,1)S(1)} %get-tuple-element.33), channel_id=1, source_target_pairs={{0,3},{1,2},{2,1},{3,0},{4,7},{5,6},{6,5},{7,4},{8,11},{9,10},{10,... | collective-permute-start | bytes 98312 | tf_op jit(solution)/shard_map/ppermute | solution.py:165
  22.9 3.0 %collective-permute-start.9 = (bf16[192,256]{1,0:T(8,128)(2,1)S(1)}, bf16[192,256]{1,0:T(8,128)(2,1)S(1)}, u32[]{:S(2)}, u32[]{:S(2)}) collective-permute-start(bf16[192,256]{1,0:T(8,128)(2,1)S(1)} %get-tuple-element.30), channel_id=1, source_target_pairs={{0,1},{1,0},{2,3},{3,2},{4,5},{5,4},{6,7},{7,6},{8,9},{9,8},{10,11... | collective-permute-start | bytes 294920 | tf_op jit(solution)/shard_map/ppermute | solution.py:165
  25.9 4.9 %collective-permute-start.14 = (bf16[64,256]{1,0:T(8,128)(2,1)S(1)}, bf16[64,256]{1,0:T(8,128)(2,1)S(1)}, u32[]{:S(2)}, u32[]{:S(2)}) collective-permute-start(bf16[64,256]{1,0:T(8,128)(2,1)S(1)} %grad_col.1.refs_1_), channel_id=1, source_target_pairs={{0,12},{4,8},{8,4},{12,0},{16,28},{20,24},{24,20},{28,16},{1,13},{... | collective-permute-start | bytes 98312 | tf_op jit(solution)/shard_map/ppermute | solution.py:165
  28.7 3.9 %collective-permute-start.13 = (bf16[64,256]{1,0:T(8,128)(2,1)S(1)}, bf16[64,256]{1,0:T(8,128)(2,1)S(1)}, u32[]{:S(2)}, u32[]{:S(2)}) collective-permute-start(bf16[64,256]{1,0:T(8,128)(2,1)S(1)} %grad_col.1.refs_1_), channel_id=1, source_target_pairs={{0,8},{4,12},{8,0},{12,4},{16,24},{20,28},{24,16},{28,20},{1,9},{5... | collective-permute-start | bytes 98312 | tf_op jit(solution)/shard_map/ppermute | solution.py:165
  29.4 3.9 %collective-permute-start.12 = (bf16[64,256]{1,0:T(8,128)(2,1)S(1)}, bf16[64,256]{1,0:T(8,128)(2,1)S(1)}, u32[]{:S(2)}, u32[]{:S(2)}) collective-permute-start(bf16[64,256]{1,0:T(8,128)(2,1)S(1)} %grad_col.1.refs_1_), channel_id=1, source_target_pairs={{0,4},{4,0},{8,12},{12,8},{16,20},{20,16},{24,28},{28,24},{1,5},{5... | collective-permute-start | bytes 98312 | tf_op jit(solution)/shard_map/ppermute | solution.py:165
  33.3 6.6 %collective-permute-start.15 = (bf16[192,256]{1,0:T(8,128)(2,1)S(1)}, bf16[192,256]{1,0:T(8,128)(2,1)S(1)}, u32[]{:S(2)}, u32[]{:S(2)}) collective-permute-start(bf16[192,256]{1,0:T(8,128)(2,1)S(1)} %grad_near.1.held_ref), channel_id=1, source_target_pairs={{0,16},{4,20},{8,24},{12,28},{16,0},{20,4},{24,8},{28,12},{1,17},{... | collective-permute-start | bytes 294920 | tf_op jit(solution)/shard_map/ppermute | solution.py:165
  34.1 7.8 %copy-start.1 = (bf16[256,256]{1,0:T(8,128)(2,1)S(1)}, bf16[256,256]{1,0:T(8,128)(2,1)}, u32[]{:S(2)}) copy-start(bf16[256,256]{1,0:T(8,128)(2,1)} %weight_ref.1) | copy-start | bytes 393220
  34.1 7.8 %collective-permute-start.16 = (bf16[128,256]{1,0:T(8,128)(2,1)S(1)}, bf16[128,256]{1,0:T(8,128)(2,1)S(1)}, u32[]{:S(2)}, u32[]{:S(2)}) collective-permute-start(bf16[128,256]{1,0:T(8,128)(2,1)S(1)} %get-tuple-element.37), channel_id=1, source_target_pairs={{0,2},{1,3},{2,0},{3,1},{4,6},{5,7},{6,4},{7,5},{8,10},{9,11},{10,... | collective-permute-start | bytes 196616 | tf_op jit(solution)/shard_map/ppermute | solution.py:165
  35.2 6.7 %collective-permute-start.17 = (bf16[128,256]{1,0:T(8,128)(2,1)S(1)}, bf16[128,256]{1,0:T(8,128)(2,1)S(1)}, u32[]{:S(2)}, u32[]{:S(2)}) collective-permute-start(bf16[128,256]{1,0:T(8,128)(2,1)S(1)} %get-tuple-element.38), channel_id=1, source_target_pairs={{0,3},{1,2},{2,1},{3,0},{4,7},{5,6},{6,5},{7,4},{8,11},{9,10},{10,... | collective-permute-start | bytes 196616 | tf_op jit(solution)/shard_map/ppermute | solution.py:165
  39.9 3.4 %collective-permute-start.20 = (bf16[64,256]{1,0:T(8,128)(2,1)S(1)}, bf16[64,256]{1,0:T(8,128)(2,1)S(1)}, u32[]{:S(2)}, u32[]{:S(2)}) collective-permute-start(bf16[64,256]{1,0:T(8,128)(2,1)S(1)} %grad_row.1.refs_0_), channel_id=1, source_target_pairs={{0,3},{1,2},{2,1},{3,0},{4,7},{5,6},{6,5},{7,4},{8,11},{9,10},{10,... | collective-permute-start | bytes 98312 | tf_op jit(solution)/shard_map/ppermute | solution.py:165
  40.0 4.2 %collective-permute-start.19 = (bf16[64,256]{1,0:T(8,128)(2,1)S(1)}, bf16[64,256]{1,0:T(8,128)(2,1)S(1)}, u32[]{:S(2)}, u32[]{:S(2)}) collective-permute-start(bf16[64,256]{1,0:T(8,128)(2,1)S(1)} %grad_row.1.refs_0_), channel_id=1, source_target_pairs={{0,2},{1,3},{2,0},{3,1},{4,6},{5,7},{6,4},{7,5},{8,10},{9,11},{10,... | collective-permute-start | bytes 98312 | tf_op jit(solution)/shard_map/ppermute | solution.py:165
  41.1 3.2 %collective-permute-start.18 = (bf16[64,256]{1,0:T(8,128)(2,1)S(1)}, bf16[64,256]{1,0:T(8,128)(2,1)S(1)}, u32[]{:S(2)}, u32[]{:S(2)}) collective-permute-start(bf16[64,256]{1,0:T(8,128)(2,1)S(1)} %grad_row.1.refs_0_), channel_id=1, source_target_pairs={{0,1},{1,0},{2,3},{3,2},{4,5},{5,4},{6,7},{7,6},{8,9},{9,8},{10,11... | collective-permute-start | bytes 98312 | tf_op jit(solution)/shard_map/ppermute | solution.py:165

commit v3 on v2

--- a/solution.py
+++ b/solution.py
@@ -38,11 +38,11 @@
 def dense_kernel(meta_ref, tiles_ref, adj_ref, sems):
     slot_count, tile, _ = tiles_ref.shape
     col_tiles = adj_ref.shape[1] // tile
-    live = jnp.minimum(meta_ref[2], slot_count)
+    live = jnp.minimum(meta_ref[0], slot_count)
     adj_ref[...] = jnp.zeros_like(adj_ref)
 
     def copy(k):
-        slot = meta_ref[3 + k]
+        slot = meta_ref[1 + k]
         row = pl.multiple_of((slot // col_tiles) * tile, tile)
         col = pl.multiple_of((slot % col_tiles) * tile, tile)
         place = adj_ref.at[pl.ds(row, tile), pl.ds(col, tile)]
@@ -66,22 +66,22 @@
         out_ref[k] = refs[k][...]
 
 
-def place_cots(meta_ref, near_ref, other_ref, out_ref):
+def place_cots(near_ref, other_ref, out_ref):
     slab = near_ref.shape[1]
     for k in range(near_ref.shape[0]):
-        out_ref[rows_of(meta_ref[1] ^ (2 * k), slab), :] = near_ref[k]
-        out_ref[rows_of(meta_ref[1] ^ (2 * k + 1), slab), :] = other_ref[k]
-
-
-def forward_kernel(meta_ref, adj_ref, near_ref, other_ref, *refs, half):
+        out_ref[rows_of(lax.axis_index("col") ^ (2 * k), slab), :] = near_ref[k]
+        out_ref[rows_of(lax.axis_index("col") ^ (2 * k + 1), slab), :] = other_ref[k]
+
+
+def forward_kernel(adj_ref, near_ref, other_ref, *refs, half):
     pair_refs, (*out_refs, both_ref, column, cots, part, grad) = refs[:half], refs[half:]
     slab = near_ref.shape[1]
     others = len(out_refs) // 2
     piece = both_ref.shape[0] - slab
-    place_cots(meta_ref, near_ref, other_ref, cots)
-    for k, ref in enumerate(pair_refs[::-1]):
-        column[rows_of(meta_ref[0] ^ k, slab), :] = ref[0]
-        column[rows_of(meta_ref[0] ^ k ^ half, slab), :] = ref[1]
+    place_cots(near_ref, other_ref, cots)
+    for k, ref in enumerate(pair_refs):
+        column[rows_of(lax.axis_index("row") ^ k, slab), :] = ref[0]
+        column[rows_of(lax.axis_index("row") ^ k ^ half, slab), :] = ref[1]
     product = jnp.dot(adj_ref[...], column[...], preferred_element_type=F32).astype(BF16)
     part[...] = product
     grad[...] = lax.dot_general(
@@ -89,22 +89,22 @@
     ).astype(BF16)
     for n in range(others):
         k = n + 1 if n else 0
-        out_refs[n][...] = part[rows_of(meta_ref[1] ^ k, slab), :]
-        out_refs[others + n][...] = grad[rows_of(meta_ref[1] ^ k, piece), :]
-    both_ref[:slab, :] = part[rows_of(meta_ref[1] ^ 1, slab), :]
-    both_ref[slab:, :] = grad[rows_of(meta_ref[1] ^ 1, piece), :]
-
-
-def backward_kernel(meta_ref, adj_ref, near_ref, other_ref, *refs):
+        out_refs[n][...] = part[rows_of(lax.axis_index("col") ^ k, slab), :]
+        out_refs[others + n][...] = grad[rows_of(lax.axis_index("col") ^ k, piece), :]
+    both_ref[:slab, :] = part[rows_of(lax.axis_index("col") ^ 1, slab), :]
+    both_ref[slab:, :] = grad[rows_of(lax.axis_index("col") ^ 1, piece), :]
+
+
+def backward_kernel(adj_ref, near_ref, other_ref, *refs):
     *pair_refs, cots, total = refs
     half, slab = len(pair_refs), pair_refs[0].shape[1]
-    place_cots(meta_ref, near_ref, other_ref, cots)
+    place_cots(near_ref, other_ref, cots)
     total[...] = lax.dot_general(
         adj_ref[...], cots[...], (((0,), (0,)), ((), ())), preferred_element_type=F32
     ).astype(BF16)
     for k, ref in enumerate(pair_refs):
-        ref[0] = total[rows_of(meta_ref[0] ^ k, slab), :]
-        ref[1] = total[rows_of(meta_ref[0] ^ k ^ half, slab), :]
+        ref[0] = total[rows_of(lax.axis_index("row") ^ k, slab), :]
+        ref[1] = total[rows_of(lax.axis_index("row") ^ k ^ half, slab), :]
 
 
 def pair_sum_kernel(*refs):
@@ -153,11 +153,11 @@
     out_ref[...] = summed([held_ref.at[slab:, :], got_ref.at[slab:, :]]).astype(BF16)
 
 
-def gather_kernel(meta_ref, *refs):
+def gather_kernel(*refs):
     *piece_refs, out_ref = refs
     piece = piece_refs[0].shape[0]
     for k, ref in enumerate(piece_refs):
-        out_ref[rows_of(meta_ref[1] ^ k, piece), :] = ref[...]
+        out_ref[rows_of(lax.axis_index("col") ^ k, piece), :] = ref[...]
 
 
 def swap(array, axis, distance):
@@ -177,8 +177,7 @@
     slab, width = features.shape[1:]
     rows, cols = col_devices * slab, row_devices * slab
     piece = width // col_devices
-    place = jnp.stack([lax.axis_index("row"), lax.axis_index("col")]).astype(jnp.int32)
-    me = jnp.concatenate([place, tile_counts[0], tile_slots[0, 0]])
+    live = jnp.concatenate([tile_counts[0], tile_slots[0, 0]])
 
     def call(kernel, name, out_shape, in_specs, args, scratch=(), micros=None):
         many = isinstance(out_shape, list)
@@ -198,7 +197,7 @@
     own = features[0]
     far = swap(own, "row", half)
     adj = call(
-        dense_kernel, "dense", shape(rows, cols), [SMEM, ANY], (me, tile_values[0, 0]),
+        dense_kernel, "dense", shape(rows, cols), [SMEM, ANY], (live, tile_values[0, 0]),
         scratch=[pltpu.SemaphoreType.DMA((slots,))],
     )
 
@@ -214,7 +213,7 @@
             [VMEM] * len(arrays) + [ANY] * len(after), (*arrays, *after), micros=3,
         )
 
-    kept = hold([own, cotangent[0]], me, "own")
+    kept = hold([own, cotangent[0]], live, "own")
     pair = stack([kept[0], far], "pair")
     features_got = exchange([pair] * half, "row")
     cot_near = stack(
@@ -227,7 +226,7 @@
         [shape(slab, width)] * (col_devices - 1)
         + [shape(piece, width)] * (col_devices - 1)
         + [shape(slab + piece, width)],
-        [SMEM] + [VMEM] * (3 + half), (me, adj, cot_near, cot_other, *features_got[::-1]),
+        [VMEM] * (3 + half), (adj, cot_near, cot_other, *features_got),
         scratch=[
             pltpu.VMEM((cols, width), BF16),
             pltpu.VMEM((rows, width), BF16),
@@ -237,7 +236,7 @@
     )
     column_pairs = call(
         backward_kernel, "backward", [shape(2, slab, width)] * half,
-        [SMEM] + [VMEM] * 3, (me, adj, cot_near, cot_other),
+        [VMEM] * 3, (adj, cot_near, cot_other),
         scratch=[pltpu.VMEM((rows, width), BF16), pltpu.VMEM((cols, width), BF16)],
     )
     chunks, pieces = outs[: col_devices - 1], outs[col_devices - 1 : -1]
@@ -269,8 +268,8 @@
         (weight, column_keep, both_far, first, *row_got),
     )
     gathered = call(
-        gather_kernel, "weight_grad", shape(width, width), [SMEM] + [VMEM] * col_devices,
-        (me, *exchange([grad_row] * col_devices, "col")),
+        gather_kernel, "weight_grad", shape(width, width), [VMEM] * col_devices,
+        exchange([grad_row] * col_devices, "col"),
     )
     weight_grad = gathered.astype(F32) * (1.0 / math.sqrt(row_devices * col_devices * slab))
     return (layer_out[None], feature_grad[None], weight_grad)

time: 45.3 us -> 43.2 us (0.954); the launches traced: 45.6 us -> 43 us
  waiting for transfers between devices: 13.7 us -> 11.3 us
  Pallas kernels: 5.29 us -> 3.37 us
  starting transfers between devices: 22 us -> 23.8 us
    ppermute x21, waiting for transfers between devices: 13.7 us -> 11.3 us  [swap(): return lax.ppermute(array, axis, pairs)]
    pallas_call x13, Pallas kernels: 5.29 us -> 3.37 us  [call(): pl.pallas_call(kernel, out_shape=out_shape, in_specs=in_specs, out_specs=...]
    ppermute x21, starting transfers between devices: 22 us -> 23.8 us  [swap(): return lax.ppermute(array, axis, pairs)]
  transfers between devices with their start and end apart: 21 -> 21, of which waited for: 10 -> 11; matrix products, arithmetic and copies ran while one was open for 0% -> 0% of each run, Pallas kernels for 10% -> 8%
where the time goes in v3:
time: 43.2 us; the launch traced here: 43 us
  starting transfers between devices  23.8 us (55%)
  waiting for transfers between devices  11.3 us (26%)
  Pallas kernels  3.37 us (8%)
  local copies, waits for them, and re-layouts  2.34 us (5%)
  between operations  1.44 us (3%)
  other arithmetic  0.8 us (2%)
    ppermute x21, starting transfers between devices, swap(): return lax.ppermute(array, axis, pairs)  23.8 us
    ppermute x21, waiting for transfers between devices, swap(): return lax.ppermute(array, axis, pairs)  11.3 us
    pallas_call x13, Pallas kernels, call(): pl.pallas_call(kernel, out_shape=out_shape, in_specs=in_specs, out_specs=...  3.37 us
    unnamed x10, local copies, waits for them, and re-layouts  2.34 us
  transfers between devices with their start and end apart: 21, of which 11 were waited for; matrix products, arithmetic and copies ran while one was open for 0% of the time, Pallas kernels for 8%

profile of v3, /device:TPU:0, one launch (start us, length us, event | category | flops | bytes accessed | tf_op | source)
XLA Modules:
  0.0 43.0 jit_solution(14551391872721660239)
XLA Ops:
  0.6 4.1 %collective-permute-start.5 = (bf16[128,256]{1,0:T(8,128)(2,1)}, bf16[128,256]{1,0:T(8,128)(2,1)S(1)}, u32[]{:S(2)}, u32[]{:S(2)}) collective-permute-start(bf16[128,256]{1,0:T(8,128)(2,1)} %bitcast.11), channel_id=1, source_target_pairs={{0,16},{4,20},{8,24},{12,28},{16,0},{20,4},{24,8},{28,12},{1,17},{... | collective-permute-start | bytes 196616 | tf_op jit(solution)/shard_map/ppermute | solution.py:165
  4.7 1.5 %collective-permute-start = (bf16[128,256]{1,0:T(8,128)(2,1)}, bf16[128,256]{1,0:T(8,128)(2,1)S(1)}, u32[]{:S(2)}, u32[]{:S(2)}) collective-permute-start(bf16[128,256]{1,0:T(8,128)(2,1)} %bitcast.9), channel_id=1, source_target_pairs={{0,2},{1,3},{2,0},{3,1},{4,6},{5,7},{6,4},{7,5},{8,10},{9,11},{10,... | collective-permute-start | bytes 196616 | tf_op jit(solution)/shard_map/ppermute | solution.py:165
  6.9 0.6 %copy-done.4 = s32[1,1,32]{2,1,0:T(1,128)S(1)} copy-done((s32[1,1,32]{2,1,0:T(1,128)S(1)}, s32[1,1,32]{2,1,0:T(1,128)}, u32[]{:S(2)}) %copy-start.4) | copy-done | bytes 152
  7.6 0.1 pad_add_fusion.meta_ref.refs_2_
  7.6 0.8 %copy-done.2 = bf16[1,128,256]{2,1,0:T(8,128)(2,1)S(1)} copy-done((bf16[1,128,256]{2,1,0:T(8,128)(2,1)S(1)}, bf16[1,128,256]{2,1,0:T(8,128)(2,1)}, u32[]{:S(2)}) %copy-start.2) | copy-done | bytes 65560
  8.5 0.8 %copy-done.3 = bf16[1,128,256]{2,1,0:T(8,128)(2,1)S(1)} copy-done((bf16[1,128,256]{2,1,0:T(8,128)(2,1)S(1)}, bf16[1,128,256]{2,1,0:T(8,128)(2,1)}, u32[]{:S(2)}) %copy-start.3) | copy-done | bytes 65560
  9.3 0.0 collective-permute-done.refs_1_
  9.4 0.1 collective-permute-start.1
  9.4 0.0 collective-permute-done.5.refs_1_
  9.4 0.0 copy-start
  9.5 2.6 %collective-permute-start.8 = (bf16[2,128,256]{2,1,0:T(8,128)(2,1)S(1)}, bf16[2,128,256]{2,1,0:T(8,128)(2,1)S(1)}, u32[]{:S(2)}, u32[]{:S(2)}) collective-permute-start(bf16[2,128,256]{2,1,0:T(8,128)(2,1)S(1)} %pair.1.refs_3_), channel_id=1, source_target_pairs={{0,12},{4,8},{8,4},{12,0},{16,28},{20,24},{24,20},{28,16},{1,13},{... | collective-permute-start | bytes 393224 | tf_op jit(solution)/shard_map/ppermute | solution.py:165
  12.0 0.4 %collective-permute-start.7 = (bf16[2,128,256]{2,1,0:T(8,128)(2,1)S(1)}, bf16[2,128,256]{2,1,0:T(8,128)(2,1)S(1)}, u32[]{:S(2)}, u32[]{:S(2)}) collective-permute-start(bf16[2,128,256]{2,1,0:T(8,128)(2,1)S(1)} %pair.1.refs_3_), channel_id=1, source_target_pairs={{0,8},{4,12},{8,0},{12,4},{16,24},{20,28},{24,16},{28,20},{1,9},{5... | collective-permute-start | bytes 393224 | tf_op jit(solution)/shard_map/ppermute | solution.py:165
  12.5 0.5 %collective-permute-start.6 = (bf16[2,128,256]{2,1,0:T(8,128)(2,1)S(1)}, bf16[2,128,256]{2,1,0:T(8,128)(2,1)S(1)}, u32[]{:S(2)}, u32[]{:S(2)}) collective-permute-start(bf16[2,128,256]{2,1,0:T(8,128)(2,1)S(1)} %pair.1.refs_3_), channel_id=1, source_target_pairs={{0,4},{4,0},{8,12},{12,8},{16,20},{20,16},{24,28},{28,24},{1,5},{5... | collective-permute-start | bytes 393224 | tf_op jit(solution)/shard_map/ppermute | solution.py:165
  13.0 1.0 %dense.1.adj_ref.refs_0_ = bf16[512,1024]{1,0:T(8,128)(2,1)S(1)} custom-call(s32[33]{0:T(128)S(1)} %pad_add_fusion.meta_ref.refs_2_, bf16[32,128,128]{2,1,0:T(8,128)(2,1)S(1)} %bitcast.8), custom_call_target="tpu_custom_call" | custom-call | tf_op jit(solution)/shard_map/dense/pallas_call | solution.py:184
  14.1 0.6 %backward.1 = (bf16[2,128,256]{2,1,0:T(8,128)(2,1)S(1)}, bf16[2,128,256]{2,1,0:T(8,128)(2,1)S(1)}, bf16[2,128,256]{2,1,0:T(8,128)(2,1)S(1)}, bf16[2,128,256]{2,1,0:T(8,128)(2,1)S(1)}) custom-call(bf16[512,1024]{1,0:T(8,128)(2,1)S(1)} %dense.1.adj_ref.refs_0_, bf16[2,128,256]{2,1,0:T(8,128)(2,1)S(1)} %cot_near.1.near_ref.refs_1_, ...), custom_call_target="tpu_custom_call" | custom-call | tf_op jit(solution)/shard_map/backward/pallas_call | solution.py:184
  14.6 3.3 %collective-permute-start.2 = (bf16[2,128,256]{2,1,0:T(8,128)(2,1)S(1)}, bf16[2,128,256]{2,1,0:T(8,128)(2,1)S(1)}, u32[]{:S(2)}, u32[]{:S(2)}) collective-permute-start(bf16[2,128,256]{2,1,0:T(8,128)(2,1)S(1)} %get-tuple-element.23), channel_id=1, source_target_pairs={{0,12},{4,8},{8,4},{12,0},{16,28},{20,24},{24,20},{28,16},{1,13},{... | collective-permute-start | bytes 393224 | tf_op jit(solution)/shard_map/ppermute | solution.py:165
  18.0 0.6 %collective-permute-start.4 = (bf16[2,128,256]{2,1,0:T(8,128)(2,1)S(1)}, bf16[2,128,256]{2,1,0:T(8,128)(2,1)S(1)}, u32[]{:S(2)}, u32[]{:S(2)}) collective-permute-start(bf16[2,128,256]{2,1,0:T(8,128)(2,1)S(1)} %get-tuple-element.25), channel_id=1, source_target_pairs={{0,4},{4,0},{8,12},{12,8},{16,20},{20,16},{24,28},{28,24},{1,5},{5... | collective-permute-start | bytes 393224 | tf_op jit(solution)/shard_map/ppermute | solution.py:165
  18.6 1.0 %collective-permute-done.7.refs_5_ = bf16[2,128,256]{2,1,0:T(8,128)(2,1)S(1)} collective-permute-done((bf16[2,128,256]{2,1,0:T(8,128)(2,1)S(1)}, bf16[2,128,256]{2,1,0:T(8,128)(2,1)S(1)}, u32[]{:S(2)}, u32[]{:S(2)}) %collective-permute-start.7) | collective-permute-done | bytes 131104 | tf_op jit(solution)/shard_map/ppermute | solution.py:165
  19.6 0.0 collective-permute-done.6.refs_4_
  19.6 0.8 %forward.1 = (bf16[128,256]{1,0:T(8,128)(2,1)S(1)}, bf16[128,256]{1,0:T(8,128)(2,1)S(1)}, bf16[128,256]{1,0:T(8,128)(2,1)S(1)}, bf16[64,256]{1,0:T(8,128)(2,1)S(...) custom-call(bf16[512,1024]{1,0:T(8,128)(2,1)S(1)} %dense.1.adj_ref.refs_0_, ...), custom_call_target="tpu_custom_call" | custom-call | tf_op jit(solution)/shard_map/forward/pallas_call | solution.py:184
  20.4 1.4 %collective-permute-start.10 = (bf16[64,256]{1,0:T(8,128)(2,1)S(1)}, bf16[64,256]{1,0:T(8,128)(2,1)S(1)}, u32[]{:S(2)}, u32[]{:S(2)}) collective-permute-start(bf16[64,256]{1,0:T(8,128)(2,1)S(1)} %get-tuple-element.32), channel_id=1, source_target_pairs={{0,2},{1,3},{2,0},{3,1},{4,6},{5,7},{6,4},{7,5},{8,10},{9,11},{10,... | collective-permute-start | bytes 98312 | tf_op jit(solution)/shard_map/ppermute | solution.py:165
  21.9 0.5 %collective-permute-done.2.refs_0_ = bf16[2,128,256]{2,1,0:T(8,128)(2,1)S(1)} collective-permute-done((bf16[2,128,256]{2,1,0:T(8,128)(2,1)S(1)}, bf16[2,128,256]{2,1,0:T(8,128)(2,1)S(1)}, u32[]{:S(2)}, u32[]{:S(2)}) %collective-permute-start.2) | collective-permute-done | bytes 131104 | tf_op jit(solution)/shard_map/ppermute | solution.py:165
  22.4 0.3 collective-permute-start.9
  22.6 2.2 %collective-permute-done.3.refs_1_ = bf16[2,128,256]{2,1,0:T(8,128)(2,1)S(1)} collective-permute-done((bf16[2,128,256]{2,1,0:T(8,128)(2,1)S(1)}, bf16[2,128,256]{2,1,0:T(8,128)(2,1)S(1)}, u32[]{:S(2)}, u32[]{:S(2)}) %collective-permute-start.3) | collective-permute-done | bytes 131104 | tf_op jit(solution)/shard_map/ppermute | solution.py:165
  24.9 0.1 pair_sum.1
  24.9 0.0 collective-permute-done.10.refs_2_
  24.9 0.4 collective-permute-done.11.refs_3_
  25.3 0.0 collective-permute-done.9.refs_0_.first_ref
  25.3 2.5 %collective-permute-start.14 = (bf16[64,256]{1,0:T(8,128)(2,1)S(1)}, bf16[64,256]{1,0:T(8,128)(2,1)S(1)}, u32[]{:S(2)}, u32[]{:S(2)}) collective-permute-start(bf16[64,256]{1,0:T(8,128)(2,1)S(1)} %grad_col.1.refs_1_), channel_id=1, source_target_pairs={{0,12},{4,8},{8,4},{12,0},{16,28},{20,24},{24,20},{28,16},{1,13},{... | collective-permute-start | bytes 98312 | tf_op jit(solution)/shard_map/ppermute | solution.py:165
  27.9 0.4 %collective-permute-start.13 = (bf16[64,256]{1,0:T(8,128)(2,1)S(1)}, bf16[64,256]{1,0:T(8,128)(2,1)S(1)}, u32[]{:S(2)}, u32[]{:S(2)}) collective-permute-start(bf16[64,256]{1,0:T(8,128)(2,1)S(1)} %grad_col.1.refs_1_), channel_id=1, source_target_pairs={{0,8},{4,12},{8,0},{12,4},{16,24},{20,28},{24,16},{28,20},{1,9},{5... | collective-permute-start | bytes 98312 | tf_op jit(solution)/shard_map/ppermute | solution.py:165
  28.3 0.6 %collective-permute-start.12 = (bf16[64,256]{1,0:T(8,128)(2,1)S(1)}, bf16[64,256]{1,0:T(8,128)(2,1)S(1)}, u32[]{:S(2)}, u32[]{:S(2)}) collective-permute-start(bf16[64,256]{1,0:T(8,128)(2,1)S(1)} %grad_col.1.refs_1_), channel_id=1, source_target_pairs={{0,4},{4,0},{8,12},{12,8},{16,20},{20,16},{24,28},{28,24},{1,5},{5... | collective-permute-start | bytes 98312 | tf_op jit(solution)/shard_map/ppermute | solution.py:165
  28.9 1.5 %collective-permute-done.14.refs_4_.refs_2_ = bf16[64,256]{1,0:T(8,128)(2,1)S(1)} collective-permute-done((bf16[64,256]{1,0:T(8,128)(2,1)S(1)}, bf16[64,256]{1,0:T(8,128)(2,1)S(1)}, u32[]{:S(2)}, u32[]{:S(2)}) %collective-permute-start.14) | collective-permute-done | bytes 32800 | tf_op jit(solution)/shard_map/ppermute | solution.py:165
  30.4 1.4 %collective-permute-done.13.refs_3_ = bf16[64,256]{1,0:T(8,128)(2,1)S(1)} collective-permute-done((bf16[64,256]{1,0:T(8,128)(2,1)S(1)}, bf16[64,256]{1,0:T(8,128)(2,1)S(1)}, u32[]{:S(2)}, u32[]{:S(2)}) %collective-permute-start.13) | collective-permute-done | bytes 32800 | tf_op jit(solution)/shard_map/ppermute | solution.py:165
  31.8 0.4 %collective-permute-done.12.refs_2_ = bf16[64,256]{1,0:T(8,128)(2,1)S(1)} collective-permute-done((bf16[64,256]{1,0:T(8,128)(2,1)S(1)}, bf16[64,256]{1,0:T(8,128)(2,1)S(1)}, u32[]{:S(2)}, u32[]{:S(2)}) %collective-permute-start.12) | collective-permute-done | bytes 32800 | tf_op jit(solution)/shard_map/ppermute | solution.py:165
  32.3 2.7 %collective-permute-start.15 = (bf16[192,256]{1,0:T(8,128)(2,1)S(1)}, bf16[192,256]{1,0:T(8,128)(2,1)S(1)}, u32[]{:S(2)}, u32[]{:S(2)}) collective-permute-start(bf16[192,256]{1,0:T(8,128)(2,1)S(1)} %grad_near.1.held_ref), channel_id=1, source_target_pairs={{0,16},{4,20},{8,24},{12,28},{16,0},{20,4},{24,8},{28,12},{1,17},{... | collective-permute-start | bytes 294920 | tf_op jit(solution)/shard_map/ppermute | solution.py:165
  35.0 0.0 copy-start.1
  35.0 0.6 %collective-permute-start.16 = (bf16[128,256]{1,0:T(8,128)(2,1)S(1)}, bf16[128,256]{1,0:T(8,128)(2,1)S(1)}, u32[]{:S(2)}, u32[]{:S(2)}) collective-permute-start(bf16[128,256]{1,0:T(8,128)(2,1)S(1)} %get-tuple-element.37), channel_id=1, source_target_pairs={{0,2},{1,3},{2,0},{3,1},{4,6},{5,7},{6,4},{7,5},{8,10},{9,11},{10,... | collective-permute-start | bytes 196616 | tf_op jit(solution)/shard_map/ppermute | solution.py:165
  35.6 0.0 collective-permute-start.17
  35.6 2.2 %collective-permute-done.15.far_ref.got_ref = bf16[192,256]{1,0:T(8,128)(2,1)S(1)} collective-permute-done((bf16[192,256]{1,0:T(8,128)(2,1)S(1)}, bf16[192,256]{1,0:T(8,128)(2,1)S(1)}, u32[]{:S(2)}, u32[]{:S(2)}) %collective-permute-start.15) | collective-permute-done | bytes 98336 | tf_op jit(solution)/shard_map/ppermute | solution.py:165
  37.9 0.1 collective-permute-start.20
  37.9 1.0 %collective-permute-start.19 = (bf16[64,256]{1,0:T(8,128)(2,1)S(1)}, bf16[64,256]{1,0:T(8,128)(2,1)S(1)}, u32[]{:S(2)}, u32[]{:S(2)}) collective-permute-start(bf16[64,256]{1,0:T(8,128)(2,1)S(1)} %grad_row.1.refs_0_), channel_id=1, source_target_pairs={{0,2},{1,3},{2,0},{3,1},{4,6},{5,7},{6,4},{7,5},{8,10},{9,11},{10,... | collective-permute-start | bytes 98312 | tf_op jit(solution)/shard_map/ppermute | solution.py:165
  39.0 0.8 %collective-permute-start.18 = (bf16[64,256]{1,0:T(8,128)(2,1)S(1)}, bf16[64,256]{1,0:T(8,128)(2,1)S(1)}, u32[]{:S(2)}, u32[]{:S(2)}) collective-permute-start(bf16[64,256]{1,0:T(8,128)(2,1)S(1)} %grad_row.1.refs_0_), channel_id=1, source_target_pairs={{0,1},{1,0},{2,3},{3,2},{4,5},{5,4},{6,7},{7,6},{8,9},{9,8},{10,11... | collective-permute-start | bytes 98312 | tf_op jit(solution)/shard_map/ppermute | solution.py:165
  39.8 0.2 collective-permute-done.16.refs_1_
  40.0 0.0 collective-permute-done.17.refs_2_
  40.0 0.8 %outputs.1 = (bf16[128,256]{1,0:T(8,128)(2,1)}, bf16[128,256]{1,0:T(8,128)(2,1)}) custom-call(bf16[256,256]{1,0:T(8,128)(2,1)S(1)} %copy-done.1, f32[128,256]{1,0:T(8,128)S(1)} %get-tuple-element.27.keep_ref, bf16[192,256]{1,0:T(8,128)(2,1)S(1)} %collective-permute-done.15.far_ref.got_ref, bf16[192,256]{1,0:T(8,128)(2,1)S(1)} %collective-permute-done.9.refs_0_.first_ref, ...), custom_call_target="tpu_custom_call" | custom-call | tf_op jit(solution)/shard_map/outputs/pallas_call | solution.py:184
  40.9 0.6 %collective-permute-done.20.refs_3_ = bf16[64,256]{1,0:T(8,128)(2,1)S(1)} collective-permute-done((bf16[64,256]{1,0:T(8,128)(2,1)S(1)}, bf16[64,256]{1,0:T(8,128)(2,1)S(1)}, u32[]{:S(2)}, u32[]{:S(2)}) %collective-permute-start.20) | collective-permute-done | bytes 32800 | tf_op jit(solution)/shard_map/ppermute | solution.py:165
  41.4 0.8 %collective-permute-done.19.refs_2_ = bf16[64,256]{1,0:T(8,128)(2,1)S(1)} collective-permute-done((bf16[64,256]{1,0:T(8,128)(2,1)S(1)}, bf16[64,256]{1,0:T(8,128)(2,1)S(1)}, u32[]{:S(2)}, u32[]{:S(2)}) %collective-permute-start.19) | collective-permute-done | bytes 32800 | tf_op jit(solution)/shard_map/ppermute | solution.py:165
  42.2 0.7 %convert_multiply_fusion = f32[256,256]{1,0:T(8,128)} fusion(bf16[256,256]{1,0:T(8,128)(2,1)S(1)} %weight_grad.1), kind=kLoop, calls=%fused_computation | loop fusion | flops 131072 | bytes 393216 | tf_op jit(solution)/shard_map/mul | solution.py:274
  (19 shorter events, 0.1 us)
Async XLA Ops:
  0.6 8.8 %collective-permute-start.5 = (bf16[128,256]{1,0:T(8,128)(2,1)}, bf16[128,256]{1,0:T(8,128)(2,1)S(1)}, u32[]{:S(2)}, u32[]{:S(2)}) collective-permute-start(bf16[128,256]{1,0:T(8,128)(2,1)} %bitcast.11), channel_id=1, source_target_pairs={{0,16},{4,20},{8,24},{12,28},{16,0},{20,4},{24,8},{28,12},{1,17},{... | collective-permute-start | bytes 196616 | tf_op jit(solution)/shard_map/ppermute | solution.py:165
  4.7 4.6 %collective-permute-start = (bf16[128,256]{1,0:T(8,128)(2,1)}, bf16[128,256]{1,0:T(8,128)(2,1)S(1)}, u32[]{:S(2)}, u32[]{:S(2)}) collective-permute-start(bf16[128,256]{1,0:T(8,128)(2,1)} %bitcast.9), channel_id=1, source_target_pairs={{0,2},{1,3},{2,0},{3,1},{4,6},{5,7},{6,4},{7,5},{8,10},{9,11},{10,... | collective-permute-start | bytes 196616 | tf_op jit(solution)/shard_map/ppermute | solution.py:165
  6.9 0.7 %copy-start.4 = (s32[1,1,32]{2,1,0:T(1,128)S(1)}, s32[1,1,32]{2,1,0:T(1,128)}, u32[]{:S(2)}) copy-start(s32[1,1,32]{2,1,0:T(1,128)} %param.9) | copy-start | bytes 388
  7.6 0.8 %copy-start.2 = (bf16[1,128,256]{2,1,0:T(8,128)(2,1)S(1)}, bf16[1,128,256]{2,1,0:T(8,128)(2,1)}, u32[]{:S(2)}) copy-start(bf16[1,128,256]{2,1,0:T(8,128)(2,1)} %param.11) | copy-start | bytes 196612
  8.5 0.8 %copy-start.3 = (bf16[1,128,256]{2,1,0:T(8,128)(2,1)S(1)}, bf16[1,128,256]{2,1,0:T(8,128)(2,1)}, u32[]{:S(2)}) copy-start(bf16[1,128,256]{2,1,0:T(8,128)(2,1)} %param.6) | copy-start | bytes 196612
  9.4 4.7 %collective-permute-start.1 = (bf16[2,128,256]{2,1,0:T(8,128)(2,1)S(1)}, bf16[2,128,256]{2,1,0:T(8,128)(2,1)S(1)}, u32[]{:S(2)}, u32[]{:S(2)}) collective-permute-start(bf16[2,128,256]{2,1,0:T(8,128)(2,1)S(1)} %cot_near.1.near_ref.refs_1_), channel_id=1, source_target_pairs={{0,1},{1,0},{2,3},{3,2},{4,5},{5,4},{6,7},{7,6},{8,9},{9,8},{10,11... | collective-permute-start | bytes 393224 | tf_op jit(solution)/shard_map/ppermute | solution.py:165
  9.4 3.6 %copy-start = (bf16[1,1,32,128,128]{4,3,2,1,0:T(8,128)(2,1)S(1)}, bf16[1,1,32,128,128]{4,3,2,1,0:T(8,128)(2,1)}, u32[]{:S(2)}) copy-start(bf16[1,1,32,128,128]{4,3,2,1,0:T(8,128)(2,1)} %param.8) | copy-start | bytes 3145732
  9.5 8.5 %collective-permute-start.8 = (bf16[2,128,256]{2,1,0:T(8,128)(2,1)S(1)}, bf16[2,128,256]{2,1,0:T(8,128)(2,1)S(1)}, u32[]{:S(2)}, u32[]{:S(2)}) collective-permute-start(bf16[2,128,256]{2,1,0:T(8,128)(2,1)S(1)} %pair.1.refs_3_), channel_id=1, source_target_pairs={{0,12},{4,8},{8,4},{12,0},{16,28},{20,24},{24,20},{28,16},{1,13},{... | collective-permute-start | bytes 393224 | tf_op jit(solution)/shard_map/ppermute | solution.py:165
  12.0 7.6 %collective-permute-start.7 = (bf16[2,128,256]{2,1,0:T(8,128)(2,1)S(1)}, bf16[2,128,256]{2,1,0:T(8,128)(2,1)S(1)}, u32[]{:S(2)}, u32[]{:S(2)}) collective-permute-start(bf16[2,128,256]{2,1,0:T(8,128)(2,1)S(1)} %pair.1.refs_3_), channel_id=1, source_target_pairs={{0,8},{4,12},{8,0},{12,4},{16,24},{20,28},{24,16},{28,20},{1,9},{5... | collective-permute-start | bytes 393224 | tf_op jit(solution)/shard_map/ppermute | solution.py:165
  12.5 7.1 %collective-permute-start.6 = (bf16[2,128,256]{2,1,0:T(8,128)(2,1)S(1)}, bf16[2,128,256]{2,1,0:T(8,128)(2,1)S(1)}, u32[]{:S(2)}, u32[]{:S(2)}) collective-permute-start(bf16[2,128,256]{2,1,0:T(8,128)(2,1)S(1)} %pair.1.refs_3_), channel_id=1, source_target_pairs={{0,4},{4,0},{8,12},{12,8},{16,20},{20,16},{24,28},{28,24},{1,5},{5... | collective-permute-start | bytes 393224 | tf_op jit(solution)/shard_map/ppermute | solution.py:165
  14.6 7.7 %collective-permute-start.2 = (bf16[2,128,256]{2,1,0:T(8,128)(2,1)S(1)}, bf16[2,128,256]{2,1,0:T(8,128)(2,1)S(1)}, u32[]{:S(2)}, u32[]{:S(2)}) collective-permute-start(bf16[2,128,256]{2,1,0:T(8,128)(2,1)S(1)} %get-tuple-element.23), channel_id=1, source_target_pairs={{0,12},{4,8},{8,4},{12,0},{16,28},{20,24},{24,20},{28,16},{1,13},{... | collective-permute-start | bytes 393224 | tf_op jit(solution)/shard_map/ppermute | solution.py:165
  18.0 6.9 %collective-permute-start.3 = (bf16[2,128,256]{2,1,0:T(8,128)(2,1)S(1)}, bf16[2,128,256]{2,1,0:T(8,128)(2,1)S(1)}, u32[]{:S(2)}, u32[]{:S(2)}) collective-permute-start(bf16[2,128,256]{2,1,0:T(8,128)(2,1)S(1)} %get-tuple-element.24), channel_id=1, source_target_pairs={{0,8},{4,12},{8,0},{12,4},{16,24},{20,28},{24,16},{28,20},{1,9},{5... | collective-permute-start | bytes 393224 | tf_op jit(solution)/shard_map/ppermute | solution.py:165
  18.0 6.9 %collective-permute-start.4 = (bf16[2,128,256]{2,1,0:T(8,128)(2,1)S(1)}, bf16[2,128,256]{2,1,0:T(8,128)(2,1)S(1)}, u32[]{:S(2)}, u32[]{:S(2)}) collective-permute-start(bf16[2,128,256]{2,1,0:T(8,128)(2,1)S(1)} %get-tuple-element.25), channel_id=1, source_target_pairs={{0,4},{4,0},{8,12},{12,8},{16,20},{20,16},{24,28},{28,24},{1,5},{5... | collective-permute-start | bytes 393224 | tf_op jit(solution)/shard_map/ppermute | solution.py:165
  20.4 4.5 %collective-permute-start.10 = (bf16[64,256]{1,0:T(8,128)(2,1)S(1)}, bf16[64,256]{1,0:T(8,128)(2,1)S(1)}, u32[]{:S(2)}, u32[]{:S(2)}) collective-permute-start(bf16[64,256]{1,0:T(8,128)(2,1)S(1)} %get-tuple-element.32), channel_id=1, source_target_pairs={{0,2},{1,3},{2,0},{3,1},{4,6},{5,7},{6,4},{7,5},{8,10},{9,11},{10,... | collective-permute-start | bytes 98312 | tf_op jit(solution)/shard_map/ppermute | solution.py:165
  21.9 3.4 %collective-permute-start.11 = (bf16[64,256]{1,0:T(8,128)(2,1)S(1)}, bf16[64,256]{1,0:T(8,128)(2,1)S(1)}, u32[]{:S(2)}, u32[]{:S(2)}) collective-permute-start(bf16[64,256]{1,0:T(8,128)(2,1)S(1)} %get-tuple-element.33), channel_id=1, source_target_pairs={{0,3},{1,2},{2,1},{3,0},{4,7},{5,6},{6,5},{7,4},{8,11},{9,10},{10,... | collective-permute-start | bytes 98312 | tf_op jit(solution)/shard_map/ppermute | solution.py:165
  22.4 2.9 %collective-permute-start.9 = (bf16[192,256]{1,0:T(8,128)(2,1)S(1)}, bf16[192,256]{1,0:T(8,128)(2,1)S(1)}, u32[]{:S(2)}, u32[]{:S(2)}) collective-permute-start(bf16[192,256]{1,0:T(8,128)(2,1)S(1)} %get-tuple-element.30), channel_id=1, source_target_pairs={{0,1},{1,0},{2,3},{3,2},{4,5},{5,4},{6,7},{7,6},{8,9},{9,8},{10,11... | collective-permute-start | bytes 294920 | tf_op jit(solution)/shard_map/ppermute | solution.py:165
  25.3 5.1 %collective-permute-start.14 = (bf16[64,256]{1,0:T(8,128)(2,1)S(1)}, bf16[64,256]{1,0:T(8,128)(2,1)S(1)}, u32[]{:S(2)}, u32[]{:S(2)}) collective-permute-start(bf16[64,256]{1,0:T(8,128)(2,1)S(1)} %grad_col.1.refs_1_), channel_id=1, source_target_pairs={{0,12},{4,8},{8,4},{12,0},{16,28},{20,24},{24,20},{28,16},{1,13},{... | collective-permute-start | bytes 98312 | tf_op jit(solution)/shard_map/ppermute | solution.py:165
  27.9 3.9 %collective-permute-start.13 = (bf16[64,256]{1,0:T(8,128)(2,1)S(1)}, bf16[64,256]{1,0:T(8,128)(2,1)S(1)}, u32[]{:S(2)}, u32[]{:S(2)}) collective-permute-start(bf16[64,256]{1,0:T(8,128)(2,1)S(1)} %grad_col.1.refs_1_), channel_id=1, source_target_pairs={{0,8},{4,12},{8,0},{12,4},{16,24},{20,28},{24,16},{28,20},{1,9},{5... | collective-permute-start | bytes 98312 | tf_op jit(solution)/shard_map/ppermute | solution.py:165
  28.3 3.9 %collective-permute-start.12 = (bf16[64,256]{1,0:T(8,128)(2,1)S(1)}, bf16[64,256]{1,0:T(8,128)(2,1)S(1)}, u32[]{:S(2)}, u32[]{:S(2)}) collective-permute-start(bf16[64,256]{1,0:T(8,128)(2,1)S(1)} %grad_col.1.refs_1_), channel_id=1, source_target_pairs={{0,4},{4,0},{8,12},{12,8},{16,20},{20,16},{24,28},{28,24},{1,5},{5... | collective-permute-start | bytes 98312 | tf_op jit(solution)/shard_map/ppermute | solution.py:165
  32.3 5.6 %collective-permute-start.15 = (bf16[192,256]{1,0:T(8,128)(2,1)S(1)}, bf16[192,256]{1,0:T(8,128)(2,1)S(1)}, u32[]{:S(2)}, u32[]{:S(2)}) collective-permute-start(bf16[192,256]{1,0:T(8,128)(2,1)S(1)} %grad_near.1.held_ref), channel_id=1, source_target_pairs={{0,16},{4,20},{8,24},{12,28},{16,0},{20,4},{24,8},{28,12},{1,17},{... | collective-permute-start | bytes 294920 | tf_op jit(solution)/shard_map/ppermute | solution.py:165
  35.0 5.0 %copy-start.1 = (bf16[256,256]{1,0:T(8,128)(2,1)S(1)}, bf16[256,256]{1,0:T(8,128)(2,1)}, u32[]{:S(2)}) copy-start(bf16[256,256]{1,0:T(8,128)(2,1)} %weight_ref.1) | copy-start | bytes 393220
  35.0 5.0 %collective-permute-start.16 = (bf16[128,256]{1,0:T(8,128)(2,1)S(1)}, bf16[128,256]{1,0:T(8,128)(2,1)S(1)}, u32[]{:S(2)}, u32[]{:S(2)}) collective-permute-start(bf16[128,256]{1,0:T(8,128)(2,1)S(1)} %get-tuple-element.37), channel_id=1, source_target_pairs={{0,2},{1,3},{2,0},{3,1},{4,6},{5,7},{6,4},{7,5},{8,10},{9,11},{10,... | collective-permute-start | bytes 196616 | tf_op jit(solution)/shard_map/ppermute | solution.py:165
  35.6 4.4 %collective-permute-start.17 = (bf16[128,256]{1,0:T(8,128)(2,1)S(1)}, bf16[128,256]{1,0:T(8,128)(2,1)S(1)}, u32[]{:S(2)}, u32[]{:S(2)}) collective-permute-start(bf16[128,256]{1,0:T(8,128)(2,1)S(1)} %get-tuple-element.38), channel_id=1, source_target_pairs={{0,3},{1,2},{2,1},{3,0},{4,7},{5,6},{6,5},{7,4},{8,11},{9,10},{10,... | collective-permute-start | bytes 196616 | tf_op jit(solution)/shard_map/ppermute | solution.py:165
  37.9 3.6 %collective-permute-start.20 = (bf16[64,256]{1,0:T(8,128)(2,1)S(1)}, bf16[64,256]{1,0:T(8,128)(2,1)S(1)}, u32[]{:S(2)}, u32[]{:S(2)}) collective-permute-start(bf16[64,256]{1,0:T(8,128)(2,1)S(1)} %grad_row.1.refs_0_), channel_id=1, source_target_pairs={{0,3},{1,2},{2,1},{3,0},{4,7},{5,6},{6,5},{7,4},{8,11},{9,10},{10,... | collective-permute-start | bytes 98312 | tf_op jit(solution)/shard_map/ppermute | solution.py:165
  37.9 4.3 %collective-permute-start.19 = (bf16[64,256]{1,0:T(8,128)(2,1)S(1)}, bf16[64,256]{1,0:T(8,128)(2,1)S(1)}, u32[]{:S(2)}, u32[]{:S(2)}) collective-permute-start(bf16[64,256]{1,0:T(8,128)(2,1)S(1)} %grad_row.1.refs_0_), channel_id=1, source_target_pairs={{0,2},{1,3},{2,0},{3,1},{4,6},{5,7},{6,4},{7,5},{8,10},{9,11},{10,... | collective-permute-start | bytes 98312 | tf_op jit(solution)/shard_map/ppermute | solution.py:165
  39.0 3.3 %collective-permute-start.18 = (bf16[64,256]{1,0:T(8,128)(2,1)S(1)}, bf16[64,256]{1,0:T(8,128)(2,1)S(1)}, u32[]{:S(2)}, u32[]{:S(2)}) collective-permute-start(bf16[64,256]{1,0:T(8,128)(2,1)S(1)} %grad_row.1.refs_0_), channel_id=1, source_target_pairs={{0,1},{1,0},{2,3},{3,2},{4,5},{5,4},{6,7},{7,6},{8,9},{9,8},{10,11... | collective-permute-start | bytes 98312 | tf_op jit(solution)/shard_map/ppermute | solution.py:165

commit v4 on v3

--- a/solution.py
+++ b/solution.py
@@ -74,14 +74,14 @@
 
 
 def forward_kernel(adj_ref, near_ref, other_ref, *refs, half):
-    pair_refs, (*out_refs, both_ref, column, cots, part, grad) = refs[:half], refs[half:]
+    shard_refs, refs = refs[: 2 * half], refs[2 * half :]
+    *out_refs, both_ref, column, cots, part, grad = refs
     slab = near_ref.shape[1]
     others = len(out_refs) // 2
     piece = both_ref.shape[0] - slab
     place_cots(near_ref, other_ref, cots)
-    for k, ref in enumerate(pair_refs):
-        column[rows_of(lax.axis_index("row") ^ k, slab), :] = ref[0]
-        column[rows_of(lax.axis_index("row") ^ k ^ half, slab), :] = ref[1]
+    for k, ref in enumerate(shard_refs):
+        column[rows_of(lax.axis_index("row") ^ k, slab), :] = ref[...]
     product = jnp.dot(adj_ref[...], column[...], preferred_element_type=F32).astype(BF16)
     part[...] = product
     grad[...] = lax.dot_general(
@@ -213,11 +213,12 @@
             [VMEM] * len(arrays) + [ANY] * len(after), (*arrays, *after), micros=3,
         )
 
-    kept = hold([own, cotangent[0]], live, "own")
-    pair = stack([kept[0], far], "pair")
-    features_got = exchange([pair] * half, "row")
+    near = exchange([own] * half, "row")
+    ready = stack([far], "ready", near[1:]).reshape(own.shape)
+    shards = near + exchange([ready] * half, "row")
+    (cot_own,) = hold([cotangent[0]], live, "own")
     cot_near = stack(
-        [kept[1]] + exchange([cotangent[0]] * (col_devices // 2), "col", 2)[1:], "cot_near"
+        [cot_own] + exchange([cotangent[0]] * (col_devices // 2), "col", 2)[1:], "cot_near"
     )
     cot_other = swap(cot_near, "col", 1)
 
@@ -226,7 +227,7 @@
         [shape(slab, width)] * (col_devices - 1)
         + [shape(piece, width)] * (col_devices - 1)
         + [shape(slab + piece, width)],
-        [VMEM] * (3 + half), (adj, cot_near, cot_other, *features_got),
+        [VMEM] * (3 + 2 * half), (adj, cot_near, cot_other, *shards),
         scratch=[
             pltpu.VMEM((cols, width), BF16),
             pltpu.VMEM((rows, width), BF16),
@@ -244,7 +245,7 @@
 
     column_keep, column_send = call(
         pair_sum_kernel, "pair_sum", [shape(slab, width, dtype=F32), shape(slab, width)],
-        [VMEM] * half, exchange(column_pairs, "row")[::-1], micros=5,
+        [VMEM] * half, exchange(column_pairs, "row")[::-1], micros=None,
     )
     def fetch(arrays):
         return [arrays[0]] + [swap(arrays[k - 1], "col", k) for k in range(2, col_devices)]

time: 43.2 us -> 47.8 us (1.11)
  starting transfers between devices: 23.8 us -> 26.9 us
  waiting for transfers between devices: 11.3 us -> 13.1 us
  local copies, waits for them, and re-layouts: 2.34 us -> 1.51 us
    ppermute x21 -> x24, starting transfers between devices: 23.8 us -> 26.9 us  [swap(): return lax.ppermute(array, axis, pairs)]
    ppermute x21 -> x24, waiting for transfers between devices: 11.3 us -> 13.1 us  [swap(): return lax.ppermute(array, axis, pairs)]
    unnamed x10, local copies, waits for them, and re-layouts: 2.34 us -> 1.51 us
  transfers between devices with their start and end apart: 21 -> 24, of which waited for: 11 -> 11; matrix products, arithmetic and copies ran while one was open for 0% -> 0% of each run, Pallas kernels for 8% -> 7%
where the time goes in v4:
time: 47.8 us; the launch traced here: 47.4 us
  starting transfers between devices  26.9 us (56%)
  waiting for transfers between devices  13.1 us (27%)
  Pallas kernels  3.59 us (8%)
  local copies, waits for them, and re-layouts  1.51 us (3%)
  between operations  1.46 us (3%)
  other arithmetic  0.8 us (2%)
    ppermute x24, starting transfers between devices, swap(): return lax.ppermute(array, axis, pairs)  26.9 us
    ppermute x24, waiting for transfers between devices, swap(): return lax.ppermute(array, axis, pairs)  13.1 us
    pallas_call x13, Pallas kernels, call(): pl.pallas_call(kernel, out_shape=out_shape, in_specs=in_specs, out_specs=...  3.59 us
    unnamed x10, local copies, waits for them, and re-layouts  1.51 us
  transfers between devices with their start and end apart: 24, of which 11 were waited for; matrix products, arithmetic and copies ran while one was open for 0% of the time, Pallas kernels for 7%

profile of v4, /device:TPU:0, one launch (start us, length us, event | category | flops | bytes accessed | tf_op | source)
XLA Modules:
  0.0 47.4 jit_solution(10075628522310698300)
XLA Ops:
  0.6 4.1 %collective-permute-start.8 = (bf16[128,256]{1,0:T(8,128)(2,1)}, bf16[128,256]{1,0:T(8,128)(2,1)S(1)}, u32[]{:S(2)}, u32[]{:S(2)}) collective-permute-start(bf16[128,256]{1,0:T(8,128)(2,1)} %bitcast.10), channel_id=1, source_target_pairs={{0,16},{4,20},{8,24},{12,28},{16,0},{20,4},{24,8},{28,12},{1,17},{... | collective-permute-start | bytes 196616 | tf_op jit(solution)/shard_map/ppermute | solution.py:165
  4.7 2.5 %collective-permute-start.7 = (bf16[128,256]{1,0:T(8,128)(2,1)}, bf16[128,256]{1,0:T(8,128)(2,1)S(1)}, u32[]{:S(2)}, u32[]{:S(2)}) collective-permute-start(bf16[128,256]{1,0:T(8,128)(2,1)} %bitcast.11), channel_id=1, source_target_pairs={{0,12},{4,8},{8,4},{12,0},{16,28},{20,24},{24,20},{28,16},{1,13},{... | collective-permute-start | bytes 196616 | tf_op jit(solution)/shard_map/ppermute | solution.py:165
  7.2 0.4 collective-permute-start.6
  7.7 0.5 %collective-permute-start.5 = (bf16[128,256]{1,0:T(8,128)(2,1)}, bf16[128,256]{1,0:T(8,128)(2,1)S(1)}, u32[]{:S(2)}, u32[]{:S(2)}) collective-permute-start(bf16[128,256]{1,0:T(8,128)(2,1)} %bitcast.13), channel_id=1, source_target_pairs={{0,4},{4,0},{8,12},{12,8},{16,20},{20,16},{24,28},{28,24},{1,5},{5... | collective-permute-start | bytes 196616 | tf_op jit(solution)/shard_map/ppermute | solution.py:165
  8.2 1.5 %collective-permute-start = (bf16[128,256]{1,0:T(8,128)(2,1)}, bf16[128,256]{1,0:T(8,128)(2,1)S(1)}, u32[]{:S(2)}, u32[]{:S(2)}) collective-permute-start(bf16[128,256]{1,0:T(8,128)(2,1)} %bitcast.19), channel_id=1, source_target_pairs={{0,2},{1,3},{2,0},{3,1},{4,6},{5,7},{6,4},{7,5},{8,10},{9,11},{10,... | collective-permute-start | bytes 196616 | tf_op jit(solution)/shard_map/ppermute | solution.py:165
  10.4 0.6 %copy-done.4 = s32[1,1,32]{2,1,0:T(1,128)S(1)} copy-done((s32[1,1,32]{2,1,0:T(1,128)S(1)}, s32[1,1,32]{2,1,0:T(1,128)}, u32[]{:S(2)}) %copy-start.4) | copy-done | bytes 152
  11.1 0.1 pad_add_fusion.meta_ref.refs_1_
  11.1 0.8 %copy-done.3 = bf16[1,128,256]{2,1,0:T(8,128)(2,1)S(1)} copy-done((bf16[1,128,256]{2,1,0:T(8,128)(2,1)S(1)}, bf16[1,128,256]{2,1,0:T(8,128)(2,1)}, u32[]{:S(2)}) %copy-start.3) | copy-done | bytes 65560
  12.0 0.7 %collective-permute-done.refs_1_ = bf16[128,256]{1,0:T(8,128)(2,1)S(1)} collective-permute-done((bf16[128,256]{1,0:T(8,128)(2,1)}, bf16[128,256]{1,0:T(8,128)(2,1)S(1)}, u32[]{:S(2)}, u32[]{:S(2)}) %collective-permute-start) | collective-permute-done | bytes 65568 | tf_op jit(solution)/shard_map/ppermute | solution.py:165
  12.7 0.0 copy-start
  12.7 0.1 collective-permute-start.1
  12.8 0.0 collective-permute-done.8.refs_0_
  12.8 0.0 collective-permute-done.7.refs_3_.refs_6_
  12.8 0.0 collective-permute-done.5.refs_1_.refs_4_
  12.9 2.6 %collective-permute-start.11 = (bf16[128,256]{1,0:T(8,128)(2,1)S(1)}, bf16[128,256]{1,0:T(8,128)(2,1)S(1)}, u32[]{:S(2)}, u32[]{:S(2)}) collective-permute-start(bf16[128,256]{1,0:T(8,128)(2,1)S(1)} %bitcast.15), channel_id=1, source_target_pairs={{0,12},{4,8},{8,4},{12,0},{16,28},{20,24},{24,20},{28,16},{1,13},{... | collective-permute-start | bytes 196616 | tf_op jit(solution)/shard_map/ppermute | solution.py:165
  15.4 1.2 %dense.1.adj_ref.refs_0_ = bf16[512,1024]{1,0:T(8,128)(2,1)S(1)} custom-call(s32[33]{0:T(128)S(1)} %pad_add_fusion.meta_ref.refs_1_, bf16[32,128,128]{2,1,0:T(8,128)(2,1)S(1)} %bitcast.9), custom_call_target="tpu_custom_call" | custom-call | tf_op jit(solution)/shard_map/dense/pallas_call | solution.py:184
  16.7 0.0 copy-start.2
  16.7 0.5 collective-permute-start.10
  17.1 1.7 %collective-permute-start.9 = (bf16[128,256]{1,0:T(8,128)(2,1)S(1)}, bf16[128,256]{1,0:T(8,128)(2,1)S(1)}, u32[]{:S(2)}, u32[]{:S(2)}) collective-permute-start(bf16[128,256]{1,0:T(8,128)(2,1)S(1)} %bitcast.17), channel_id=1, source_target_pairs={{0,4},{4,0},{8,12},{12,8},{16,20},{20,16},{24,28},{28,24},{1,5},{5... | collective-permute-start | bytes 196616 | tf_op jit(solution)/shard_map/ppermute | solution.py:165
  18.9 0.6 %backward.1 = (bf16[2,128,256]{2,1,0:T(8,128)(2,1)S(1)}, bf16[2,128,256]{2,1,0:T(8,128)(2,1)S(1)}, bf16[2,128,256]{2,1,0:T(8,128)(2,1)S(1)}, bf16[2,128,256]{2,1,0:T(8,128)(2,1)S(1)}) custom-call(bf16[512,1024]{1,0:T(8,128)(2,1)S(1)} %dense.1.adj_ref.refs_0_, bf16[2,128,256]{2,1,0:T(8,128)(2,1)S(1)} %cot_near.1.near_ref.refs_1_, ...), custom_call_target="tpu_custom_call" | custom-call | tf_op jit(solution)/shard_map/backward/pallas_call | solution.py:184
  19.4 1.4 %collective-permute-start.2 = (bf16[2,128,256]{2,1,0:T(8,128)(2,1)S(1)}, bf16[2,128,256]{2,1,0:T(8,128)(2,1)S(1)}, u32[]{:S(2)}, u32[]{:S(2)}) collective-permute-start(bf16[2,128,256]{2,1,0:T(8,128)(2,1)S(1)} %get-tuple-element.20), channel_id=1, source_target_pairs={{0,12},{4,8},{8,4},{12,0},{16,28},{20,24},{24,20},{28,16},{1,13},{... | collective-permute-start | bytes 393224 | tf_op jit(solution)/shard_map/ppermute | solution.py:165
  20.9 0.4 collective-permute-start.3
  21.3 1.7 %collective-permute-start.4 = (bf16[2,128,256]{2,1,0:T(8,128)(2,1)S(1)}, bf16[2,128,256]{2,1,0:T(8,128)(2,1)S(1)}, u32[]{:S(2)}, u32[]{:S(2)}) collective-permute-start(bf16[2,128,256]{2,1,0:T(8,128)(2,1)S(1)} %get-tuple-element.22), channel_id=1, source_target_pairs={{0,4},{4,0},{8,12},{12,8},{16,20},{20,16},{24,28},{28,24},{1,5},{5... | collective-permute-start | bytes 393224 | tf_op jit(solution)/shard_map/ppermute | solution.py:165
  23.0 0.8 %forward.1 = (bf16[128,256]{1,0:T(8,128)(2,1)S(1)}, bf16[128,256]{1,0:T(8,128)(2,1)S(1)}, bf16[128,256]{1,0:T(8,128)(2,1)S(1)}, bf16[64,256]{1,0:T(8,128)(2,1)S(...) custom-call(bf16[512,1024]{1,0:T(8,128)(2,1)S(1)} %dense.1.adj_ref.refs_0_, ...), custom_call_target="tpu_custom_call" | custom-call | tf_op jit(solution)/shard_map/forward/pallas_call | solution.py:184
  23.8 0.1 collective-permute-start.12
  23.9 1.5 %collective-permute-start.13 = (bf16[64,256]{1,0:T(8,128)(2,1)S(1)}, bf16[64,256]{1,0:T(8,128)(2,1)S(1)}, u32[]{:S(2)}, u32[]{:S(2)}) collective-permute-start(bf16[64,256]{1,0:T(8,128)(2,1)S(1)} %get-tuple-element.28), channel_id=1, source_target_pairs={{0,2},{1,3},{2,0},{3,1},{4,6},{5,7},{6,4},{7,5},{8,10},{9,11},{10,... | collective-permute-start | bytes 98312 | tf_op jit(solution)/shard_map/ppermute | solution.py:165
  25.4 0.6 %collective-permute-done.2.refs_0_ = bf16[2,128,256]{2,1,0:T(8,128)(2,1)S(1)} collective-permute-done((bf16[2,128,256]{2,1,0:T(8,128)(2,1)S(1)}, bf16[2,128,256]{2,1,0:T(8,128)(2,1)S(1)}, u32[]{:S(2)}, u32[]{:S(2)}) %collective-permute-start.2) | collective-permute-done | bytes 131104 | tf_op jit(solution)/shard_map/ppermute | solution.py:165
  26.0 1.0 %collective-permute-done.3.refs_1_ = bf16[2,128,256]{2,1,0:T(8,128)(2,1)S(1)} collective-permute-done((bf16[2,128,256]{2,1,0:T(8,128)(2,1)S(1)}, bf16[2,128,256]{2,1,0:T(8,128)(2,1)S(1)}, u32[]{:S(2)}, u32[]{:S(2)}) %collective-permute-start.3) | collective-permute-done | bytes 131104 | tf_op jit(solution)/shard_map/ppermute | solution.py:165
  27.0 0.3 collective-permute-done.4.refs_2_
  27.3 0.1 pair_sum.1
  27.4 0.5 %collective-permute-done.13.refs_2_ = bf16[64,256]{1,0:T(8,128)(2,1)S(1)} collective-permute-done((bf16[64,256]{1,0:T(8,128)(2,1)S(1)}, bf16[64,256]{1,0:T(8,128)(2,1)S(1)}, u32[]{:S(2)}, u32[]{:S(2)}) %collective-permute-start.13) | collective-permute-done | bytes 32800 | tf_op jit(solution)/shard_map/ppermute | solution.py:165
  27.9 1.8 %collective-permute-done.14.refs_3_ = bf16[64,256]{1,0:T(8,128)(2,1)S(1)} collective-permute-done((bf16[64,256]{1,0:T(8,128)(2,1)S(1)}, bf16[64,256]{1,0:T(8,128)(2,1)S(1)}, u32[]{:S(2)}, u32[]{:S(2)}) %collective-permute-start.14) | collective-permute-done | bytes 32800 | tf_op jit(solution)/shard_map/ppermute | solution.py:165
  29.7 2.1 %collective-permute-start.17 = (bf16[64,256]{1,0:T(8,128)(2,1)S(1)}, bf16[64,256]{1,0:T(8,128)(2,1)S(1)}, u32[]{:S(2)}, u32[]{:S(2)}) collective-permute-start(bf16[64,256]{1,0:T(8,128)(2,1)S(1)} %grad_col.1.refs_1_), channel_id=1, source_target_pairs={{0,12},{4,8},{8,4},{12,0},{16,28},{20,24},{24,20},{28,16},{1,13},{... | collective-permute-start | bytes 98312 | tf_op jit(solution)/shard_map/ppermute | solution.py:165
  31.8 0.5 %collective-permute-start.16 = (bf16[64,256]{1,0:T(8,128)(2,1)S(1)}, bf16[64,256]{1,0:T(8,128)(2,1)S(1)}, u32[]{:S(2)}, u32[]{:S(2)}) collective-permute-start(bf16[64,256]{1,0:T(8,128)(2,1)S(1)} %grad_col.1.refs_1_), channel_id=1, source_target_pairs={{0,8},{4,12},{8,0},{12,4},{16,24},{20,28},{24,16},{28,20},{1,9},{5... | collective-permute-start | bytes 98312 | tf_op jit(solution)/shard_map/ppermute | solution.py:165
  32.3 1.0 %collective-permute-start.15 = (bf16[64,256]{1,0:T(8,128)(2,1)S(1)}, bf16[64,256]{1,0:T(8,128)(2,1)S(1)}, u32[]{:S(2)}, u32[]{:S(2)}) collective-permute-start(bf16[64,256]{1,0:T(8,128)(2,1)S(1)} %grad_col.1.refs_1_), channel_id=1, source_target_pairs={{0,4},{4,0},{8,12},{12,8},{16,20},{20,16},{24,28},{28,24},{1,5},{5... | collective-permute-start | bytes 98312 | tf_op jit(solution)/shard_map/ppermute | solution.py:165
  33.2 1.5 %collective-permute-done.17.refs_4_.refs_2_ = bf16[64,256]{1,0:T(8,128)(2,1)S(1)} collective-permute-done((bf16[64,256]{1,0:T(8,128)(2,1)S(1)}, bf16[64,256]{1,0:T(8,128)(2,1)S(1)}, u32[]{:S(2)}, u32[]{:S(2)}) %collective-permute-start.17) | collective-permute-done | bytes 32800 | tf_op jit(solution)/shard_map/ppermute | solution.py:165
  34.8 0.9 %collective-permute-done.16.refs_3_ = bf16[64,256]{1,0:T(8,128)(2,1)S(1)} collective-permute-done((bf16[64,256]{1,0:T(8,128)(2,1)S(1)}, bf16[64,256]{1,0:T(8,128)(2,1)S(1)}, u32[]{:S(2)}, u32[]{:S(2)}) %collective-permute-start.16) | collective-permute-done | bytes 32800 | tf_op jit(solution)/shard_map/ppermute | solution.py:165
  35.7 0.5 %collective-permute-done.15.refs_2_ = bf16[64,256]{1,0:T(8,128)(2,1)S(1)} collective-permute-done((bf16[64,256]{1,0:T(8,128)(2,1)S(1)}, bf16[64,256]{1,0:T(8,128)(2,1)S(1)}, u32[]{:S(2)}, u32[]{:S(2)}) %collective-permute-start.15) | collective-permute-done | bytes 32800 | tf_op jit(solution)/shard_map/ppermute | solution.py:165
  36.2 0.3 collective-permute-start.18
  36.6 0.0 copy-start.1
  36.6 1.2 %collective-permute-start.19 = (bf16[128,256]{1,0:T(8,128)(2,1)S(1)}, bf16[128,256]{1,0:T(8,128)(2,1)S(1)}, u32[]{:S(2)}, u32[]{:S(2)}) collective-permute-start(bf16[128,256]{1,0:T(8,128)(2,1)S(1)} %get-tuple-element.33), channel_id=1, source_target_pairs={{0,2},{1,3},{2,0},{3,1},{4,6},{5,7},{6,4},{7,5},{8,10},{9,11},{10,... | collective-permute-start | bytes 196616 | tf_op jit(solution)/shard_map/ppermute | solution.py:165
  37.8 4.0 %collective-permute-done.18.far_ref.got_ref = bf16[192,256]{1,0:T(8,128)(2,1)S(1)} collective-permute-done((bf16[192,256]{1,0:T(8,128)(2,1)S(1)}, bf16[192,256]{1,0:T(8,128)(2,1)S(1)}, u32[]{:S(2)}, u32[]{:S(2)}) %collective-permute-start.18) | collective-permute-done | bytes 98336 | tf_op jit(solution)/shard_map/ppermute | solution.py:165
  41.8 0.1 collective-permute-start.23
  41.9 2.5 %collective-permute-start.22 = (bf16[64,256]{1,0:T(8,128)(2,1)S(1)}, bf16[64,256]{1,0:T(8,128)(2,1)S(1)}, u32[]{:S(2)}, u32[]{:S(2)}) collective-permute-start(bf16[64,256]{1,0:T(8,128)(2,1)S(1)} %grad_row.1.refs_0_), channel_id=1, source_target_pairs={{0,2},{1,3},{2,0},{3,1},{4,6},{5,7},{6,4},{7,5},{8,10},{9,11},{10,... | collective-permute-start | bytes 98312 | tf_op jit(solution)/shard_map/ppermute | solution.py:165
  44.4 0.0 collective-permute-start.21
  44.5 0.8 %outputs.1 = (bf16[128,256]{1,0:T(8,128)(2,1)}, bf16[128,256]{1,0:T(8,128)(2,1)}) custom-call(bf16[256,256]{1,0:T(8,128)(2,1)S(1)} %copy-done.1, f32[128,256]{1,0:T(8,128)S(1)} %get-tuple-element.24.keep_ref, bf16[192,256]{1,0:T(8,128)(2,1)S(1)} %collective-permute-done.18.far_ref.got_ref, bf16[192,256]{1,0:T(8,128)(2,1)S(1)} %collective-permute-done.12.refs_0_.first_ref, ...), custom_call_target="tpu_custom_call" | custom-call | tf_op jit(solution)/shard_map/outputs/pallas_call | solution.py:184
  45.3 1.3 %collective-permute-done.22.refs_2_ = bf16[64,256]{1,0:T(8,128)(2,1)S(1)} collective-permute-done((bf16[64,256]{1,0:T(8,128)(2,1)S(1)}, bf16[64,256]{1,0:T(8,128)(2,1)S(1)}, u32[]{:S(2)}, u32[]{:S(2)}) %collective-permute-start.22) | collective-permute-done | bytes 32800 | tf_op jit(solution)/shard_map/ppermute | solution.py:165
  46.6 0.7 %convert_multiply_fusion = f32[256,256]{1,0:T(8,128)} fusion(bf16[256,256]{1,0:T(8,128)(2,1)S(1)} %weight_grad.1), kind=kLoop, calls=%fused_computation | loop fusion | flops 131072 | bytes 393216 | tf_op jit(solution)/shard_map/mul | solution.py:275
  (25 shorter events, 0.1 us)
Async XLA Ops:
  0.6 12.2 %collective-permute-start.8 = (bf16[128,256]{1,0:T(8,128)(2,1)}, bf16[128,256]{1,0:T(8,128)(2,1)S(1)}, u32[]{:S(2)}, u32[]{:S(2)}) collective-permute-start(bf16[128,256]{1,0:T(8,128)(2,1)} %bitcast.10), channel_id=1, source_target_pairs={{0,16},{4,20},{8,24},{12,28},{16,0},{20,4},{24,8},{28,12},{1,17},{... | collective-permute-start | bytes 196616 | tf_op jit(solution)/shard_map/ppermute | solution.py:165
  4.7 8.1 %collective-permute-start.7 = (bf16[128,256]{1,0:T(8,128)(2,1)}, bf16[128,256]{1,0:T(8,128)(2,1)S(1)}, u32[]{:S(2)}, u32[]{:S(2)}) collective-permute-start(bf16[128,256]{1,0:T(8,128)(2,1)} %bitcast.11), channel_id=1, source_target_pairs={{0,12},{4,8},{8,4},{12,0},{16,28},{20,24},{24,20},{28,16},{1,13},{... | collective-permute-start | bytes 196616 | tf_op jit(solution)/shard_map/ppermute | solution.py:165
  7.2 5.6 %collective-permute-start.6 = (bf16[128,256]{1,0:T(8,128)(2,1)}, bf16[128,256]{1,0:T(8,128)(2,1)S(1)}, u32[]{:S(2)}, u32[]{:S(2)}) collective-permute-start(bf16[128,256]{1,0:T(8,128)(2,1)} %bitcast.12), channel_id=1, source_target_pairs={{0,8},{4,12},{8,0},{12,4},{16,24},{20,28},{24,16},{28,20},{1,9},{5... | collective-permute-start | bytes 196616 | tf_op jit(solution)/shard_map/ppermute | solution.py:165
  7.7 5.2 %collective-permute-start.5 = (bf16[128,256]{1,0:T(8,128)(2,1)}, bf16[128,256]{1,0:T(8,128)(2,1)S(1)}, u32[]{:S(2)}, u32[]{:S(2)}) collective-permute-start(bf16[128,256]{1,0:T(8,128)(2,1)} %bitcast.13), channel_id=1, source_target_pairs={{0,4},{4,0},{8,12},{12,8},{16,20},{20,16},{24,28},{28,24},{1,5},{5... | collective-permute-start | bytes 196616 | tf_op jit(solution)/shard_map/ppermute | solution.py:165
  8.2 4.5 %collective-permute-start = (bf16[128,256]{1,0:T(8,128)(2,1)}, bf16[128,256]{1,0:T(8,128)(2,1)S(1)}, u32[]{:S(2)}, u32[]{:S(2)}) collective-permute-start(bf16[128,256]{1,0:T(8,128)(2,1)} %bitcast.19), channel_id=1, source_target_pairs={{0,2},{1,3},{2,0},{3,1},{4,6},{5,7},{6,4},{7,5},{8,10},{9,11},{10,... | collective-permute-start | bytes 196616 | tf_op jit(solution)/shard_map/ppermute | solution.py:165
  10.4 0.7 %copy-start.4 = (s32[1,1,32]{2,1,0:T(1,128)S(1)}, s32[1,1,32]{2,1,0:T(1,128)}, u32[]{:S(2)}) copy-start(s32[1,1,32]{2,1,0:T(1,128)} %param.9) | copy-start | bytes 388
  11.1 0.8 %copy-start.3 = (bf16[1,128,256]{2,1,0:T(8,128)(2,1)S(1)}, bf16[1,128,256]{2,1,0:T(8,128)(2,1)}, u32[]{:S(2)}) copy-start(bf16[1,128,256]{2,1,0:T(8,128)(2,1)} %param.11) | copy-start | bytes 196612
  12.7 2.7 %copy-start = (bf16[1,1,32,128,128]{4,3,2,1,0:T(8,128)(2,1)S(1)}, bf16[1,1,32,128,128]{4,3,2,1,0:T(8,128)(2,1)}, u32[]{:S(2)}) copy-start(bf16[1,1,32,128,128]{4,3,2,1,0:T(8,128)(2,1)} %param.8) | copy-start | bytes 3145732
  12.7 6.1 %collective-permute-start.1 = (bf16[2,128,256]{2,1,0:T(8,128)(2,1)S(1)}, bf16[2,128,256]{2,1,0:T(8,128)(2,1)S(1)}, u32[]{:S(2)}, u32[]{:S(2)}) collective-permute-start(bf16[2,128,256]{2,1,0:T(8,128)(2,1)S(1)} %cot_near.1.near_ref.refs_1_), channel_id=1, source_target_pairs={{0,1},{1,0},{2,3},{3,2},{4,5},{5,4},{6,7},{7,6},{8,9},{9,8},{10,11... | collective-permute-start | bytes 393224 | tf_op jit(solution)/shard_map/ppermute | solution.py:165
  12.9 8.4 %collective-permute-start.11 = (bf16[128,256]{1,0:T(8,128)(2,1)S(1)}, bf16[128,256]{1,0:T(8,128)(2,1)S(1)}, u32[]{:S(2)}, u32[]{:S(2)}) collective-permute-start(bf16[128,256]{1,0:T(8,128)(2,1)S(1)} %bitcast.15), channel_id=1, source_target_pairs={{0,12},{4,8},{8,4},{12,0},{16,28},{20,24},{24,20},{28,16},{1,13},{... | collective-permute-start | bytes 196616 | tf_op jit(solution)/shard_map/ppermute | solution.py:165
  16.7 6.3 %copy-start.2 = (bf16[1,128,256]{2,1,0:T(8,128)(2,1)S(1)}, bf16[1,128,256]{2,1,0:T(8,128)(2,1)}, u32[]{:S(2)}) copy-start(bf16[1,128,256]{2,1,0:T(8,128)(2,1)} %param.6) | copy-start | bytes 196612
  16.7 6.3 %collective-permute-start.10 = (bf16[128,256]{1,0:T(8,128)(2,1)S(1)}, bf16[128,256]{1,0:T(8,128)(2,1)S(1)}, u32[]{:S(2)}, u32[]{:S(2)}) collective-permute-start(bf16[128,256]{1,0:T(8,128)(2,1)S(1)} %bitcast.16), channel_id=1, source_target_pairs={{0,8},{4,12},{8,0},{12,4},{16,24},{20,28},{24,16},{28,20},{1,9},{5... | collective-permute-start | bytes 196616 | tf_op jit(solution)/shard_map/ppermute | solution.py:165
  17.1 5.9 %collective-permute-start.9 = (bf16[128,256]{1,0:T(8,128)(2,1)S(1)}, bf16[128,256]{1,0:T(8,128)(2,1)S(1)}, u32[]{:S(2)}, u32[]{:S(2)}) collective-permute-start(bf16[128,256]{1,0:T(8,128)(2,1)S(1)} %bitcast.17), channel_id=1, source_target_pairs={{0,4},{4,0},{8,12},{12,8},{16,20},{20,16},{24,28},{28,24},{1,5},{5... | collective-permute-start | bytes 196616 | tf_op jit(solution)/shard_map/ppermute | solution.py:165
  19.4 6.6 %collective-permute-start.2 = (bf16[2,128,256]{2,1,0:T(8,128)(2,1)S(1)}, bf16[2,128,256]{2,1,0:T(8,128)(2,1)S(1)}, u32[]{:S(2)}, u32[]{:S(2)}) collective-permute-start(bf16[2,128,256]{2,1,0:T(8,128)(2,1)S(1)} %get-tuple-element.20), channel_id=1, source_target_pairs={{0,12},{4,8},{8,4},{12,0},{16,28},{20,24},{24,20},{28,16},{1,13},{... | collective-permute-start | bytes 393224 | tf_op jit(solution)/shard_map/ppermute | solution.py:165
  20.9 6.1 %collective-permute-start.3 = (bf16[2,128,256]{2,1,0:T(8,128)(2,1)S(1)}, bf16[2,128,256]{2,1,0:T(8,128)(2,1)S(1)}, u32[]{:S(2)}, u32[]{:S(2)}) collective-permute-start(bf16[2,128,256]{2,1,0:T(8,128)(2,1)S(1)} %get-tuple-element.21), channel_id=1, source_target_pairs={{0,8},{4,12},{8,0},{12,4},{16,24},{20,28},{24,16},{28,20},{1,9},{5... | collective-permute-start | bytes 393224 | tf_op jit(solution)/shard_map/ppermute | solution.py:165
  21.3 6.0 %collective-permute-start.4 = (bf16[2,128,256]{2,1,0:T(8,128)(2,1)S(1)}, bf16[2,128,256]{2,1,0:T(8,128)(2,1)S(1)}, u32[]{:S(2)}, u32[]{:S(2)}) collective-permute-start(bf16[2,128,256]{2,1,0:T(8,128)(2,1)S(1)} %get-tuple-element.22), channel_id=1, source_target_pairs={{0,4},{4,0},{8,12},{12,8},{16,20},{20,16},{24,28},{28,24},{1,5},{5... | collective-permute-start | bytes 393224 | tf_op jit(solution)/shard_map/ppermute | solution.py:165
  23.8 5.9 %collective-permute-start.12 = (bf16[192,256]{1,0:T(8,128)(2,1)S(1)}, bf16[192,256]{1,0:T(8,128)(2,1)S(1)}, u32[]{:S(2)}, u32[]{:S(2)}) collective-permute-start(bf16[192,256]{1,0:T(8,128)(2,1)S(1)} %get-tuple-element.26), channel_id=1, source_target_pairs={{0,1},{1,0},{2,3},{3,2},{4,5},{5,4},{6,7},{7,6},{8,9},{9,8},{10,11... | collective-permute-start | bytes 294920 | tf_op jit(solution)/shard_map/ppermute | solution.py:165
  23.9 4.0 %collective-permute-start.13 = (bf16[64,256]{1,0:T(8,128)(2,1)S(1)}, bf16[64,256]{1,0:T(8,128)(2,1)S(1)}, u32[]{:S(2)}, u32[]{:S(2)}) collective-permute-start(bf16[64,256]{1,0:T(8,128)(2,1)S(1)} %get-tuple-element.28), channel_id=1, source_target_pairs={{0,2},{1,3},{2,0},{3,1},{4,6},{5,7},{6,4},{7,5},{8,10},{9,11},{10,... | collective-permute-start | bytes 98312 | tf_op jit(solution)/shard_map/ppermute | solution.py:165
  26.0 3.7 %collective-permute-start.14 = (bf16[64,256]{1,0:T(8,128)(2,1)S(1)}, bf16[64,256]{1,0:T(8,128)(2,1)S(1)}, u32[]{:S(2)}, u32[]{:S(2)}) collective-permute-start(bf16[64,256]{1,0:T(8,128)(2,1)S(1)} %get-tuple-element.29), channel_id=1, source_target_pairs={{0,3},{1,2},{2,1},{3,0},{4,7},{5,6},{6,5},{7,4},{8,11},{9,10},{10,... | collective-permute-start | bytes 98312 | tf_op jit(solution)/shard_map/ppermute | solution.py:165
  29.7 5.1 %collective-permute-start.17 = (bf16[64,256]{1,0:T(8,128)(2,1)S(1)}, bf16[64,256]{1,0:T(8,128)(2,1)S(1)}, u32[]{:S(2)}, u32[]{:S(2)}) collective-permute-start(bf16[64,256]{1,0:T(8,128)(2,1)S(1)} %grad_col.1.refs_1_), channel_id=1, source_target_pairs={{0,12},{4,8},{8,4},{12,0},{16,28},{20,24},{24,20},{28,16},{1,13},{... | collective-permute-start | bytes 98312 | tf_op jit(solution)/shard_map/ppermute | solution.py:165
  31.8 3.9 %collective-permute-start.16 = (bf16[64,256]{1,0:T(8,128)(2,1)S(1)}, bf16[64,256]{1,0:T(8,128)(2,1)S(1)}, u32[]{:S(2)}, u32[]{:S(2)}) collective-permute-start(bf16[64,256]{1,0:T(8,128)(2,1)S(1)} %grad_col.1.refs_1_), channel_id=1, source_target_pairs={{0,8},{4,12},{8,0},{12,4},{16,24},{20,28},{24,16},{28,20},{1,9},{5... | collective-permute-start | bytes 98312 | tf_op jit(solution)/shard_map/ppermute | solution.py:165
  32.3 3.9 %collective-permute-start.15 = (bf16[64,256]{1,0:T(8,128)(2,1)S(1)}, bf16[64,256]{1,0:T(8,128)(2,1)S(1)}, u32[]{:S(2)}, u32[]{:S(2)}) collective-permute-start(bf16[64,256]{1,0:T(8,128)(2,1)S(1)} %grad_col.1.refs_1_), channel_id=1, source_target_pairs={{0,4},{4,0},{8,12},{12,8},{16,20},{20,16},{24,28},{28,24},{1,5},{5... | collective-permute-start | bytes 98312 | tf_op jit(solution)/shard_map/ppermute | solution.py:165
  36.2 5.6 %collective-permute-start.18 = (bf16[192,256]{1,0:T(8,128)(2,1)S(1)}, bf16[192,256]{1,0:T(8,128)(2,1)S(1)}, u32[]{:S(2)}, u32[]{:S(2)}) collective-permute-start(bf16[192,256]{1,0:T(8,128)(2,1)S(1)} %grad_near.1.held_ref), channel_id=1, source_target_pairs={{0,16},{4,20},{8,24},{12,28},{16,0},{20,4},{24,8},{28,12},{1,17},{... | collective-permute-start | bytes 294920 | tf_op jit(solution)/shard_map/ppermute | solution.py:165
  36.6 7.9 %copy-start.1 = (bf16[256,256]{1,0:T(8,128)(2,1)S(1)}, bf16[256,256]{1,0:T(8,128)(2,1)}, u32[]{:S(2)}) copy-start(bf16[256,256]{1,0:T(8,128)(2,1)} %weight_ref.1) | copy-start | bytes 393220
  36.6 7.9 %collective-permute-start.19 = (bf16[128,256]{1,0:T(8,128)(2,1)S(1)}, bf16[128,256]{1,0:T(8,128)(2,1)S(1)}, u32[]{:S(2)}, u32[]{:S(2)}) collective-permute-start(bf16[128,256]{1,0:T(8,128)(2,1)S(1)} %get-tuple-element.33), channel_id=1, source_target_pairs={{0,2},{1,3},{2,0},{3,1},{4,6},{5,7},{6,4},{7,5},{8,10},{9,11},{10,... | collective-permute-start | bytes 196616 | tf_op jit(solution)/shard_map/ppermute | solution.py:165
  37.8 6.7 %collective-permute-start.20 = (bf16[128,256]{1,0:T(8,128)(2,1)S(1)}, bf16[128,256]{1,0:T(8,128)(2,1)S(1)}, u32[]{:S(2)}, u32[]{:S(2)}) collective-permute-start(bf16[128,256]{1,0:T(8,128)(2,1)S(1)} %get-tuple-element.34), channel_id=1, source_target_pairs={{0,3},{1,2},{2,1},{3,0},{4,7},{5,6},{6,5},{7,4},{8,11},{9,10},{10,... | collective-permute-start | bytes 196616 | tf_op jit(solution)/shard_map/ppermute | solution.py:165
  41.8 3.5 %collective-permute-start.23 = (bf16[64,256]{1,0:T(8,128)(2,1)S(1)}, bf16[64,256]{1,0:T(8,128)(2,1)S(1)}, u32[]{:S(2)}, u32[]{:S(2)}) collective-permute-start(bf16[64,256]{1,0:T(8,128)(2,1)S(1)} %grad_row.1.refs_0_), channel_id=1, source_target_pairs={{0,3},{1,2},{2,1},{3,0},{4,7},{5,6},{6,5},{7,4},{8,11},{9,10},{10,... | collective-permute-start | bytes 98312 | tf_op jit(solution)/shard_map/ppermute | solution.py:165
  41.9 4.7 %collective-permute-start.22 = (bf16[64,256]{1,0:T(8,128)(2,1)S(1)}, bf16[64,256]{1,0:T(8,128)(2,1)S(1)}, u32[]{:S(2)}, u32[]{:S(2)}) collective-permute-start(bf16[64,256]{1,0:T(8,128)(2,1)S(1)} %grad_row.1.refs_0_), channel_id=1, source_target_pairs={{0,2},{1,3},{2,0},{3,1},{4,6},{5,7},{6,4},{7,5},{8,10},{9,11},{10,... | collective-permute-start | bytes 98312 | tf_op jit(solution)/shard_map/ppermute | solution.py:165
  44.4 2.2 %collective-permute-start.21 = (bf16[64,256]{1,0:T(8,128)(2,1)S(1)}, bf16[64,256]{1,0:T(8,128)(2,1)S(1)}, u32[]{:S(2)}, u32[]{:S(2)}) collective-permute-start(bf16[64,256]{1,0:T(8,128)(2,1)S(1)} %grad_row.1.refs_0_), channel_id=1, source_target_pairs={{0,1},{1,0},{2,3},{3,2},{4,5},{5,4},{6,7},{7,6},{8,9},{9,8},{10,11... | collective-permute-start | bytes 98312 | tf_op jit(solution)/shard_map/ppermute | solution.py:165

commit v5 on v3

--- a/solution.py
+++ b/solution.py
@@ -95,23 +95,25 @@
     both_ref[slab:, :] = grad[rows_of(lax.axis_index("col") ^ 1, piece), :]
 
 
-def backward_kernel(adj_ref, near_ref, other_ref, *refs):
-    *pair_refs, cots, total = refs
-    half, slab = len(pair_refs), pair_refs[0].shape[1]
+def backward_kernel(adj_ref, near_ref, other_ref, keep_ref, *refs):
+    *send_refs, cots, total = refs
+    slab = near_ref.shape[1]
     place_cots(near_ref, other_ref, cots)
     total[...] = lax.dot_general(
         adj_ref[...], cots[...], (((0,), (0,)), ((), ())), preferred_element_type=F32
     ).astype(BF16)
-    for k, ref in enumerate(pair_refs):
-        ref[0] = total[rows_of(lax.axis_index("row") ^ k, slab), :]
-        ref[1] = total[rows_of(lax.axis_index("row") ^ k ^ half, slab), :]
-
-
-def pair_sum_kernel(*refs):
-    *pair_refs, keep_ref, send_ref = refs
-    total = summed(pair_refs)
-    keep_ref[...] = total[0]
-    send_ref[...] = total[1].astype(BF16)
+    sends = [ref.at[m] for ref in send_refs for m in range(ref.shape[0])]
+    for m, send in enumerate(sends):
+        keep_ref[m] = total[rows_of(lax.axis_index("row") ^ (2 * m), slab), :]
+        send[...] = total[rows_of(lax.axis_index("row") ^ (2 * m + 1), slab), :]
+
+
+def halve_kernel(held_ref, *refs, count):
+    got_refs, (keep_ref, send_ref) = refs[:count], refs[-2:]
+    got = [ref.at[m] for ref in got_refs for m in range(ref.shape[0])]
+    for m in range(keep_ref.shape[0]):
+        keep_ref[m] = summed([held_ref.at[2 * m], got[2 * m]]).astype(BF16)
+        send_ref[m] = summed([held_ref.at[2 * m + 1], got[2 * m + 1]]).astype(BF16)
 
 
 def weighted(weight_ref, term_refs, contract):
@@ -234,24 +236,33 @@
             pltpu.VMEM((width, width), BF16),
         ],
     )
-    column_pairs = call(
-        backward_kernel, "backward", [shape(2, slab, width)] * half,
+    keep, *send = call(
+        backward_kernel, "backward",
+        [shape(half, slab, width)] + [shape(half // 2, slab, width)] * 2,
         [VMEM] * 3, (adj, cot_near, cot_other),
         scratch=[pltpu.VMEM((rows, width), BF16), pltpu.VMEM((cols, width), BF16)],
     )
     chunks, pieces = outs[: col_devices - 1], outs[col_devices - 1 : -1]
     first = swap(outs[-1], "col", 1)
 
-    column_keep, column_send = call(
-        pair_sum_kernel, "pair_sum", [shape(slab, width, dtype=F32), shape(slab, width)],
-        [VMEM] * half, exchange(column_pairs, "row")[::-1], micros=5,
-    )
     def fetch(arrays):
         return [arrays[0]] + [swap(arrays[k - 1], "col", k) for k in range(2, col_devices)]
 
+    grad_got = fetch(pieces)
+    distance, after = 1, [first, *grad_got[1:]]
+    while distance < half:
+        got = [swap(array, "row", distance) for array in send]
+        keep, *send = call(
+            lambda *refs: halve_kernel(*refs, count=len(got)), "halve",
+            [shape(half // (2 * distance), slab, width)] * 2,
+            [VMEM] * (1 + len(got)) + [ANY] * len(after), (keep, *got, *after), micros=None,
+        )
+        distance, after = 2 * distance, []
+    column_keep, column_send = keep[0], send[0][0]
+
     grad_col = call(
         lambda *refs: col_kernel(*refs, terms=col_devices - 1), "grad_col", shape(piece, width),
-        [VMEM] * col_devices + [ANY], (first, *fetch(pieces), column_send),
+        [VMEM] * col_devices, (first, *grad_got),
     )
     near_terms = exchange([grad_col] * half, "row")
     row_got = fetch([chunks[0], *hold(chunks[1:], near_terms[3], "hold_chunks")])

time: 43.2 us -> 45.4 us (1.051)
  waiting for transfers between devices: 11.3 us -> 14.3 us
  starting transfers between devices: 23.8 us -> 22.6 us
    ppermute x21, waiting for transfers between devices: 11.3 us -> 14.3 us  [swap(): return lax.ppermute(array, axis, pairs)]
    ppermute x21, starting transfers between devices: 23.8 us -> 22.6 us  [swap(): return lax.ppermute(array, axis, pairs)]
    pallas_call x13 -> x14, Pallas kernels: 3.37 us -> 3.54 us  [call(): pl.pallas_call(kernel, out_shape=out_shape, in_specs=in_specs, out_specs=...]
  transfers between devices with their start and end apart: 21 -> 21, of which waited for: 11 -> 9; matrix products, arithmetic and copies ran while one was open for 0% -> 0% of each run, Pallas kernels for 8% -> 8%
where the time goes in v5:
time: 45.4 us; the launch traced here: 45.1 us
  starting transfers between devices  22.6 us (50%)
  waiting for transfers between devices  14.3 us (31%)
  Pallas kernels  3.54 us (8%)
  local copies, waits for them, and re-layouts  2.34 us (5%)
  between operations  1.45 us (3%)
  other arithmetic  0.8 us (2%)
    ppermute x21, starting transfers between devices, swap(): return lax.ppermute(array, axis, pairs)  22.6 us
    ppermute x21, waiting for transfers between devices, swap(): return lax.ppermute(array, axis, pairs)  14.3 us
    pallas_call x14, Pallas kernels, call(): pl.pallas_call(kernel, out_shape=out_shape, in_specs=in_specs, out_specs=...  3.54 us
    unnamed x10, local copies, waits for them, and re-layouts  2.34 us
  transfers between devices with their start and end apart: 21, of which 9 were waited for; matrix products, arithmetic and copies ran while one was open for 0% of the time, Pallas kernels for 8%

profile of v5, /device:TPU:0, one launch (start us, length us, event | category | flops | bytes accessed | tf_op | source)
XLA Modules:
  0.0 45.1 jit_solution(6007622995093275592)
XLA Ops:
  0.6 4.1 %collective-permute-start.4 = (bf16[128,256]{1,0:T(8,128)(2,1)}, bf16[128,256]{1,0:T(8,128)(2,1)S(1)}, u32[]{:S(2)}, u32[]{:S(2)}) collective-permute-start(bf16[128,256]{1,0:T(8,128)(2,1)} %bitcast.14), channel_id=1, source_target_pairs={{0,16},{4,20},{8,24},{12,28},{16,0},{20,4},{24,8},{28,12},{1,17},{... | collective-permute-start | bytes 196616 | tf_op jit(solution)/shard_map/ppermute | solution.py:167
  4.7 1.5 %collective-permute-start = (bf16[128,256]{1,0:T(8,128)(2,1)}, bf16[128,256]{1,0:T(8,128)(2,1)S(1)}, u32[]{:S(2)}, u32[]{:S(2)}) collective-permute-start(bf16[128,256]{1,0:T(8,128)(2,1)} %bitcast.12), channel_id=1, source_target_pairs={{0,2},{1,3},{2,0},{3,1},{4,6},{5,7},{6,4},{7,5},{8,10},{9,11},{10,... | collective-permute-start | bytes 196616 | tf_op jit(solution)/shard_map/ppermute | solution.py:167
  6.9 0.6 %copy-done.4 = s32[1,1,32]{2,1,0:T(1,128)S(1)} copy-done((s32[1,1,32]{2,1,0:T(1,128)S(1)}, s32[1,1,32]{2,1,0:T(1,128)}, u32[]{:S(2)}) %copy-start.4) | copy-done | bytes 152
  7.6 0.1 pad_add_fusion.meta_ref.refs_2_
  7.6 0.8 %copy-done.2 = bf16[1,128,256]{2,1,0:T(8,128)(2,1)S(1)} copy-done((bf16[1,128,256]{2,1,0:T(8,128)(2,1)S(1)}, bf16[1,128,256]{2,1,0:T(8,128)(2,1)}, u32[]{:S(2)}) %copy-start.2) | copy-done | bytes 65560
  8.5 0.8 %copy-done.3 = bf16[1,128,256]{2,1,0:T(8,128)(2,1)S(1)} copy-done((bf16[1,128,256]{2,1,0:T(8,128)(2,1)S(1)}, bf16[1,128,256]{2,1,0:T(8,128)(2,1)}, u32[]{:S(2)}) %copy-start.3) | copy-done | bytes 65560
  9.3 0.0 collective-permute-done.refs_1_
  9.4 0.1 collective-permute-start.1
  9.4 0.0 copy-start
  9.5 2.6 %collective-permute-start.7 = (bf16[2,128,256]{2,1,0:T(8,128)(2,1)S(1)}, bf16[2,128,256]{2,1,0:T(8,128)(2,1)S(1)}, u32[]{:S(2)}, u32[]{:S(2)}) collective-permute-start(bf16[2,128,256]{2,1,0:T(8,128)(2,1)S(1)} %pair.1.refs_3_), channel_id=1, source_target_pairs={{0,12},{4,8},{8,4},{12,0},{16,28},{20,24},{24,20},{28,16},{1,13},{... | collective-permute-start | bytes 393224 | tf_op jit(solution)/shard_map/ppermute | solution.py:167
  12.0 0.4 collective-permute-start.6
  12.5 0.5 %collective-permute-start.5 = (bf16[2,128,256]{2,1,0:T(8,128)(2,1)S(1)}, bf16[2,128,256]{2,1,0:T(8,128)(2,1)S(1)}, u32[]{:S(2)}, u32[]{:S(2)}) collective-permute-start(bf16[2,128,256]{2,1,0:T(8,128)(2,1)S(1)} %pair.1.refs_3_), channel_id=1, source_target_pairs={{0,4},{4,0},{8,12},{12,8},{16,20},{20,16},{24,28},{28,24},{1,5},{5... | collective-permute-start | bytes 393224 | tf_op jit(solution)/shard_map/ppermute | solution.py:167
  13.0 1.1 %dense.1.adj_ref.refs_0_ = bf16[512,1024]{1,0:T(8,128)(2,1)S(1)} custom-call(s32[33]{0:T(128)S(1)} %pad_add_fusion.meta_ref.refs_2_, bf16[32,128,128]{2,1,0:T(8,128)(2,1)S(1)} %bitcast.10), custom_call_target="tpu_custom_call" | custom-call | tf_op jit(solution)/shard_map/dense/pallas_call | solution.py:186
  14.2 0.0 collective-permute-done.1.other_ref.refs_2_
  14.2 0.6 %backward.1 = (bf16[4,128,256]{2,1,0:T(8,128)(2,1)S(1)}, bf16[2,128,256]{2,1,0:T(8,128)(2,1)S(1)}, bf16[2,128,256]{2,1,0:T(8,128)(2,1)S(1)}) custom-call(bf16[512,1024]{1,0:T(8,128)(2,1)S(1)} %dense.1.adj_ref.refs_0_, bf16[2,128,256]{2,1,0:T(8,128)(2,1)S(1)} %cot_near.1.near_ref.refs_1_, bf16[2,128,256]{2,1,0:T(8,128)(2,1)S(1)} %collective-permute-done.1.other_ref.refs_2_), custom_call_target="tpu_custom_call" | custom-call | tf_op jit(solution)/shard_map/backward/pallas_call | solution.py:186
  14.8 1.4 %collective-permute-start.2 = (bf16[2,128,256]{2,1,0:T(8,128)(2,1)S(1)}, bf16[2,128,256]{2,1,0:T(8,128)(2,1)S(1)}, u32[]{:S(2)}, u32[]{:S(2)}) collective-permute-start(bf16[2,128,256]{2,1,0:T(8,128)(2,1)S(1)} %get-tuple-element.25), channel_id=1, source_target_pairs={{0,4},{4,0},{8,12},{12,8},{16,20},{20,16},{24,28},{28,24},{1,5},{5... | collective-permute-start | bytes 393224 | tf_op jit(solution)/shard_map/ppermute | solution.py:167
  16.2 0.7 %collective-permute-start.3 = (bf16[2,128,256]{2,1,0:T(8,128)(2,1)S(1)}, bf16[2,128,256]{2,1,0:T(8,128)(2,1)S(1)}, u32[]{:S(2)}, u32[]{:S(2)}) collective-permute-start(bf16[2,128,256]{2,1,0:T(8,128)(2,1)S(1)} %get-tuple-element.26), channel_id=1, source_target_pairs={{0,4},{4,0},{8,12},{12,8},{16,20},{20,16},{24,28},{28,24},{1,5},{5... | collective-permute-start | bytes 393224 | tf_op jit(solution)/shard_map/ppermute | solution.py:167
  16.8 0.0 collective-permute-done.7.refs_6_
  16.9 2.3 %collective-permute-done.6.refs_5_ = bf16[2,128,256]{2,1,0:T(8,128)(2,1)S(1)} collective-permute-done((bf16[2,128,256]{2,1,0:T(8,128)(2,1)S(1)}, bf16[2,128,256]{2,1,0:T(8,128)(2,1)S(1)}, u32[]{:S(2)}, u32[]{:S(2)}) %collective-permute-start.6) | collective-permute-done | bytes 131104 | tf_op jit(solution)/shard_map/ppermute | solution.py:167
  19.2 0.0 collective-permute-done.5.refs_4_
  19.2 0.8 %forward.1 = (bf16[128,256]{1,0:T(8,128)(2,1)S(1)}, bf16[128,256]{1,0:T(8,128)(2,1)S(1)}, bf16[128,256]{1,0:T(8,128)(2,1)S(1)}, bf16[64,256]{1,0:T(8,128)(2,1)S(...) custom-call(bf16[512,1024]{1,0:T(8,128)(2,1)S(1)} %dense.1.adj_ref.refs_0_, ...), custom_call_target="tpu_custom_call" | custom-call | tf_op jit(solution)/shard_map/forward/pallas_call | solution.py:186
  20.0 0.1 collective-permute-start.8
  20.1 1.4 %collective-permute-start.9 = (bf16[64,256]{1,0:T(8,128)(2,1)S(1)}, bf16[64,256]{1,0:T(8,128)(2,1)S(1)}, u32[]{:S(2)}, u32[]{:S(2)}) collective-permute-start(bf16[64,256]{1,0:T(8,128)(2,1)S(1)} %get-tuple-element.29), channel_id=1, source_target_pairs={{0,2},{1,3},{2,0},{3,1},{4,6},{5,7},{6,4},{7,5},{8,10},{9,11},{10,... | collective-permute-start | bytes 98312 | tf_op jit(solution)/shard_map/ppermute | solution.py:167
  21.6 0.4 collective-permute-start.10
  22.0 2.1 %collective-permute-done.9.refs_4_.refs_2_ = bf16[64,256]{1,0:T(8,128)(2,1)S(1)} collective-permute-done((bf16[64,256]{1,0:T(8,128)(2,1)S(1)}, bf16[64,256]{1,0:T(8,128)(2,1)S(1)}, u32[]{:S(2)}, u32[]{:S(2)}) %collective-permute-start.9) | collective-permute-done | bytes 32800 | tf_op jit(solution)/shard_map/ppermute | solution.py:167
  24.1 0.8 %collective-permute-done.10.refs_5_.refs_3_ = bf16[64,256]{1,0:T(8,128)(2,1)S(1)} collective-permute-done((bf16[64,256]{1,0:T(8,128)(2,1)S(1)}, bf16[64,256]{1,0:T(8,128)(2,1)S(1)}, u32[]{:S(2)}, u32[]{:S(2)}) %collective-permute-start.10) | collective-permute-done | bytes 32800 | tf_op jit(solution)/shard_map/ppermute | solution.py:167
  24.9 0.1 halve.2
  25.0 1.6 %collective-permute-start.11 = (bf16[2,128,256]{2,1,0:T(8,128)(2,1)S(1)}, bf16[2,128,256]{2,1,0:T(8,128)(2,1)S(1)}, u32[]{:S(2)}, u32[]{:S(2)}) collective-permute-start(bf16[2,128,256]{2,1,0:T(8,128)(2,1)S(1)} %get-tuple-element.32), channel_id=1, source_target_pairs={{0,8},{4,12},{8,0},{12,4},{16,24},{20,28},{24,16},{28,20},{1,9},{5... | collective-permute-start | bytes 393224 | tf_op jit(solution)/shard_map/ppermute | solution.py:167
  26.6 1.4 %collective-permute-start.14 = (bf16[64,256]{1,0:T(8,128)(2,1)S(1)}, bf16[64,256]{1,0:T(8,128)(2,1)S(1)}, u32[]{:S(2)}, u32[]{:S(2)}) collective-permute-start(bf16[64,256]{1,0:T(8,128)(2,1)S(1)} %grad_col.1.refs_1_), channel_id=1, source_target_pairs={{0,12},{4,8},{8,4},{12,0},{16,28},{20,24},{24,20},{28,16},{1,13},{... | collective-permute-start | bytes 98312 | tf_op jit(solution)/shard_map/ppermute | solution.py:167
  28.1 1.6 %collective-permute-start.13 = (bf16[64,256]{1,0:T(8,128)(2,1)S(1)}, bf16[64,256]{1,0:T(8,128)(2,1)S(1)}, u32[]{:S(2)}, u32[]{:S(2)}) collective-permute-start(bf16[64,256]{1,0:T(8,128)(2,1)S(1)} %grad_col.1.refs_1_), channel_id=1, source_target_pairs={{0,8},{4,12},{8,0},{12,4},{16,24},{20,28},{24,16},{28,20},{1,9},{5... | collective-permute-start | bytes 98312 | tf_op jit(solution)/shard_map/ppermute | solution.py:167
  29.7 0.5 %collective-permute-start.12 = (bf16[64,256]{1,0:T(8,128)(2,1)S(1)}, bf16[64,256]{1,0:T(8,128)(2,1)S(1)}, u32[]{:S(2)}, u32[]{:S(2)}) collective-permute-start(bf16[64,256]{1,0:T(8,128)(2,1)S(1)} %grad_col.1.refs_1_), channel_id=1, source_target_pairs={{0,4},{4,0},{8,12},{12,8},{16,20},{20,16},{24,28},{28,24},{1,5},{5... | collective-permute-start | bytes 98312 | tf_op jit(solution)/shard_map/ppermute | solution.py:167
  30.2 0.8 %collective-permute-done.11.refs_1_ = bf16[2,128,256]{2,1,0:T(8,128)(2,1)S(1)} collective-permute-done((bf16[2,128,256]{2,1,0:T(8,128)(2,1)S(1)}, bf16[2,128,256]{2,1,0:T(8,128)(2,1)S(1)}, u32[]{:S(2)}, u32[]{:S(2)}) %collective-permute-start.11) | collective-permute-done | bytes 131104 | tf_op jit(solution)/shard_map/ppermute | solution.py:167
  31.1 1.5 %collective-permute-done.14.refs_4_.refs_2_ = bf16[64,256]{1,0:T(8,128)(2,1)S(1)} collective-permute-done((bf16[64,256]{1,0:T(8,128)(2,1)S(1)}, bf16[64,256]{1,0:T(8,128)(2,1)S(1)}, u32[]{:S(2)}, u32[]{:S(2)}) %collective-permute-start.14) | collective-permute-done | bytes 32800 | tf_op jit(solution)/shard_map/ppermute | solution.py:167
  32.6 0.0 collective-permute-done.13.refs_3_
  32.6 1.0 %collective-permute-done.12.refs_2_ = bf16[64,256]{1,0:T(8,128)(2,1)S(1)} collective-permute-done((bf16[64,256]{1,0:T(8,128)(2,1)S(1)}, bf16[64,256]{1,0:T(8,128)(2,1)S(1)}, u32[]{:S(2)}, u32[]{:S(2)}) %collective-permute-start.12) | collective-permute-done | bytes 32800 | tf_op jit(solution)/shard_map/ppermute | solution.py:167
  33.6 1.3 %collective-permute-start.15 = (bf16[192,256]{1,0:T(8,128)(2,1)S(1)}, bf16[192,256]{1,0:T(8,128)(2,1)S(1)}, u32[]{:S(2)}, u32[]{:S(2)}) collective-permute-start(bf16[192,256]{1,0:T(8,128)(2,1)S(1)} %grad_near.1.held_ref), channel_id=1, source_target_pairs={{0,16},{4,20},{8,24},{12,28},{16,0},{20,4},{24,8},{28,12},{1,17},{... | collective-permute-start | bytes 294920 | tf_op jit(solution)/shard_map/ppermute | solution.py:167
  35.0 0.0 copy-start.1
  35.0 0.9 %collective-permute-start.16 = (bf16[128,256]{1,0:T(8,128)(2,1)S(1)}, bf16[128,256]{1,0:T(8,128)(2,1)S(1)}, u32[]{:S(2)}, u32[]{:S(2)}) collective-permute-start(bf16[128,256]{1,0:T(8,128)(2,1)S(1)} %get-tuple-element.39), channel_id=1, source_target_pairs={{0,2},{1,3},{2,0},{3,1},{4,6},{5,7},{6,4},{7,5},{8,10},{9,11},{10,... | collective-permute-start | bytes 196616 | tf_op jit(solution)/shard_map/ppermute | solution.py:167
  35.9 0.0 collective-permute-start.17
  35.9 4.3 %collective-permute-done.15.far_ref.got_ref = bf16[192,256]{1,0:T(8,128)(2,1)S(1)} collective-permute-done((bf16[192,256]{1,0:T(8,128)(2,1)S(1)}, bf16[192,256]{1,0:T(8,128)(2,1)S(1)}, u32[]{:S(2)}, u32[]{:S(2)}) %collective-permute-start.15) | collective-permute-done | bytes 98336 | tf_op jit(solution)/shard_map/ppermute | solution.py:167
  40.3 0.1 collective-permute-start.20
  40.3 1.3 %collective-permute-start.19 = (bf16[64,256]{1,0:T(8,128)(2,1)S(1)}, bf16[64,256]{1,0:T(8,128)(2,1)S(1)}, u32[]{:S(2)}, u32[]{:S(2)}) collective-permute-start(bf16[64,256]{1,0:T(8,128)(2,1)S(1)} %grad_row.1.refs_0_), channel_id=1, source_target_pairs={{0,2},{1,3},{2,0},{3,1},{4,6},{5,7},{6,4},{7,5},{8,10},{9,11},{10,... | collective-permute-start | bytes 98312 | tf_op jit(solution)/shard_map/ppermute | solution.py:167
  41.6 0.6 %collective-permute-start.18 = (bf16[64,256]{1,0:T(8,128)(2,1)S(1)}, bf16[64,256]{1,0:T(8,128)(2,1)S(1)}, u32[]{:S(2)}, u32[]{:S(2)}) collective-permute-start(bf16[64,256]{1,0:T(8,128)(2,1)S(1)} %grad_row.1.refs_0_), channel_id=1, source_target_pairs={{0,1},{1,0},{2,3},{3,2},{4,5},{5,4},{6,7},{7,6},{8,9},{9,8},{10,11... | collective-permute-start | bytes 98312 | tf_op jit(solution)/shard_map/ppermute | solution.py:167
  42.2 0.8 %outputs.1 = (bf16[128,256]{1,0:T(8,128)(2,1)}, bf16[128,256]{1,0:T(8,128)(2,1)}) custom-call(bf16[256,256]{1,0:T(8,128)(2,1)S(1)} %copy-done.1, bf16[128,256]{1,0:T(8,128)(2,1)S(1)} %bitcast.11, bf16[192,256]{1,0:T(8,128)(2,1)S(1)} %collective-permute-done.15.far_ref.got_ref, bf16[192,256]{1,0:T(8,128)(2,1)S(1)} %collective-permute-done.8.refs_3_.refs_0_.first_ref, ...), custom_call_target="tpu_custom_call" | custom-call | tf_op jit(solution)/shard_map/outputs/pallas_call | solution.py:186
  43.0 0.7 %collective-permute-done.20.refs_3_ = bf16[64,256]{1,0:T(8,128)(2,1)S(1)} collective-permute-done((bf16[64,256]{1,0:T(8,128)(2,1)S(1)}, bf16[64,256]{1,0:T(8,128)(2,1)S(1)}, u32[]{:S(2)}, u32[]{:S(2)}) %collective-permute-start.20) | collective-permute-done | bytes 32800 | tf_op jit(solution)/shard_map/ppermute | solution.py:167
  43.8 0.6 %collective-permute-done.19.refs_2_ = bf16[64,256]{1,0:T(8,128)(2,1)S(1)} collective-permute-done((bf16[64,256]{1,0:T(8,128)(2,1)S(1)}, bf16[64,256]{1,0:T(8,128)(2,1)S(1)}, u32[]{:S(2)}, u32[]{:S(2)}) %collective-permute-start.19) | collective-permute-done | bytes 32800 | tf_op jit(solution)/shard_map/ppermute | solution.py:167
  44.4 0.0 collective-permute-done.18.refs_1_
  44.4 0.7 %convert_multiply_fusion = f32[256,256]{1,0:T(8,128)} fusion(bf16[256,256]{1,0:T(8,128)(2,1)S(1)} %weight_grad.1), kind=kLoop, calls=%fused_computation | loop fusion | flops 131072 | bytes 393216 | tf_op jit(solution)/shard_map/mul | solution.py:285
  (20 shorter events, 0.2 us)
Async XLA Ops:
  0.6 8.8 %collective-permute-start.4 = (bf16[128,256]{1,0:T(8,128)(2,1)}, bf16[128,256]{1,0:T(8,128)(2,1)S(1)}, u32[]{:S(2)}, u32[]{:S(2)}) collective-permute-start(bf16[128,256]{1,0:T(8,128)(2,1)} %bitcast.14), channel_id=1, source_target_pairs={{0,16},{4,20},{8,24},{12,28},{16,0},{20,4},{24,8},{28,12},{1,17},{... | collective-permute-start | bytes 196616 | tf_op jit(solution)/shard_map/ppermute | solution.py:167
  4.7 4.6 %collective-permute-start = (bf16[128,256]{1,0:T(8,128)(2,1)}, bf16[128,256]{1,0:T(8,128)(2,1)S(1)}, u32[]{:S(2)}, u32[]{:S(2)}) collective-permute-start(bf16[128,256]{1,0:T(8,128)(2,1)} %bitcast.12), channel_id=1, source_target_pairs={{0,2},{1,3},{2,0},{3,1},{4,6},{5,7},{6,4},{7,5},{8,10},{9,11},{10,... | collective-permute-start | bytes 196616 | tf_op jit(solution)/shard_map/ppermute | solution.py:167
  6.9 0.7 %copy-start.4 = (s32[1,1,32]{2,1,0:T(1,128)S(1)}, s32[1,1,32]{2,1,0:T(1,128)}, u32[]{:S(2)}) copy-start(s32[1,1,32]{2,1,0:T(1,128)} %param.9) | copy-start | bytes 388
  7.6 0.8 %copy-start.2 = (bf16[1,128,256]{2,1,0:T(8,128)(2,1)S(1)}, bf16[1,128,256]{2,1,0:T(8,128)(2,1)}, u32[]{:S(2)}) copy-start(bf16[1,128,256]{2,1,0:T(8,128)(2,1)} %param.11) | copy-start | bytes 196612
  8.5 0.8 %copy-start.3 = (bf16[1,128,256]{2,1,0:T(8,128)(2,1)S(1)}, bf16[1,128,256]{2,1,0:T(8,128)(2,1)}, u32[]{:S(2)}) copy-start(bf16[1,128,256]{2,1,0:T(8,128)(2,1)} %param.6) | copy-start | bytes 196612
  9.4 4.8 %collective-permute-start.1 = (bf16[2,128,256]{2,1,0:T(8,128)(2,1)S(1)}, bf16[2,128,256]{2,1,0:T(8,128)(2,1)S(1)}, u32[]{:S(2)}, u32[]{:S(2)}) collective-permute-start(bf16[2,128,256]{2,1,0:T(8,128)(2,1)S(1)} %cot_near.1.near_ref.refs_1_), channel_id=1, source_target_pairs={{0,1},{1,0},{2,3},{3,2},{4,5},{5,4},{6,7},{7,6},{8,9},{9,8},{10,11... | collective-permute-start | bytes 393224 | tf_op jit(solution)/shard_map/ppermute | solution.py:167
  9.4 3.6 %copy-start = (bf16[1,1,32,128,128]{4,3,2,1,0:T(8,128)(2,1)S(1)}, bf16[1,1,32,128,128]{4,3,2,1,0:T(8,128)(2,1)}, u32[]{:S(2)}) copy-start(bf16[1,1,32,128,128]{4,3,2,1,0:T(8,128)(2,1)} %param.8) | copy-start | bytes 3145732
  9.5 7.4 %collective-permute-start.7 = (bf16[2,128,256]{2,1,0:T(8,128)(2,1)S(1)}, bf16[2,128,256]{2,1,0:T(8,128)(2,1)S(1)}, u32[]{:S(2)}, u32[]{:S(2)}) collective-permute-start(bf16[2,128,256]{2,1,0:T(8,128)(2,1)S(1)} %pair.1.refs_3_), channel_id=1, source_target_pairs={{0,12},{4,8},{8,4},{12,0},{16,28},{20,24},{24,20},{28,16},{1,13},{... | collective-permute-start | bytes 393224 | tf_op jit(solution)/shard_map/ppermute | solution.py:167
  12.0 7.1 %collective-permute-start.6 = (bf16[2,128,256]{2,1,0:T(8,128)(2,1)S(1)}, bf16[2,128,256]{2,1,0:T(8,128)(2,1)S(1)}, u32[]{:S(2)}, u32[]{:S(2)}) collective-permute-start(bf16[2,128,256]{2,1,0:T(8,128)(2,1)S(1)} %pair.1.refs_3_), channel_id=1, source_target_pairs={{0,8},{4,12},{8,0},{12,4},{16,24},{20,28},{24,16},{28,20},{1,9},{5... | collective-permute-start | bytes 393224 | tf_op jit(solution)/shard_map/ppermute | solution.py:167
  12.5 6.7 %collective-permute-start.5 = (bf16[2,128,256]{2,1,0:T(8,128)(2,1)S(1)}, bf16[2,128,256]{2,1,0:T(8,128)(2,1)S(1)}, u32[]{:S(2)}, u32[]{:S(2)}) collective-permute-start(bf16[2,128,256]{2,1,0:T(8,128)(2,1)S(1)} %pair.1.refs_3_), channel_id=1, source_target_pairs={{0,4},{4,0},{8,12},{12,8},{16,20},{20,16},{24,28},{28,24},{1,5},{5... | collective-permute-start | bytes 393224 | tf_op jit(solution)/shard_map/ppermute | solution.py:167
  14.8 10.2 %collective-permute-start.2 = (bf16[2,128,256]{2,1,0:T(8,128)(2,1)S(1)}, bf16[2,128,256]{2,1,0:T(8,128)(2,1)S(1)}, u32[]{:S(2)}, u32[]{:S(2)}) collective-permute-start(bf16[2,128,256]{2,1,0:T(8,128)(2,1)S(1)} %get-tuple-element.25), channel_id=1, source_target_pairs={{0,4},{4,0},{8,12},{12,8},{16,20},{20,16},{24,28},{28,24},{1,5},{5... | collective-permute-start | bytes 393224 | tf_op jit(solution)/shard_map/ppermute | solution.py:167
  16.2 8.7 %collective-permute-start.3 = (bf16[2,128,256]{2,1,0:T(8,128)(2,1)S(1)}, bf16[2,128,256]{2,1,0:T(8,128)(2,1)S(1)}, u32[]{:S(2)}, u32[]{:S(2)}) collective-permute-start(bf16[2,128,256]{2,1,0:T(8,128)(2,1)S(1)} %get-tuple-element.26), channel_id=1, source_target_pairs={{0,4},{4,0},{8,12},{12,8},{16,20},{20,16},{24,28},{28,24},{1,5},{5... | collective-permute-start | bytes 393224 | tf_op jit(solution)/shard_map/ppermute | solution.py:167
  20.0 4.9 %collective-permute-start.8 = (bf16[192,256]{1,0:T(8,128)(2,1)S(1)}, bf16[192,256]{1,0:T(8,128)(2,1)S(1)}, u32[]{:S(2)}, u32[]{:S(2)}) collective-permute-start(bf16[192,256]{1,0:T(8,128)(2,1)S(1)} %get-tuple-element.28), channel_id=1, source_target_pairs={{0,1},{1,0},{2,3},{3,2},{4,5},{5,4},{6,7},{7,6},{8,9},{9,8},{10,11... | collective-permute-start | bytes 294920 | tf_op jit(solution)/shard_map/ppermute | solution.py:167
  20.1 4.0 %collective-permute-start.9 = (bf16[64,256]{1,0:T(8,128)(2,1)S(1)}, bf16[64,256]{1,0:T(8,128)(2,1)S(1)}, u32[]{:S(2)}, u32[]{:S(2)}) collective-permute-start(bf16[64,256]{1,0:T(8,128)(2,1)S(1)} %get-tuple-element.29), channel_id=1, source_target_pairs={{0,2},{1,3},{2,0},{3,1},{4,6},{5,7},{6,4},{7,5},{8,10},{9,11},{10,... | collective-permute-start | bytes 98312 | tf_op jit(solution)/shard_map/ppermute | solution.py:167
  21.6 3.3 %collective-permute-start.10 = (bf16[64,256]{1,0:T(8,128)(2,1)S(1)}, bf16[64,256]{1,0:T(8,128)(2,1)S(1)}, u32[]{:S(2)}, u32[]{:S(2)}) collective-permute-start(bf16[64,256]{1,0:T(8,128)(2,1)S(1)} %get-tuple-element.30), channel_id=1, source_target_pairs={{0,3},{1,2},{2,1},{3,0},{4,7},{5,6},{6,5},{7,4},{8,11},{9,10},{10,... | collective-permute-start | bytes 98312 | tf_op jit(solution)/shard_map/ppermute | solution.py:167
  25.0 6.1 %collective-permute-start.11 = (bf16[2,128,256]{2,1,0:T(8,128)(2,1)S(1)}, bf16[2,128,256]{2,1,0:T(8,128)(2,1)S(1)}, u32[]{:S(2)}, u32[]{:S(2)}) collective-permute-start(bf16[2,128,256]{2,1,0:T(8,128)(2,1)S(1)} %get-tuple-element.32), channel_id=1, source_target_pairs={{0,8},{4,12},{8,0},{12,4},{16,24},{20,28},{24,16},{28,20},{1,9},{5... | collective-permute-start | bytes 393224 | tf_op jit(solution)/shard_map/ppermute | solution.py:167
  26.6 5.9 %collective-permute-start.14 = (bf16[64,256]{1,0:T(8,128)(2,1)S(1)}, bf16[64,256]{1,0:T(8,128)(2,1)S(1)}, u32[]{:S(2)}, u32[]{:S(2)}) collective-permute-start(bf16[64,256]{1,0:T(8,128)(2,1)S(1)} %grad_col.1.refs_1_), channel_id=1, source_target_pairs={{0,12},{4,8},{8,4},{12,0},{16,28},{20,24},{24,20},{28,16},{1,13},{... | collective-permute-start | bytes 98312 | tf_op jit(solution)/shard_map/ppermute | solution.py:167
  28.1 4.5 %collective-permute-start.13 = (bf16[64,256]{1,0:T(8,128)(2,1)S(1)}, bf16[64,256]{1,0:T(8,128)(2,1)S(1)}, u32[]{:S(2)}, u32[]{:S(2)}) collective-permute-start(bf16[64,256]{1,0:T(8,128)(2,1)S(1)} %grad_col.1.refs_1_), channel_id=1, source_target_pairs={{0,8},{4,12},{8,0},{12,4},{16,24},{20,28},{24,16},{28,20},{1,9},{5... | collective-permute-start | bytes 98312 | tf_op jit(solution)/shard_map/ppermute | solution.py:167
  29.7 3.9 %collective-permute-start.12 = (bf16[64,256]{1,0:T(8,128)(2,1)S(1)}, bf16[64,256]{1,0:T(8,128)(2,1)S(1)}, u32[]{:S(2)}, u32[]{:S(2)}) collective-permute-start(bf16[64,256]{1,0:T(8,128)(2,1)S(1)} %grad_col.1.refs_1_), channel_id=1, source_target_pairs={{0,4},{4,0},{8,12},{12,8},{16,20},{20,16},{24,28},{28,24},{1,5},{5... | collective-permute-start | bytes 98312 | tf_op jit(solution)/shard_map/ppermute | solution.py:167
  33.6 6.6 %collective-permute-start.15 = (bf16[192,256]{1,0:T(8,128)(2,1)S(1)}, bf16[192,256]{1,0:T(8,128)(2,1)S(1)}, u32[]{:S(2)}, u32[]{:S(2)}) collective-permute-start(bf16[192,256]{1,0:T(8,128)(2,1)S(1)} %grad_near.1.held_ref), channel_id=1, source_target_pairs={{0,16},{4,20},{8,24},{12,28},{16,0},{20,4},{24,8},{28,12},{1,17},{... | collective-permute-start | bytes 294920 | tf_op jit(solution)/shard_map/ppermute | solution.py:167
  35.0 7.2 %copy-start.1 = (bf16[256,256]{1,0:T(8,128)(2,1)S(1)}, bf16[256,256]{1,0:T(8,128)(2,1)}, u32[]{:S(2)}) copy-start(bf16[256,256]{1,0:T(8,128)(2,1)} %weight_ref.1) | copy-start | bytes 393220
  35.0 7.2 %collective-permute-start.16 = (bf16[128,256]{1,0:T(8,128)(2,1)S(1)}, bf16[128,256]{1,0:T(8,128)(2,1)S(1)}, u32[]{:S(2)}, u32[]{:S(2)}) collective-permute-start(bf16[128,256]{1,0:T(8,128)(2,1)S(1)} %get-tuple-element.39), channel_id=1, source_target_pairs={{0,2},{1,3},{2,0},{3,1},{4,6},{5,7},{6,4},{7,5},{8,10},{9,11},{10,... | collective-permute-start | bytes 196616 | tf_op jit(solution)/shard_map/ppermute | solution.py:167
  35.9 6.3 %collective-permute-start.17 = (bf16[128,256]{1,0:T(8,128)(2,1)S(1)}, bf16[128,256]{1,0:T(8,128)(2,1)S(1)}, u32[]{:S(2)}, u32[]{:S(2)}) collective-permute-start(bf16[128,256]{1,0:T(8,128)(2,1)S(1)} %get-tuple-element.40), channel_id=1, source_target_pairs={{0,3},{1,2},{2,1},{3,0},{4,7},{5,6},{6,5},{7,4},{8,11},{9,10},{10,... | collective-permute-start | bytes 196616 | tf_op jit(solution)/shard_map/ppermute | solution.py:167
  40.3 3.5 %collective-permute-start.20 = (bf16[64,256]{1,0:T(8,128)(2,1)S(1)}, bf16[64,256]{1,0:T(8,128)(2,1)S(1)}, u32[]{:S(2)}, u32[]{:S(2)}) collective-permute-start(bf16[64,256]{1,0:T(8,128)(2,1)S(1)} %grad_row.1.refs_0_), channel_id=1, source_target_pairs={{0,3},{1,2},{2,1},{3,0},{4,7},{5,6},{6,5},{7,4},{8,11},{9,10},{10,... | collective-permute-start | bytes 98312 | tf_op jit(solution)/shard_map/ppermute | solution.py:167
  40.3 4.0 %collective-permute-start.19 = (bf16[64,256]{1,0:T(8,128)(2,1)S(1)}, bf16[64,256]{1,0:T(8,128)(2,1)S(1)}, u32[]{:S(2)}, u32[]{:S(2)}) collective-permute-start(bf16[64,256]{1,0:T(8,128)(2,1)S(1)} %grad_row.1.refs_0_), channel_id=1, source_target_pairs={{0,2},{1,3},{2,0},{3,1},{4,6},{5,7},{6,4},{7,5},{8,10},{9,11},{10,... | collective-permute-start | bytes 98312 | tf_op jit(solution)/shard_map/ppermute | solution.py:167
  41.6 2.8 %collective-permute-start.18 = (bf16[64,256]{1,0:T(8,128)(2,1)S(1)}, bf16[64,256]{1,0:T(8,128)(2,1)S(1)}, u32[]{:S(2)}, u32[]{:S(2)}) collective-permute-start(bf16[64,256]{1,0:T(8,128)(2,1)S(1)} %grad_row.1.refs_0_), channel_id=1, source_target_pairs={{0,1},{1,0},{2,3},{3,2},{4,5},{5,4},{6,7},{7,6},{8,9},{9,8},{10,11... | collective-permute-start | bytes 98312 | tf_op jit(solution)/shard_map/ppermute | solution.py:167

commit v6 on v3

--- a/solution.py
+++ b/solution.py
@@ -35,14 +35,14 @@
     return total
 
 
-def dense_kernel(meta_ref, tiles_ref, adj_ref, sems):
+def dense_kernel(slots_ref, count_ref, tiles_ref, adj_ref, sems):
     slot_count, tile, _ = tiles_ref.shape
     col_tiles = adj_ref.shape[1] // tile
-    live = jnp.minimum(meta_ref[0], slot_count)
+    live = jnp.minimum(count_ref[0], slot_count)
     adj_ref[...] = jnp.zeros_like(adj_ref)
 
     def copy(k):
-        slot = meta_ref[1 + k]
+        slot = slots_ref[k]
         row = pl.multiple_of((slot // col_tiles) * tile, tile)
         col = pl.multiple_of((slot % col_tiles) * tile, tile)
         place = adj_ref.at[pl.ds(row, tile), pl.ds(col, tile)]
@@ -177,7 +177,6 @@
     slab, width = features.shape[1:]
     rows, cols = col_devices * slab, row_devices * slab
     piece = width // col_devices
-    live = jnp.concatenate([tile_counts[0], tile_slots[0, 0]])
 
     def call(kernel, name, out_shape, in_specs, args, scratch=(), micros=None):
         many = isinstance(out_shape, list)
@@ -197,7 +196,8 @@
     own = features[0]
     far = swap(own, "row", half)
     adj = call(
-        dense_kernel, "dense", shape(rows, cols), [SMEM, ANY], (live, tile_values[0, 0]),
+        dense_kernel, "dense", shape(rows, cols), [SMEM, SMEM, ANY],
+        (tile_slots[0, 0], tile_counts[0], tile_values[0, 0]),
         scratch=[pltpu.SemaphoreType.DMA((slots,))],
     )
 
@@ -213,7 +213,7 @@
             [VMEM] * len(arrays) + [ANY] * len(after), (*arrays, *after), micros=3,
         )
 
-    kept = hold([own, cotangent[0]], live, "own")
+    kept = hold([own, cotangent[0]], tile_counts, "own")
     pair = stack([kept[0], far], "pair")
     features_got = exchange([pair] * half, "row")
     cot_near = stack(

time: 43.2 us -> 42.8 us (level); the launches traced: 43 us -> 43.5 us
  waiting for transfers between devices: 11.3 us -> 13.4 us
  starting transfers between devices: 23.8 us -> 22.2 us
    ppermute x21, waiting for transfers between devices: 11.3 us -> 13.4 us  [swap(): return lax.ppermute(array, axis, pairs)]
    ppermute x21, starting transfers between devices: 23.8 us -> 22.2 us  [swap(): return lax.ppermute(array, axis, pairs)]
  transfers between devices with their start and end apart: 21 -> 21, of which waited for: 11 -> 10; matrix products, arithmetic and copies ran while one was open for 0% -> 0% of each run, Pallas kernels for 8% -> 8%
where the time goes in v6:
time: 42.8 us; the launch traced here: 43.5 us
  starting transfers between devices  22.2 us (52%)
  waiting for transfers between devices  13.4 us (31%)
  Pallas kernels  3.37 us (8%)
  local copies, waits for them, and re-layouts  2.33 us (5%)
  between operations  1.44 us (3%)
  other arithmetic  0.72 us (2%)
    ppermute x21, starting transfers between devices, swap(): return lax.ppermute(array, axis, pairs)  22.2 us
    ppermute x21, waiting for transfers between devices, swap(): return lax.ppermute(array, axis, pairs)  13.4 us
    pallas_call x13, Pallas kernels, call(): pl.pallas_call(kernel, out_shape=out_shape, in_specs=in_specs, out_specs=...  3.37 us
    unnamed x10, local copies, waits for them, and re-layouts  2.33 us
  transfers between devices with their start and end apart: 21, of which 10 were waited for; matrix products, arithmetic and copies ran while one was open for 0% of the time, Pallas kernels for 8%

profile of v6, /device:TPU:0, one launch (start us, length us, event | category | flops | bytes accessed | tf_op | source)
XLA Modules:
  0.0 43.5 jit_solution(3415997678274214771)
XLA Ops:
  0.6 3.0 %collective-permute-start = (bf16[128,256]{1,0:T(8,128)(2,1)}, bf16[128,256]{1,0:T(8,128)(2,1)S(1)}, u32[]{:S(2)}, u32[]{:S(2)}) collective-permute-start(bf16[128,256]{1,0:T(8,128)(2,1)} %bitcast.9), channel_id=1, source_target_pairs={{0,2},{1,3},{2,0},{3,1},{4,6},{5,7},{6,4},{7,5},{8,10},{9,11},{10,... | collective-permute-start | bytes 196616 | tf_op jit(solution)/shard_map/ppermute | solution.py:165
  3.7 2.6 %collective-permute-start.5 = (bf16[128,256]{1,0:T(8,128)(2,1)}, bf16[128,256]{1,0:T(8,128)(2,1)S(1)}, u32[]{:S(2)}, u32[]{:S(2)}) collective-permute-start(bf16[128,256]{1,0:T(8,128)(2,1)} %bitcast.11), channel_id=1, source_target_pairs={{0,16},{4,20},{8,24},{12,28},{16,0},{20,4},{24,8},{28,12},{1,17},{... | collective-permute-start | bytes 196616 | tf_op jit(solution)/shard_map/ppermute | solution.py:165
  6.9 0.8 %copy-done.2 = bf16[1,128,256]{2,1,0:T(8,128)(2,1)S(1)} copy-done((bf16[1,128,256]{2,1,0:T(8,128)(2,1)S(1)}, bf16[1,128,256]{2,1,0:T(8,128)(2,1)}, u32[]{:S(2)}) %copy-start.2) | copy-done | bytes 65560
  7.7 0.8 %copy-done.3 = bf16[1,128,256]{2,1,0:T(8,128)(2,1)S(1)} copy-done((bf16[1,128,256]{2,1,0:T(8,128)(2,1)S(1)}, bf16[1,128,256]{2,1,0:T(8,128)(2,1)}, u32[]{:S(2)}) %copy-start.3) | copy-done | bytes 65560
  8.6 0.1 collective-permute-start.1
  8.7 0.6 %collective-permute-done.5.refs_1_ = bf16[128,256]{1,0:T(8,128)(2,1)S(1)} collective-permute-done((bf16[128,256]{1,0:T(8,128)(2,1)}, bf16[128,256]{1,0:T(8,128)(2,1)S(1)}, u32[]{:S(2)}, u32[]{:S(2)}) %collective-permute-start.5) | collective-permute-done | bytes 65568 | tf_op jit(solution)/shard_map/ppermute | solution.py:165
  9.4 2.3 %collective-permute-start.8 = (bf16[2,128,256]{2,1,0:T(8,128)(2,1)S(1)}, bf16[2,128,256]{2,1,0:T(8,128)(2,1)S(1)}, u32[]{:S(2)}, u32[]{:S(2)}) collective-permute-start(bf16[2,128,256]{2,1,0:T(8,128)(2,1)S(1)} %pair.1.refs_3_), channel_id=1, source_target_pairs={{0,12},{4,8},{8,4},{12,0},{16,28},{20,24},{24,20},{28,16},{1,13},{... | collective-permute-start | bytes 393224 | tf_op jit(solution)/shard_map/ppermute | solution.py:165
  11.6 0.7 %collective-permute-start.7 = (bf16[2,128,256]{2,1,0:T(8,128)(2,1)S(1)}, bf16[2,128,256]{2,1,0:T(8,128)(2,1)S(1)}, u32[]{:S(2)}, u32[]{:S(2)}) collective-permute-start(bf16[2,128,256]{2,1,0:T(8,128)(2,1)S(1)} %pair.1.refs_3_), channel_id=1, source_target_pairs={{0,8},{4,12},{8,0},{12,4},{16,24},{20,28},{24,16},{28,20},{1,9},{5... | collective-permute-start | bytes 393224 | tf_op jit(solution)/shard_map/ppermute | solution.py:165
  12.4 0.5 %collective-permute-start.6 = (bf16[2,128,256]{2,1,0:T(8,128)(2,1)S(1)}, bf16[2,128,256]{2,1,0:T(8,128)(2,1)S(1)}, u32[]{:S(2)}, u32[]{:S(2)}) collective-permute-start(bf16[2,128,256]{2,1,0:T(8,128)(2,1)S(1)} %pair.1.refs_3_), channel_id=1, source_target_pairs={{0,4},{4,0},{8,12},{12,8},{16,20},{20,16},{24,28},{28,24},{1,5},{5... | collective-permute-start | bytes 393224 | tf_op jit(solution)/shard_map/ppermute | solution.py:165
  12.9 0.7 %copy-done.4 = s32[1,1,32]{2,1,0:T(1,128)S(1)} copy-done((s32[1,1,32]{2,1,0:T(1,128)S(1)}, s32[1,1,32]{2,1,0:T(1,128)}, u32[]{:S(2)}) %copy-start.4) | copy-done | bytes 152
  13.6 1.0 %dense.1.adj_ref.refs_0_ = bf16[512,1024]{1,0:T(8,128)(2,1)S(1)} custom-call(s32[32]{0:T(128)S(1)} %bitcast.13, s32[1]{0:T(128)} %bitcast.7.count_ref, bf16[32,128,128]{2,1,0:T(8,128)(2,1)S(1)} %bitcast.8), custom_call_target="tpu_custom_call" | custom-call | tf_op jit(solution)/shard_map/dense/pallas_call | solution.py:183
  14.6 0.0 collective-permute-done.1.other_ref.refs_2_
  14.6 0.6 %backward.1 = (bf16[2,128,256]{2,1,0:T(8,128)(2,1)S(1)}, bf16[2,128,256]{2,1,0:T(8,128)(2,1)S(1)}, bf16[2,128,256]{2,1,0:T(8,128)(2,1)S(1)}, bf16[2,128,256]{2,1,0:T(8,128)(2,1)S(1)}) custom-call(bf16[512,1024]{1,0:T(8,128)(2,1)S(1)} %dense.1.adj_ref.refs_0_, bf16[2,128,256]{2,1,0:T(8,128)(2,1)S(1)} %cot_near.1.near_ref.refs_1_, ...), custom_call_target="tpu_custom_call" | custom-call | tf_op jit(solution)/shard_map/backward/pallas_call | solution.py:183
  15.1 2.7 %collective-permute-start.2 = (bf16[2,128,256]{2,1,0:T(8,128)(2,1)S(1)}, bf16[2,128,256]{2,1,0:T(8,128)(2,1)S(1)}, u32[]{:S(2)}, u32[]{:S(2)}) collective-permute-start(bf16[2,128,256]{2,1,0:T(8,128)(2,1)S(1)} %get-tuple-element.23), channel_id=1, source_target_pairs={{0,12},{4,8},{8,4},{12,0},{16,28},{20,24},{24,20},{28,16},{1,13},{... | collective-permute-start | bytes 393224 | tf_op jit(solution)/shard_map/ppermute | solution.py:165
  17.9 1.0 %collective-permute-start.3 = (bf16[2,128,256]{2,1,0:T(8,128)(2,1)S(1)}, bf16[2,128,256]{2,1,0:T(8,128)(2,1)S(1)}, u32[]{:S(2)}, u32[]{:S(2)}) collective-permute-start(bf16[2,128,256]{2,1,0:T(8,128)(2,1)S(1)} %get-tuple-element.24), channel_id=1, source_target_pairs={{0,8},{4,12},{8,0},{12,4},{16,24},{20,28},{24,16},{28,20},{1,9},{5... | collective-permute-start | bytes 393224 | tf_op jit(solution)/shard_map/ppermute | solution.py:165
  18.9 0.0 collective-permute-done.8.refs_6_
  18.9 0.0 collective-permute-start.4
  18.9 0.2 collective-permute-done.7.refs_5_
  19.0 0.0 collective-permute-done.6.refs_4_
  19.0 0.8 %forward.1 = (bf16[128,256]{1,0:T(8,128)(2,1)S(1)}, bf16[128,256]{1,0:T(8,128)(2,1)S(1)}, bf16[128,256]{1,0:T(8,128)(2,1)S(1)}, bf16[64,256]{1,0:T(8,128)(2,1)S(...) custom-call(bf16[512,1024]{1,0:T(8,128)(2,1)S(1)} %dense.1.adj_ref.refs_0_, ...), custom_call_target="tpu_custom_call" | custom-call | tf_op jit(solution)/shard_map/forward/pallas_call | solution.py:183
  19.8 0.5 %collective-permute-start.10 = (bf16[64,256]{1,0:T(8,128)(2,1)S(1)}, bf16[64,256]{1,0:T(8,128)(2,1)S(1)}, u32[]{:S(2)}, u32[]{:S(2)}) collective-permute-start(bf16[64,256]{1,0:T(8,128)(2,1)S(1)} %get-tuple-element.32), channel_id=1, source_target_pairs={{0,2},{1,3},{2,0},{3,1},{4,6},{5,7},{6,4},{7,5},{8,10},{9,11},{10,... | collective-permute-start | bytes 98312 | tf_op jit(solution)/shard_map/ppermute | solution.py:165
  20.4 2.1 %collective-permute-done.2.refs_0_ = bf16[2,128,256]{2,1,0:T(8,128)(2,1)S(1)} collective-permute-done((bf16[2,128,256]{2,1,0:T(8,128)(2,1)S(1)}, bf16[2,128,256]{2,1,0:T(8,128)(2,1)S(1)}, u32[]{:S(2)}, u32[]{:S(2)}) %collective-permute-start.2) | collective-permute-done | bytes 131104 | tf_op jit(solution)/shard_map/ppermute | solution.py:165
  22.5 0.0 collective-permute-start.9
  22.5 1.5 %collective-permute-done.3.refs_1_ = bf16[2,128,256]{2,1,0:T(8,128)(2,1)S(1)} collective-permute-done((bf16[2,128,256]{2,1,0:T(8,128)(2,1)S(1)}, bf16[2,128,256]{2,1,0:T(8,128)(2,1)S(1)}, u32[]{:S(2)}, u32[]{:S(2)}) %collective-permute-start.3) | collective-permute-done | bytes 131104 | tf_op jit(solution)/shard_map/ppermute | solution.py:165
  24.0 0.0 collective-permute-done.4.refs_2_
  24.0 0.1 pair_sum.1
  24.1 0.0 collective-permute-done.10.refs_2_
  24.1 0.0 collective-permute-done.11.refs_3_
  24.2 2.6 %collective-permute-start.14 = (bf16[64,256]{1,0:T(8,128)(2,1)S(1)}, bf16[64,256]{1,0:T(8,128)(2,1)S(1)}, u32[]{:S(2)}, u32[]{:S(2)}) collective-permute-start(bf16[64,256]{1,0:T(8,128)(2,1)S(1)} %grad_col.1.refs_1_), channel_id=1, source_target_pairs={{0,12},{4,8},{8,4},{12,0},{16,28},{20,24},{24,20},{28,16},{1,13},{... | collective-permute-start | bytes 98312 | tf_op jit(solution)/shard_map/ppermute | solution.py:165
  26.8 1.1 %collective-permute-start.13 = (bf16[64,256]{1,0:T(8,128)(2,1)S(1)}, bf16[64,256]{1,0:T(8,128)(2,1)S(1)}, u32[]{:S(2)}, u32[]{:S(2)}) collective-permute-start(bf16[64,256]{1,0:T(8,128)(2,1)S(1)} %grad_col.1.refs_1_), channel_id=1, source_target_pairs={{0,8},{4,12},{8,0},{12,4},{16,24},{20,28},{24,16},{28,20},{1,9},{5... | collective-permute-start | bytes 98312 | tf_op jit(solution)/shard_map/ppermute | solution.py:165
  27.9 0.0 collective-permute-start.12
  27.9 1.1 %collective-permute-done.14.refs_4_.refs_2_ = bf16[64,256]{1,0:T(8,128)(2,1)S(1)} collective-permute-done((bf16[64,256]{1,0:T(8,128)(2,1)S(1)}, bf16[64,256]{1,0:T(8,128)(2,1)S(1)}, u32[]{:S(2)}, u32[]{:S(2)}) %collective-permute-start.14) | collective-permute-done | bytes 32800 | tf_op jit(solution)/shard_map/ppermute | solution.py:165
  29.1 1.7 %collective-permute-done.13.refs_3_ = bf16[64,256]{1,0:T(8,128)(2,1)S(1)} collective-permute-done((bf16[64,256]{1,0:T(8,128)(2,1)S(1)}, bf16[64,256]{1,0:T(8,128)(2,1)S(1)}, u32[]{:S(2)}, u32[]{:S(2)}) %collective-permute-start.13) | collective-permute-done | bytes 32800 | tf_op jit(solution)/shard_map/ppermute | solution.py:165
  30.7 1.1 %collective-permute-done.12.refs_2_ = bf16[64,256]{1,0:T(8,128)(2,1)S(1)} collective-permute-done((bf16[64,256]{1,0:T(8,128)(2,1)S(1)}, bf16[64,256]{1,0:T(8,128)(2,1)S(1)}, u32[]{:S(2)}, u32[]{:S(2)}) %collective-permute-start.12) | collective-permute-done | bytes 32800 | tf_op jit(solution)/shard_map/ppermute | solution.py:165
  31.9 1.7 %collective-permute-start.15 = (bf16[192,256]{1,0:T(8,128)(2,1)S(1)}, bf16[192,256]{1,0:T(8,128)(2,1)S(1)}, u32[]{:S(2)}, u32[]{:S(2)}) collective-permute-start(bf16[192,256]{1,0:T(8,128)(2,1)S(1)} %grad_near.1.held_ref), channel_id=1, source_target_pairs={{0,16},{4,20},{8,24},{12,28},{16,0},{20,4},{24,8},{28,12},{1,17},{... | collective-permute-start | bytes 294920 | tf_op jit(solution)/shard_map/ppermute | solution.py:165
  33.6 0.0 copy-start.1
  33.6 1.3 %collective-permute-start.16 = (bf16[128,256]{1,0:T(8,128)(2,1)S(1)}, bf16[128,256]{1,0:T(8,128)(2,1)S(1)}, u32[]{:S(2)}, u32[]{:S(2)}) collective-permute-start(bf16[128,256]{1,0:T(8,128)(2,1)S(1)} %get-tuple-element.37), channel_id=1, source_target_pairs={{0,2},{1,3},{2,0},{3,1},{4,6},{5,7},{6,4},{7,5},{8,10},{9,11},{10,... | collective-permute-start | bytes 196616 | tf_op jit(solution)/shard_map/ppermute | solution.py:165
  34.9 0.0 collective-permute-start.17
  34.9 3.6 %collective-permute-done.15.far_ref.got_ref = bf16[192,256]{1,0:T(8,128)(2,1)S(1)} collective-permute-done((bf16[192,256]{1,0:T(8,128)(2,1)S(1)}, bf16[192,256]{1,0:T(8,128)(2,1)S(1)}, u32[]{:S(2)}, u32[]{:S(2)}) %collective-permute-start.15) | collective-permute-done | bytes 98336 | tf_op jit(solution)/shard_map/ppermute | solution.py:165
  38.5 0.1 collective-permute-start.20
  38.6 1.2 %collective-permute-start.19 = (bf16[64,256]{1,0:T(8,128)(2,1)S(1)}, bf16[64,256]{1,0:T(8,128)(2,1)S(1)}, u32[]{:S(2)}, u32[]{:S(2)}) collective-permute-start(bf16[64,256]{1,0:T(8,128)(2,1)S(1)} %grad_row.1.refs_0_), channel_id=1, source_target_pairs={{0,2},{1,3},{2,0},{3,1},{4,6},{5,7},{6,4},{7,5},{8,10},{9,11},{10,... | collective-permute-start | bytes 98312 | tf_op jit(solution)/shard_map/ppermute | solution.py:165
  39.8 0.7 %collective-permute-start.18 = (bf16[64,256]{1,0:T(8,128)(2,1)S(1)}, bf16[64,256]{1,0:T(8,128)(2,1)S(1)}, u32[]{:S(2)}, u32[]{:S(2)}) collective-permute-start(bf16[64,256]{1,0:T(8,128)(2,1)S(1)} %grad_row.1.refs_0_), channel_id=1, source_target_pairs={{0,1},{1,0},{2,3},{3,2},{4,5},{5,4},{6,7},{7,6},{8,9},{9,8},{10,11... | collective-permute-start | bytes 98312 | tf_op jit(solution)/shard_map/ppermute | solution.py:165
  40.4 0.0 collective-permute-done.16.refs_1_
  40.4 0.0 collective-permute-done.17.refs_2_
  40.5 0.8 %outputs.1 = (bf16[128,256]{1,0:T(8,128)(2,1)}, bf16[128,256]{1,0:T(8,128)(2,1)}) custom-call(bf16[256,256]{1,0:T(8,128)(2,1)S(1)} %copy-done.1, f32[128,256]{1,0:T(8,128)S(1)} %get-tuple-element.27.keep_ref, bf16[192,256]{1,0:T(8,128)(2,1)S(1)} %collective-permute-done.15.far_ref.got_ref, bf16[192,256]{1,0:T(8,128)(2,1)S(1)} %collective-permute-done.9.refs_0_.first_ref, ...), custom_call_target="tpu_custom_call" | custom-call | tf_op jit(solution)/shard_map/outputs/pallas_call | solution.py:183
  41.3 0.6 %collective-permute-done.20.refs_3_ = bf16[64,256]{1,0:T(8,128)(2,1)S(1)} collective-permute-done((bf16[64,256]{1,0:T(8,128)(2,1)S(1)}, bf16[64,256]{1,0:T(8,128)(2,1)S(1)}, u32[]{:S(2)}, u32[]{:S(2)}) %collective-permute-start.20) | collective-permute-done | bytes 32800 | tf_op jit(solution)/shard_map/ppermute | solution.py:165
  41.9 0.8 %collective-permute-done.19.refs_2_ = bf16[64,256]{1,0:T(8,128)(2,1)S(1)} collective-permute-done((bf16[64,256]{1,0:T(8,128)(2,1)S(1)}, bf16[64,256]{1,0:T(8,128)(2,1)S(1)}, u32[]{:S(2)}, u32[]{:S(2)}) %collective-permute-start.19) | collective-permute-done | bytes 32800 | tf_op jit(solution)/shard_map/ppermute | solution.py:165
  42.8 0.7 %convert_multiply_fusion = f32[256,256]{1,0:T(8,128)} fusion(bf16[256,256]{1,0:T(8,128)(2,1)S(1)} %weight_grad.1), kind=kLoop, calls=%fused_computation | loop fusion | flops 131072 | bytes 393216 | tf_op jit(solution)/shard_map/mul | solution.py:274
  (18 shorter events, 0.1 us)
Async XLA Ops:
  0.6 8.0 %collective-permute-start = (bf16[128,256]{1,0:T(8,128)(2,1)}, bf16[128,256]{1,0:T(8,128)(2,1)S(1)}, u32[]{:S(2)}, u32[]{:S(2)}) collective-permute-start(bf16[128,256]{1,0:T(8,128)(2,1)} %bitcast.9), channel_id=1, source_target_pairs={{0,2},{1,3},{2,0},{3,1},{4,6},{5,7},{6,4},{7,5},{8,10},{9,11},{10,... | collective-permute-start | bytes 196616 | tf_op jit(solution)/shard_map/ppermute | solution.py:165
  3.7 5.7 %collective-permute-start.5 = (bf16[128,256]{1,0:T(8,128)(2,1)}, bf16[128,256]{1,0:T(8,128)(2,1)S(1)}, u32[]{:S(2)}, u32[]{:S(2)}) collective-permute-start(bf16[128,256]{1,0:T(8,128)(2,1)} %bitcast.11), channel_id=1, source_target_pairs={{0,16},{4,20},{8,24},{12,28},{16,0},{20,4},{24,8},{28,12},{1,17},{... | collective-permute-start | bytes 196616 | tf_op jit(solution)/shard_map/ppermute | solution.py:165
  6.9 0.8 %copy-start.2 = (bf16[1,128,256]{2,1,0:T(8,128)(2,1)S(1)}, bf16[1,128,256]{2,1,0:T(8,128)(2,1)}, u32[]{:S(2)}) copy-start(bf16[1,128,256]{2,1,0:T(8,128)(2,1)} %param.11) | copy-start | bytes 196612
  7.7 0.8 %copy-start.3 = (bf16[1,128,256]{2,1,0:T(8,128)(2,1)S(1)}, bf16[1,128,256]{2,1,0:T(8,128)(2,1)}, u32[]{:S(2)}) copy-start(bf16[1,128,256]{2,1,0:T(8,128)(2,1)} %param.6) | copy-start | bytes 196612
  8.6 5.9 %collective-permute-start.1 = (bf16[2,128,256]{2,1,0:T(8,128)(2,1)S(1)}, bf16[2,128,256]{2,1,0:T(8,128)(2,1)S(1)}, u32[]{:S(2)}, u32[]{:S(2)}) collective-permute-start(bf16[2,128,256]{2,1,0:T(8,128)(2,1)S(1)} %cot_near.1.near_ref.refs_1_), channel_id=1, source_target_pairs={{0,1},{1,0},{2,3},{3,2},{4,5},{5,4},{6,7},{7,6},{8,9},{9,8},{10,11... | collective-permute-start | bytes 393224 | tf_op jit(solution)/shard_map/ppermute | solution.py:165
  9.3 3.6 %copy-start = (bf16[1,1,32,128,128]{4,3,2,1,0:T(8,128)(2,1)S(1)}, bf16[1,1,32,128,128]{4,3,2,1,0:T(8,128)(2,1)}, u32[]{:S(2)}) copy-start(bf16[1,1,32,128,128]{4,3,2,1,0:T(8,128)(2,1)} %param.8) | copy-start | bytes 3145732
  9.4 9.5 %collective-permute-start.8 = (bf16[2,128,256]{2,1,0:T(8,128)(2,1)S(1)}, bf16[2,128,256]{2,1,0:T(8,128)(2,1)S(1)}, u32[]{:S(2)}, u32[]{:S(2)}) collective-permute-start(bf16[2,128,256]{2,1,0:T(8,128)(2,1)S(1)} %pair.1.refs_3_), channel_id=1, source_target_pairs={{0,12},{4,8},{8,4},{12,0},{16,28},{20,24},{24,20},{28,16},{1,13},{... | collective-permute-start | bytes 393224 | tf_op jit(solution)/shard_map/ppermute | solution.py:165
  11.6 7.4 %collective-permute-start.7 = (bf16[2,128,256]{2,1,0:T(8,128)(2,1)S(1)}, bf16[2,128,256]{2,1,0:T(8,128)(2,1)S(1)}, u32[]{:S(2)}, u32[]{:S(2)}) collective-permute-start(bf16[2,128,256]{2,1,0:T(8,128)(2,1)S(1)} %pair.1.refs_3_), channel_id=1, source_target_pairs={{0,8},{4,12},{8,0},{12,4},{16,24},{20,28},{24,16},{28,20},{1,9},{5... | collective-permute-start | bytes 393224 | tf_op jit(solution)/shard_map/ppermute | solution.py:165
  12.4 6.7 %collective-permute-start.6 = (bf16[2,128,256]{2,1,0:T(8,128)(2,1)S(1)}, bf16[2,128,256]{2,1,0:T(8,128)(2,1)S(1)}, u32[]{:S(2)}, u32[]{:S(2)}) collective-permute-start(bf16[2,128,256]{2,1,0:T(8,128)(2,1)S(1)} %pair.1.refs_3_), channel_id=1, source_target_pairs={{0,4},{4,0},{8,12},{12,8},{16,20},{20,16},{24,28},{28,24},{1,5},{5... | collective-permute-start | bytes 393224 | tf_op jit(solution)/shard_map/ppermute | solution.py:165
  12.9 0.7 %copy-start.4 = (s32[1,1,32]{2,1,0:T(1,128)S(1)}, s32[1,1,32]{2,1,0:T(1,128)}, u32[]{:S(2)}) copy-start(s32[1,1,32]{2,1,0:T(1,128)} %param.9) | copy-start | bytes 388
  15.1 7.4 %collective-permute-start.2 = (bf16[2,128,256]{2,1,0:T(8,128)(2,1)S(1)}, bf16[2,128,256]{2,1,0:T(8,128)(2,1)S(1)}, u32[]{:S(2)}, u32[]{:S(2)}) collective-permute-start(bf16[2,128,256]{2,1,0:T(8,128)(2,1)S(1)} %get-tuple-element.23), channel_id=1, source_target_pairs={{0,12},{4,8},{8,4},{12,0},{16,28},{20,24},{24,20},{28,16},{1,13},{... | collective-permute-start | bytes 393224 | tf_op jit(solution)/shard_map/ppermute | solution.py:165
  17.9 6.2 %collective-permute-start.3 = (bf16[2,128,256]{2,1,0:T(8,128)(2,1)S(1)}, bf16[2,128,256]{2,1,0:T(8,128)(2,1)S(1)}, u32[]{:S(2)}, u32[]{:S(2)}) collective-permute-start(bf16[2,128,256]{2,1,0:T(8,128)(2,1)S(1)} %get-tuple-element.24), channel_id=1, source_target_pairs={{0,8},{4,12},{8,0},{12,4},{16,24},{20,28},{24,16},{28,20},{1,9},{5... | collective-permute-start | bytes 393224 | tf_op jit(solution)/shard_map/ppermute | solution.py:165
  18.9 5.2 %collective-permute-start.4 = (bf16[2,128,256]{2,1,0:T(8,128)(2,1)S(1)}, bf16[2,128,256]{2,1,0:T(8,128)(2,1)S(1)}, u32[]{:S(2)}, u32[]{:S(2)}) collective-permute-start(bf16[2,128,256]{2,1,0:T(8,128)(2,1)S(1)} %get-tuple-element.25), channel_id=1, source_target_pairs={{0,4},{4,0},{8,12},{12,8},{16,20},{20,16},{24,28},{28,24},{1,5},{5... | collective-permute-start | bytes 393224 | tf_op jit(solution)/shard_map/ppermute | solution.py:165
  19.8 4.3 %collective-permute-start.10 = (bf16[64,256]{1,0:T(8,128)(2,1)S(1)}, bf16[64,256]{1,0:T(8,128)(2,1)S(1)}, u32[]{:S(2)}, u32[]{:S(2)}) collective-permute-start(bf16[64,256]{1,0:T(8,128)(2,1)S(1)} %get-tuple-element.32), channel_id=1, source_target_pairs={{0,2},{1,3},{2,0},{3,1},{4,6},{5,7},{6,4},{7,5},{8,10},{9,11},{10,... | collective-permute-start | bytes 98312 | tf_op jit(solution)/shard_map/ppermute | solution.py:165
  20.4 3.8 %collective-permute-start.11 = (bf16[64,256]{1,0:T(8,128)(2,1)S(1)}, bf16[64,256]{1,0:T(8,128)(2,1)S(1)}, u32[]{:S(2)}, u32[]{:S(2)}) collective-permute-start(bf16[64,256]{1,0:T(8,128)(2,1)S(1)} %get-tuple-element.33), channel_id=1, source_target_pairs={{0,3},{1,2},{2,1},{3,0},{4,7},{5,6},{6,5},{7,4},{8,11},{9,10},{10,... | collective-permute-start | bytes 98312 | tf_op jit(solution)/shard_map/ppermute | solution.py:165
  22.5 1.6 %collective-permute-start.9 = (bf16[192,256]{1,0:T(8,128)(2,1)S(1)}, bf16[192,256]{1,0:T(8,128)(2,1)S(1)}, u32[]{:S(2)}, u32[]{:S(2)}) collective-permute-start(bf16[192,256]{1,0:T(8,128)(2,1)S(1)} %get-tuple-element.30), channel_id=1, source_target_pairs={{0,1},{1,0},{2,3},{3,2},{4,5},{5,4},{6,7},{7,6},{8,9},{9,8},{10,11... | collective-permute-start | bytes 294920 | tf_op jit(solution)/shard_map/ppermute | solution.py:165
  24.2 4.9 %collective-permute-start.14 = (bf16[64,256]{1,0:T(8,128)(2,1)S(1)}, bf16[64,256]{1,0:T(8,128)(2,1)S(1)}, u32[]{:S(2)}, u32[]{:S(2)}) collective-permute-start(bf16[64,256]{1,0:T(8,128)(2,1)S(1)} %grad_col.1.refs_1_), channel_id=1, source_target_pairs={{0,12},{4,8},{8,4},{12,0},{16,28},{20,24},{24,20},{28,16},{1,13},{... | collective-permute-start | bytes 98312 | tf_op jit(solution)/shard_map/ppermute | solution.py:165
  26.8 3.9 %collective-permute-start.13 = (bf16[64,256]{1,0:T(8,128)(2,1)S(1)}, bf16[64,256]{1,0:T(8,128)(2,1)S(1)}, u32[]{:S(2)}, u32[]{:S(2)}) collective-permute-start(bf16[64,256]{1,0:T(8,128)(2,1)S(1)} %grad_col.1.refs_1_), channel_id=1, source_target_pairs={{0,8},{4,12},{8,0},{12,4},{16,24},{20,28},{24,16},{28,20},{1,9},{5... | collective-permute-start | bytes 98312 | tf_op jit(solution)/shard_map/ppermute | solution.py:165
  27.9 3.9 %collective-permute-start.12 = (bf16[64,256]{1,0:T(8,128)(2,1)S(1)}, bf16[64,256]{1,0:T(8,128)(2,1)S(1)}, u32[]{:S(2)}, u32[]{:S(2)}) collective-permute-start(bf16[64,256]{1,0:T(8,128)(2,1)S(1)} %grad_col.1.refs_1_), channel_id=1, source_target_pairs={{0,4},{4,0},{8,12},{12,8},{16,20},{20,16},{24,28},{28,24},{1,5},{5... | collective-permute-start | bytes 98312 | tf_op jit(solution)/shard_map/ppermute | solution.py:165
  31.9 6.6 %collective-permute-start.15 = (bf16[192,256]{1,0:T(8,128)(2,1)S(1)}, bf16[192,256]{1,0:T(8,128)(2,1)S(1)}, u32[]{:S(2)}, u32[]{:S(2)}) collective-permute-start(bf16[192,256]{1,0:T(8,128)(2,1)S(1)} %grad_near.1.held_ref), channel_id=1, source_target_pairs={{0,16},{4,20},{8,24},{12,28},{16,0},{20,4},{24,8},{28,12},{1,17},{... | collective-permute-start | bytes 294920 | tf_op jit(solution)/shard_map/ppermute | solution.py:165
  33.6 6.9 %copy-start.1 = (bf16[256,256]{1,0:T(8,128)(2,1)S(1)}, bf16[256,256]{1,0:T(8,128)(2,1)}, u32[]{:S(2)}) copy-start(bf16[256,256]{1,0:T(8,128)(2,1)} %weight_ref.1) | copy-start | bytes 393220
  33.6 6.9 %collective-permute-start.16 = (bf16[128,256]{1,0:T(8,128)(2,1)S(1)}, bf16[128,256]{1,0:T(8,128)(2,1)S(1)}, u32[]{:S(2)}, u32[]{:S(2)}) collective-permute-start(bf16[128,256]{1,0:T(8,128)(2,1)S(1)} %get-tuple-element.37), channel_id=1, source_target_pairs={{0,2},{1,3},{2,0},{3,1},{4,6},{5,7},{6,4},{7,5},{8,10},{9,11},{10,... | collective-permute-start | bytes 196616 | tf_op jit(solution)/shard_map/ppermute | solution.py:165
  34.9 5.5 %collective-permute-start.17 = (bf16[128,256]{1,0:T(8,128)(2,1)S(1)}, bf16[128,256]{1,0:T(8,128)(2,1)S(1)}, u32[]{:S(2)}, u32[]{:S(2)}) collective-permute-start(bf16[128,256]{1,0:T(8,128)(2,1)S(1)} %get-tuple-element.38), channel_id=1, source_target_pairs={{0,3},{1,2},{2,1},{3,0},{4,7},{5,6},{6,5},{7,4},{8,11},{9,10},{10,... | collective-permute-start | bytes 196616 | tf_op jit(solution)/shard_map/ppermute | solution.py:165
  38.5 3.4 %collective-permute-start.20 = (bf16[64,256]{1,0:T(8,128)(2,1)S(1)}, bf16[64,256]{1,0:T(8,128)(2,1)S(1)}, u32[]{:S(2)}, u32[]{:S(2)}) collective-permute-start(bf16[64,256]{1,0:T(8,128)(2,1)S(1)} %grad_row.1.refs_0_), channel_id=1, source_target_pairs={{0,3},{1,2},{2,1},{3,0},{4,7},{5,6},{6,5},{7,4},{8,11},{9,10},{10,... | collective-permute-start | bytes 98312 | tf_op jit(solution)/shard_map/ppermute | solution.py:165
  38.6 4.2 %collective-permute-start.19 = (bf16[64,256]{1,0:T(8,128)(2,1)S(1)}, bf16[64,256]{1,0:T(8,128)(2,1)S(1)}, u32[]{:S(2)}, u32[]{:S(2)}) collective-permute-start(bf16[64,256]{1,0:T(8,128)(2,1)S(1)} %grad_row.1.refs_0_), channel_id=1, source_target_pairs={{0,2},{1,3},{2,0},{3,1},{4,6},{5,7},{6,4},{7,5},{8,10},{9,11},{10,... | collective-permute-start | bytes 98312 | tf_op jit(solution)/shard_map/ppermute | solution.py:165
  39.8 3.0 %collective-permute-start.18 = (bf16[64,256]{1,0:T(8,128)(2,1)S(1)}, bf16[64,256]{1,0:T(8,128)(2,1)S(1)}, u32[]{:S(2)}, u32[]{:S(2)}) collective-permute-start(bf16[64,256]{1,0:T(8,128)(2,1)S(1)} %grad_row.1.refs_0_), channel_id=1, source_target_pairs={{0,1},{1,0},{2,3},{3,2},{4,5},{5,4},{6,7},{7,6},{8,9},{9,8},{10,11... | collective-permute-start | bytes 98312 | tf_op jit(solution)/shard_map/ppermute | solution.py:165

commit v7 on v3

--- a/solution.py
+++ b/solution.py
@@ -254,10 +254,11 @@
         [VMEM] * col_devices + [ANY], (first, *fetch(pieces), column_send),
     )
     near_terms = exchange([grad_col] * half, "row")
-    row_got = fetch([chunks[0], *hold(chunks[1:], near_terms[3], "hold_chunks")])
+    held = hold(chunks[1:], near_terms[3], "hold_chunks")
+    row_got = fetch([chunks[0], *held])
     both = call(
         lambda *refs: near_kernel(*refs, terms=half), "grad_near", shape(slab + piece, width),
-        [VMEM] * (1 + half), (column_send, *near_terms),
+        [VMEM] * (1 + half) + [ANY] * len(held), (column_send, *near_terms, *held),
     )
     both_far = swap(both, "row", half)
     grad_row = call(

time: 43.2 us -> 43.2 us (level)
  no operation moved by 1% of the time
where the time goes in v7:
time: 43.2 us; the launch traced here: 43 us
  starting transfers between devices  23.4 us (54%)
  waiting for transfers between devices  11.5 us (27%)
  Pallas kernels  3.59 us (8%)
  local copies, waits for them, and re-layouts  2.34 us (5%)
  between operations  1.44 us (3%)
  other arithmetic  0.8 us (2%)
    ppermute x21, starting transfers between devices, swap(): return lax.ppermute(array, axis, pairs)  23.4 us
    ppermute x21, waiting for transfers between devices, swap(): return lax.ppermute(array, axis, pairs)  11.5 us
    pallas_call x13, Pallas kernels, call(): pl.pallas_call(kernel, out_shape=out_shape, in_specs=in_specs, out_specs=...  3.59 us
    unnamed x10, local copies, waits for them, and re-layouts  2.34 us
  transfers between devices with their start and end apart: 21, of which 11 were waited for; matrix products, arithmetic and copies ran while one was open for 0% of the time, Pallas kernels for 8%

profile of v7, /device:TPU:0, one launch (start us, length us, event | category | flops | bytes accessed | tf_op | source)
XLA Modules:
  0.0 43.0 jit_solution(15315067584701604589)
XLA Ops:
  0.6 4.1 %collective-permute-start.5 = (bf16[128,256]{1,0:T(8,128)(2,1)}, bf16[128,256]{1,0:T(8,128)(2,1)S(1)}, u32[]{:S(2)}, u32[]{:S(2)}) collective-permute-start(bf16[128,256]{1,0:T(8,128)(2,1)} %bitcast.11), channel_id=1, source_target_pairs={{0,16},{4,20},{8,24},{12,28},{16,0},{20,4},{24,8},{28,12},{1,17},{... | collective-permute-start | bytes 196616 | tf_op jit(solution)/shard_map/ppermute | solution.py:165
  4.7 1.5 %collective-permute-start = (bf16[128,256]{1,0:T(8,128)(2,1)}, bf16[128,256]{1,0:T(8,128)(2,1)S(1)}, u32[]{:S(2)}, u32[]{:S(2)}) collective-permute-start(bf16[128,256]{1,0:T(8,128)(2,1)} %bitcast.9), channel_id=1, source_target_pairs={{0,2},{1,3},{2,0},{3,1},{4,6},{5,7},{6,4},{7,5},{8,10},{9,11},{10,... | collective-permute-start | bytes 196616 | tf_op jit(solution)/shard_map/ppermute | solution.py:165
  6.9 0.6 %copy-done.4 = s32[1,1,32]{2,1,0:T(1,128)S(1)} copy-done((s32[1,1,32]{2,1,0:T(1,128)S(1)}, s32[1,1,32]{2,1,0:T(1,128)}, u32[]{:S(2)}) %copy-start.4) | copy-done | bytes 152
  7.6 0.1 pad_add_fusion.meta_ref.refs_2_
  7.6 0.8 %copy-done.2 = bf16[1,128,256]{2,1,0:T(8,128)(2,1)S(1)} copy-done((bf16[1,128,256]{2,1,0:T(8,128)(2,1)S(1)}, bf16[1,128,256]{2,1,0:T(8,128)(2,1)}, u32[]{:S(2)}) %copy-start.2) | copy-done | bytes 65560
  8.5 0.8 %copy-done.3 = bf16[1,128,256]{2,1,0:T(8,128)(2,1)S(1)} copy-done((bf16[1,128,256]{2,1,0:T(8,128)(2,1)S(1)}, bf16[1,128,256]{2,1,0:T(8,128)(2,1)}, u32[]{:S(2)}) %copy-start.3) | copy-done | bytes 65560
  9.3 0.0 collective-permute-done.refs_1_
  9.4 0.1 collective-permute-start.1
  9.4 0.0 copy-start
  9.5 2.6 %collective-permute-start.8 = (bf16[2,128,256]{2,1,0:T(8,128)(2,1)S(1)}, bf16[2,128,256]{2,1,0:T(8,128)(2,1)S(1)}, u32[]{:S(2)}, u32[]{:S(2)}) collective-permute-start(bf16[2,128,256]{2,1,0:T(8,128)(2,1)S(1)} %pair.1.refs_3_), channel_id=1, source_target_pairs={{0,12},{4,8},{8,4},{12,0},{16,28},{20,24},{24,20},{28,16},{1,13},{... | collective-permute-start | bytes 393224 | tf_op jit(solution)/shard_map/ppermute | solution.py:165
  12.0 0.4 %collective-permute-start.7 = (bf16[2,128,256]{2,1,0:T(8,128)(2,1)S(1)}, bf16[2,128,256]{2,1,0:T(8,128)(2,1)S(1)}, u32[]{:S(2)}, u32[]{:S(2)}) collective-permute-start(bf16[2,128,256]{2,1,0:T(8,128)(2,1)S(1)} %pair.1.refs_3_), channel_id=1, source_target_pairs={{0,8},{4,12},{8,0},{12,4},{16,24},{20,28},{24,16},{28,20},{1,9},{5... | collective-permute-start | bytes 393224 | tf_op jit(solution)/shard_map/ppermute | solution.py:165
  12.5 0.5 %collective-permute-start.6 = (bf16[2,128,256]{2,1,0:T(8,128)(2,1)S(1)}, bf16[2,128,256]{2,1,0:T(8,128)(2,1)S(1)}, u32[]{:S(2)}, u32[]{:S(2)}) collective-permute-start(bf16[2,128,256]{2,1,0:T(8,128)(2,1)S(1)} %pair.1.refs_3_), channel_id=1, source_target_pairs={{0,4},{4,0},{8,12},{12,8},{16,20},{20,16},{24,28},{28,24},{1,5},{5... | collective-permute-start | bytes 393224 | tf_op jit(solution)/shard_map/ppermute | solution.py:165
  13.0 1.2 %dense.1.adj_ref.refs_0_ = bf16[512,1024]{1,0:T(8,128)(2,1)S(1)} custom-call(s32[33]{0:T(128)S(1)} %pad_add_fusion.meta_ref.refs_2_, bf16[32,128,128]{2,1,0:T(8,128)(2,1)S(1)} %bitcast.8), custom_call_target="tpu_custom_call" | custom-call | tf_op jit(solution)/shard_map/dense/pallas_call | solution.py:184
  14.3 0.6 %backward.1 = (bf16[2,128,256]{2,1,0:T(8,128)(2,1)S(1)}, bf16[2,128,256]{2,1,0:T(8,128)(2,1)S(1)}, bf16[2,128,256]{2,1,0:T(8,128)(2,1)S(1)}, bf16[2,128,256]{2,1,0:T(8,128)(2,1)S(1)}) custom-call(bf16[512,1024]{1,0:T(8,128)(2,1)S(1)} %dense.1.adj_ref.refs_0_, bf16[2,128,256]{2,1,0:T(8,128)(2,1)S(1)} %cot_near.1.near_ref.refs_1_, ...), custom_call_target="tpu_custom_call" | custom-call | tf_op jit(solution)/shard_map/backward/pallas_call | solution.py:184
  14.8 2.3 %collective-permute-start.2 = (bf16[2,128,256]{2,1,0:T(8,128)(2,1)S(1)}, bf16[2,128,256]{2,1,0:T(8,128)(2,1)S(1)}, u32[]{:S(2)}, u32[]{:S(2)}) collective-permute-start(bf16[2,128,256]{2,1,0:T(8,128)(2,1)S(1)} %get-tuple-element.23), channel_id=1, source_target_pairs={{0,12},{4,8},{8,4},{12,0},{16,28},{20,24},{24,20},{28,16},{1,13},{... | collective-permute-start | bytes 393224 | tf_op jit(solution)/shard_map/ppermute | solution.py:165
  17.2 0.4 %collective-permute-start.3 = (bf16[2,128,256]{2,1,0:T(8,128)(2,1)S(1)}, bf16[2,128,256]{2,1,0:T(8,128)(2,1)S(1)}, u32[]{:S(2)}, u32[]{:S(2)}) collective-permute-start(bf16[2,128,256]{2,1,0:T(8,128)(2,1)S(1)} %get-tuple-element.24), channel_id=1, source_target_pairs={{0,8},{4,12},{8,0},{12,4},{16,24},{20,28},{24,16},{28,20},{1,9},{5... | collective-permute-start | bytes 393224 | tf_op jit(solution)/shard_map/ppermute | solution.py:165
  17.6 0.8 %collective-permute-start.4 = (bf16[2,128,256]{2,1,0:T(8,128)(2,1)S(1)}, bf16[2,128,256]{2,1,0:T(8,128)(2,1)S(1)}, u32[]{:S(2)}, u32[]{:S(2)}) collective-permute-start(bf16[2,128,256]{2,1,0:T(8,128)(2,1)S(1)} %get-tuple-element.25), channel_id=1, source_target_pairs={{0,4},{4,0},{8,12},{12,8},{16,20},{20,16},{24,28},{28,24},{1,5},{5... | collective-permute-start | bytes 393224 | tf_op jit(solution)/shard_map/ppermute | solution.py:165
  18.4 1.2 %collective-permute-done.7.refs_5_ = bf16[2,128,256]{2,1,0:T(8,128)(2,1)S(1)} collective-permute-done((bf16[2,128,256]{2,1,0:T(8,128)(2,1)S(1)}, bf16[2,128,256]{2,1,0:T(8,128)(2,1)S(1)}, u32[]{:S(2)}, u32[]{:S(2)}) %collective-permute-start.7) | collective-permute-done | bytes 131104 | tf_op jit(solution)/shard_map/ppermute | solution.py:165
  19.6 0.0 collective-permute-done.6.refs_4_
  19.7 0.8 %forward.1 = (bf16[128,256]{1,0:T(8,128)(2,1)S(1)}, bf16[128,256]{1,0:T(8,128)(2,1)S(1)}, bf16[128,256]{1,0:T(8,128)(2,1)S(1)}, bf16[64,256]{1,0:T(8,128)(2,1)S(...) custom-call(bf16[512,1024]{1,0:T(8,128)(2,1)S(1)} %dense.1.adj_ref.refs_0_, ...), custom_call_target="tpu_custom_call" | custom-call | tf_op jit(solution)/shard_map/forward/pallas_call | solution.py:184
  20.5 1.4 %collective-permute-start.10 = (bf16[64,256]{1,0:T(8,128)(2,1)S(1)}, bf16[64,256]{1,0:T(8,128)(2,1)S(1)}, u32[]{:S(2)}, u32[]{:S(2)}) collective-permute-start(bf16[64,256]{1,0:T(8,128)(2,1)S(1)} %get-tuple-element.32), channel_id=1, source_target_pairs={{0,2},{1,3},{2,0},{3,1},{4,6},{5,7},{6,4},{7,5},{8,10},{9,11},{10,... | collective-permute-start | bytes 98312 | tf_op jit(solution)/shard_map/ppermute | solution.py:165
  21.9 0.5 %collective-permute-done.2.refs_0_ = bf16[2,128,256]{2,1,0:T(8,128)(2,1)S(1)} collective-permute-done((bf16[2,128,256]{2,1,0:T(8,128)(2,1)S(1)}, bf16[2,128,256]{2,1,0:T(8,128)(2,1)S(1)}, u32[]{:S(2)}, u32[]{:S(2)}) %collective-permute-start.2) | collective-permute-done | bytes 131104 | tf_op jit(solution)/shard_map/ppermute | solution.py:165
  22.4 0.3 collective-permute-start.9
  22.7 2.2 %collective-permute-done.3.refs_1_ = bf16[2,128,256]{2,1,0:T(8,128)(2,1)S(1)} collective-permute-done((bf16[2,128,256]{2,1,0:T(8,128)(2,1)S(1)}, bf16[2,128,256]{2,1,0:T(8,128)(2,1)S(1)}, u32[]{:S(2)}, u32[]{:S(2)}) %collective-permute-start.3) | collective-permute-done | bytes 131104 | tf_op jit(solution)/shard_map/ppermute | solution.py:165
  24.9 0.0 collective-permute-done.4.refs_2_
  24.9 0.1 pair_sum.1
  24.9 0.0 collective-permute-done.10.refs_2_
  24.9 0.4 collective-permute-done.11.refs_3_
  25.3 2.5 %collective-permute-start.14 = (bf16[64,256]{1,0:T(8,128)(2,1)S(1)}, bf16[64,256]{1,0:T(8,128)(2,1)S(1)}, u32[]{:S(2)}, u32[]{:S(2)}) collective-permute-start(bf16[64,256]{1,0:T(8,128)(2,1)S(1)} %grad_col.1.refs_1_), channel_id=1, source_target_pairs={{0,12},{4,8},{8,4},{12,0},{16,28},{20,24},{24,20},{28,16},{1,13},{... | collective-permute-start | bytes 98312 | tf_op jit(solution)/shard_map/ppermute | solution.py:165
  27.9 0.4 %collective-permute-start.13 = (bf16[64,256]{1,0:T(8,128)(2,1)S(1)}, bf16[64,256]{1,0:T(8,128)(2,1)S(1)}, u32[]{:S(2)}, u32[]{:S(2)}) collective-permute-start(bf16[64,256]{1,0:T(8,128)(2,1)S(1)} %grad_col.1.refs_1_), channel_id=1, source_target_pairs={{0,8},{4,12},{8,0},{12,4},{16,24},{20,28},{24,16},{28,20},{1,9},{5... | collective-permute-start | bytes 98312 | tf_op jit(solution)/shard_map/ppermute | solution.py:165
  28.3 0.6 %collective-permute-start.12 = (bf16[64,256]{1,0:T(8,128)(2,1)S(1)}, bf16[64,256]{1,0:T(8,128)(2,1)S(1)}, u32[]{:S(2)}, u32[]{:S(2)}) collective-permute-start(bf16[64,256]{1,0:T(8,128)(2,1)S(1)} %grad_col.1.refs_1_), channel_id=1, source_target_pairs={{0,4},{4,0},{8,12},{12,8},{16,20},{20,16},{24,28},{28,24},{1,5},{5... | collective-permute-start | bytes 98312 | tf_op jit(solution)/shard_map/ppermute | solution.py:165
  28.9 1.5 %collective-permute-done.14.refs_2_.refs_4_ = bf16[64,256]{1,0:T(8,128)(2,1)S(1)} collective-permute-done((bf16[64,256]{1,0:T(8,128)(2,1)S(1)}, bf16[64,256]{1,0:T(8,128)(2,1)S(1)}, u32[]{:S(2)}, u32[]{:S(2)}) %collective-permute-start.14) | collective-permute-done | bytes 32800 | tf_op jit(solution)/shard_map/ppermute | solution.py:165
  30.4 1.4 %collective-permute-done.13.refs_3_ = bf16[64,256]{1,0:T(8,128)(2,1)S(1)} collective-permute-done((bf16[64,256]{1,0:T(8,128)(2,1)S(1)}, bf16[64,256]{1,0:T(8,128)(2,1)S(1)}, u32[]{:S(2)}, u32[]{:S(2)}) %collective-permute-start.13) | collective-permute-done | bytes 32800 | tf_op jit(solution)/shard_map/ppermute | solution.py:165
  31.8 0.4 %collective-permute-done.12.refs_2_ = bf16[64,256]{1,0:T(8,128)(2,1)S(1)} collective-permute-done((bf16[64,256]{1,0:T(8,128)(2,1)S(1)}, bf16[64,256]{1,0:T(8,128)(2,1)S(1)}, u32[]{:S(2)}, u32[]{:S(2)}) %collective-permute-start.12) | collective-permute-done | bytes 32800 | tf_op jit(solution)/shard_map/ppermute | solution.py:165
  32.3 0.0 copy-start.1
  32.3 2.6 %collective-permute-start.15 = (bf16[192,256]{1,0:T(8,128)(2,1)S(1)}, bf16[192,256]{1,0:T(8,128)(2,1)S(1)}, u32[]{:S(2)}, u32[]{:S(2)}) collective-permute-start(bf16[192,256]{1,0:T(8,128)(2,1)S(1)} %grad_near.1.held_ref), channel_id=1, source_target_pairs={{0,16},{4,20},{8,24},{12,28},{16,0},{20,4},{24,8},{28,12},{1,17},{... | collective-permute-start | bytes 294920 | tf_op jit(solution)/shard_map/ppermute | solution.py:165
  34.8 0.8 %collective-permute-start.16 = (bf16[128,256]{1,0:T(8,128)(2,1)S(1)}, bf16[128,256]{1,0:T(8,128)(2,1)S(1)}, u32[]{:S(2)}, u32[]{:S(2)}) collective-permute-start(bf16[128,256]{1,0:T(8,128)(2,1)S(1)} %get-tuple-element.36.refs_5_), channel_id=1, source_target_pairs={{0,2},{1,3},{2,0},{3,1},{4,6},{5,7},{6,4},{7,5},{8,10},{9,11},{10,... | collective-permute-start | bytes 196616 | tf_op jit(solution)/shard_map/ppermute | solution.py:165
  35.7 2.2 %collective-permute-done.15.far_ref.got_ref = bf16[192,256]{1,0:T(8,128)(2,1)S(1)} collective-permute-done((bf16[192,256]{1,0:T(8,128)(2,1)S(1)}, bf16[192,256]{1,0:T(8,128)(2,1)S(1)}, u32[]{:S(2)}, u32[]{:S(2)}) %collective-permute-start.15) | collective-permute-done | bytes 98336 | tf_op jit(solution)/shard_map/ppermute | solution.py:165
  37.9 0.1 collective-permute-start.20
  38.0 1.0 %collective-permute-start.19 = (bf16[64,256]{1,0:T(8,128)(2,1)S(1)}, bf16[64,256]{1,0:T(8,128)(2,1)S(1)}, u32[]{:S(2)}, u32[]{:S(2)}) collective-permute-start(bf16[64,256]{1,0:T(8,128)(2,1)S(1)} %grad_row.1.refs_0_), channel_id=1, source_target_pairs={{0,2},{1,3},{2,0},{3,1},{4,6},{5,7},{6,4},{7,5},{8,10},{9,11},{10,... | collective-permute-start | bytes 98312 | tf_op jit(solution)/shard_map/ppermute | solution.py:165
  39.0 0.8 %collective-permute-start.18 = (bf16[64,256]{1,0:T(8,128)(2,1)S(1)}, bf16[64,256]{1,0:T(8,128)(2,1)S(1)}, u32[]{:S(2)}, u32[]{:S(2)}) collective-permute-start(bf16[64,256]{1,0:T(8,128)(2,1)S(1)} %grad_row.1.refs_0_), channel_id=1, source_target_pairs={{0,1},{1,0},{2,3},{3,2},{4,5},{5,4},{6,7},{7,6},{8,9},{9,8},{10,11... | collective-permute-start | bytes 98312 | tf_op jit(solution)/shard_map/ppermute | solution.py:165
  39.8 0.0 collective-permute-done.16.refs_1_
  39.8 0.2 collective-permute-done.17.refs_2_
  40.0 0.8 %outputs.1 = (bf16[128,256]{1,0:T(8,128)(2,1)}, bf16[128,256]{1,0:T(8,128)(2,1)}) custom-call(bf16[256,256]{1,0:T(8,128)(2,1)S(1)} %copy-done.1, f32[128,256]{1,0:T(8,128)S(1)} %get-tuple-element.27.keep_ref, bf16[192,256]{1,0:T(8,128)(2,1)S(1)} %collective-permute-done.15.far_ref.got_ref, bf16[192,256]{1,0:T(8,128)(2,1)S(1)} %collective-permute-done.9.refs_0_.first_ref, ...), custom_call_target="tpu_custom_call" | custom-call | tf_op jit(solution)/shard_map/outputs/pallas_call | solution.py:184
  40.9 0.4 collective-permute-done.20.refs_3_
  41.3 1.0 %collective-permute-done.19.refs_2_ = bf16[64,256]{1,0:T(8,128)(2,1)S(1)} collective-permute-done((bf16[64,256]{1,0:T(8,128)(2,1)S(1)}, bf16[64,256]{1,0:T(8,128)(2,1)S(1)}, u32[]{:S(2)}, u32[]{:S(2)}) %collective-permute-start.19) | collective-permute-done | bytes 32800 | tf_op jit(solution)/shard_map/ppermute | solution.py:165
  42.3 0.0 collective-permute-done.18.refs_1_
  42.3 0.7 %convert_multiply_fusion = f32[256,256]{1,0:T(8,128)} fusion(bf16[256,256]{1,0:T(8,128)(2,1)S(1)} %weight_grad.1), kind=kLoop, calls=%fused_computation | loop fusion | flops 131072 | bytes 393216 | tf_op jit(solution)/shard_map/mul | solution.py:275
  (19 shorter events, 0.1 us)
Async XLA Ops:
  0.6 8.8 %collective-permute-start.5 = (bf16[128,256]{1,0:T(8,128)(2,1)}, bf16[128,256]{1,0:T(8,128)(2,1)S(1)}, u32[]{:S(2)}, u32[]{:S(2)}) collective-permute-start(bf16[128,256]{1,0:T(8,128)(2,1)} %bitcast.11), channel_id=1, source_target_pairs={{0,16},{4,20},{8,24},{12,28},{16,0},{20,4},{24,8},{28,12},{1,17},{... | collective-permute-start | bytes 196616 | tf_op jit(solution)/shard_map/ppermute | solution.py:165
  4.7 4.6 %collective-permute-start = (bf16[128,256]{1,0:T(8,128)(2,1)}, bf16[128,256]{1,0:T(8,128)(2,1)S(1)}, u32[]{:S(2)}, u32[]{:S(2)}) collective-permute-start(bf16[128,256]{1,0:T(8,128)(2,1)} %bitcast.9), channel_id=1, source_target_pairs={{0,2},{1,3},{2,0},{3,1},{4,6},{5,7},{6,4},{7,5},{8,10},{9,11},{10,... | collective-permute-start | bytes 196616 | tf_op jit(solution)/shard_map/ppermute | solution.py:165
  6.9 0.7 %copy-start.4 = (s32[1,1,32]{2,1,0:T(1,128)S(1)}, s32[1,1,32]{2,1,0:T(1,128)}, u32[]{:S(2)}) copy-start(s32[1,1,32]{2,1,0:T(1,128)} %param.9) | copy-start | bytes 388
  7.6 0.8 %copy-start.2 = (bf16[1,128,256]{2,1,0:T(8,128)(2,1)S(1)}, bf16[1,128,256]{2,1,0:T(8,128)(2,1)}, u32[]{:S(2)}) copy-start(bf16[1,128,256]{2,1,0:T(8,128)(2,1)} %param.11) | copy-start | bytes 196612
  8.5 0.8 %copy-start.3 = (bf16[1,128,256]{2,1,0:T(8,128)(2,1)S(1)}, bf16[1,128,256]{2,1,0:T(8,128)(2,1)}, u32[]{:S(2)}) copy-start(bf16[1,128,256]{2,1,0:T(8,128)(2,1)} %param.6) | copy-start | bytes 196612
  9.4 4.9 %collective-permute-start.1 = (bf16[2,128,256]{2,1,0:T(8,128)(2,1)S(1)}, bf16[2,128,256]{2,1,0:T(8,128)(2,1)S(1)}, u32[]{:S(2)}, u32[]{:S(2)}) collective-permute-start(bf16[2,128,256]{2,1,0:T(8,128)(2,1)S(1)} %cot_near.1.near_ref.refs_1_), channel_id=1, source_target_pairs={{0,1},{1,0},{2,3},{3,2},{4,5},{5,4},{6,7},{7,6},{8,9},{9,8},{10,11... | collective-permute-start | bytes 393224 | tf_op jit(solution)/shard_map/ppermute | solution.py:165
  9.4 3.6 %copy-start = (bf16[1,1,32,128,128]{4,3,2,1,0:T(8,128)(2,1)S(1)}, bf16[1,1,32,128,128]{4,3,2,1,0:T(8,128)(2,1)}, u32[]{:S(2)}) copy-start(bf16[1,1,32,128,128]{4,3,2,1,0:T(8,128)(2,1)} %param.8) | copy-start | bytes 3145732
  9.5 8.2 %collective-permute-start.8 = (bf16[2,128,256]{2,1,0:T(8,128)(2,1)S(1)}, bf16[2,128,256]{2,1,0:T(8,128)(2,1)S(1)}, u32[]{:S(2)}, u32[]{:S(2)}) collective-permute-start(bf16[2,128,256]{2,1,0:T(8,128)(2,1)S(1)} %pair.1.refs_3_), channel_id=1, source_target_pairs={{0,12},{4,8},{8,4},{12,0},{16,28},{20,24},{24,20},{28,16},{1,13},{... | collective-permute-start | bytes 393224 | tf_op jit(solution)/shard_map/ppermute | solution.py:165
  12.0 7.6 %collective-permute-start.7 = (bf16[2,128,256]{2,1,0:T(8,128)(2,1)S(1)}, bf16[2,128,256]{2,1,0:T(8,128)(2,1)S(1)}, u32[]{:S(2)}, u32[]{:S(2)}) collective-permute-start(bf16[2,128,256]{2,1,0:T(8,128)(2,1)S(1)} %pair.1.refs_3_), channel_id=1, source_target_pairs={{0,8},{4,12},{8,0},{12,4},{16,24},{20,28},{24,16},{28,20},{1,9},{5... | collective-permute-start | bytes 393224 | tf_op jit(solution)/shard_map/ppermute | solution.py:165
  12.5 7.2 %collective-permute-start.6 = (bf16[2,128,256]{2,1,0:T(8,128)(2,1)S(1)}, bf16[2,128,256]{2,1,0:T(8,128)(2,1)S(1)}, u32[]{:S(2)}, u32[]{:S(2)}) collective-permute-start(bf16[2,128,256]{2,1,0:T(8,128)(2,1)S(1)} %pair.1.refs_3_), channel_id=1, source_target_pairs={{0,4},{4,0},{8,12},{12,8},{16,20},{20,16},{24,28},{28,24},{1,5},{5... | collective-permute-start | bytes 393224 | tf_op jit(solution)/shard_map/ppermute | solution.py:165
  14.8 7.6 %collective-permute-start.2 = (bf16[2,128,256]{2,1,0:T(8,128)(2,1)S(1)}, bf16[2,128,256]{2,1,0:T(8,128)(2,1)S(1)}, u32[]{:S(2)}, u32[]{:S(2)}) collective-permute-start(bf16[2,128,256]{2,1,0:T(8,128)(2,1)S(1)} %get-tuple-element.23), channel_id=1, source_target_pairs={{0,12},{4,8},{8,4},{12,0},{16,28},{20,24},{24,20},{28,16},{1,13},{... | collective-permute-start | bytes 393224 | tf_op jit(solution)/shard_map/ppermute | solution.py:165
  17.2 7.7 %collective-permute-start.3 = (bf16[2,128,256]{2,1,0:T(8,128)(2,1)S(1)}, bf16[2,128,256]{2,1,0:T(8,128)(2,1)S(1)}, u32[]{:S(2)}, u32[]{:S(2)}) collective-permute-start(bf16[2,128,256]{2,1,0:T(8,128)(2,1)S(1)} %get-tuple-element.24), channel_id=1, source_target_pairs={{0,8},{4,12},{8,0},{12,4},{16,24},{20,28},{24,16},{28,20},{1,9},{5... | collective-permute-start | bytes 393224 | tf_op jit(solution)/shard_map/ppermute | solution.py:165
  17.6 7.2 %collective-permute-start.4 = (bf16[2,128,256]{2,1,0:T(8,128)(2,1)S(1)}, bf16[2,128,256]{2,1,0:T(8,128)(2,1)S(1)}, u32[]{:S(2)}, u32[]{:S(2)}) collective-permute-start(bf16[2,128,256]{2,1,0:T(8,128)(2,1)S(1)} %get-tuple-element.25), channel_id=1, source_target_pairs={{0,4},{4,0},{8,12},{12,8},{16,20},{20,16},{24,28},{28,24},{1,5},{5... | collective-permute-start | bytes 393224 | tf_op jit(solution)/shard_map/ppermute | solution.py:165
  20.5 4.5 %collective-permute-start.10 = (bf16[64,256]{1,0:T(8,128)(2,1)S(1)}, bf16[64,256]{1,0:T(8,128)(2,1)S(1)}, u32[]{:S(2)}, u32[]{:S(2)}) collective-permute-start(bf16[64,256]{1,0:T(8,128)(2,1)S(1)} %get-tuple-element.32), channel_id=1, source_target_pairs={{0,2},{1,3},{2,0},{3,1},{4,6},{5,7},{6,4},{7,5},{8,10},{9,11},{10,... | collective-permute-start | bytes 98312 | tf_op jit(solution)/shard_map/ppermute | solution.py:165
  21.9 3.4 %collective-permute-start.11 = (bf16[64,256]{1,0:T(8,128)(2,1)S(1)}, bf16[64,256]{1,0:T(8,128)(2,1)S(1)}, u32[]{:S(2)}, u32[]{:S(2)}) collective-permute-start(bf16[64,256]{1,0:T(8,128)(2,1)S(1)} %get-tuple-element.33), channel_id=1, source_target_pairs={{0,3},{1,2},{2,1},{3,0},{4,7},{5,6},{6,5},{7,4},{8,11},{9,10},{10,... | collective-permute-start | bytes 98312 | tf_op jit(solution)/shard_map/ppermute | solution.py:165
  22.4 2.9 %collective-permute-start.9 = (bf16[192,256]{1,0:T(8,128)(2,1)S(1)}, bf16[192,256]{1,0:T(8,128)(2,1)S(1)}, u32[]{:S(2)}, u32[]{:S(2)}) collective-permute-start(bf16[192,256]{1,0:T(8,128)(2,1)S(1)} %get-tuple-element.30), channel_id=1, source_target_pairs={{0,1},{1,0},{2,3},{3,2},{4,5},{5,4},{6,7},{7,6},{8,9},{9,8},{10,11... | collective-permute-start | bytes 294920 | tf_op jit(solution)/shard_map/ppermute | solution.py:165
  25.3 5.0 %collective-permute-start.14 = (bf16[64,256]{1,0:T(8,128)(2,1)S(1)}, bf16[64,256]{1,0:T(8,128)(2,1)S(1)}, u32[]{:S(2)}, u32[]{:S(2)}) collective-permute-start(bf16[64,256]{1,0:T(8,128)(2,1)S(1)} %grad_col.1.refs_1_), channel_id=1, source_target_pairs={{0,12},{4,8},{8,4},{12,0},{16,28},{20,24},{24,20},{28,16},{1,13},{... | collective-permute-start | bytes 98312 | tf_op jit(solution)/shard_map/ppermute | solution.py:165
  27.9 3.9 %collective-permute-start.13 = (bf16[64,256]{1,0:T(8,128)(2,1)S(1)}, bf16[64,256]{1,0:T(8,128)(2,1)S(1)}, u32[]{:S(2)}, u32[]{:S(2)}) collective-permute-start(bf16[64,256]{1,0:T(8,128)(2,1)S(1)} %grad_col.1.refs_1_), channel_id=1, source_target_pairs={{0,8},{4,12},{8,0},{12,4},{16,24},{20,28},{24,16},{28,20},{1,9},{5... | collective-permute-start | bytes 98312 | tf_op jit(solution)/shard_map/ppermute | solution.py:165
  28.3 3.9 %collective-permute-start.12 = (bf16[64,256]{1,0:T(8,128)(2,1)S(1)}, bf16[64,256]{1,0:T(8,128)(2,1)S(1)}, u32[]{:S(2)}, u32[]{:S(2)}) collective-permute-start(bf16[64,256]{1,0:T(8,128)(2,1)S(1)} %grad_col.1.refs_1_), channel_id=1, source_target_pairs={{0,4},{4,0},{8,12},{12,8},{16,20},{20,16},{24,28},{28,24},{1,5},{5... | collective-permute-start | bytes 98312 | tf_op jit(solution)/shard_map/ppermute | solution.py:165
  32.3 7.8 %copy-start.1 = (bf16[256,256]{1,0:T(8,128)(2,1)S(1)}, bf16[256,256]{1,0:T(8,128)(2,1)}, u32[]{:S(2)}) copy-start(bf16[256,256]{1,0:T(8,128)(2,1)} %weight_ref.1) | copy-start | bytes 393220
  32.3 5.6 %collective-permute-start.15 = (bf16[192,256]{1,0:T(8,128)(2,1)S(1)}, bf16[192,256]{1,0:T(8,128)(2,1)S(1)}, u32[]{:S(2)}, u32[]{:S(2)}) collective-permute-start(bf16[192,256]{1,0:T(8,128)(2,1)S(1)} %grad_near.1.held_ref), channel_id=1, source_target_pairs={{0,16},{4,20},{8,24},{12,28},{16,0},{20,4},{24,8},{28,12},{1,17},{... | collective-permute-start | bytes 294920 | tf_op jit(solution)/shard_map/ppermute | solution.py:165
  34.8 5.0 %collective-permute-start.16 = (bf16[128,256]{1,0:T(8,128)(2,1)S(1)}, bf16[128,256]{1,0:T(8,128)(2,1)S(1)}, u32[]{:S(2)}, u32[]{:S(2)}) collective-permute-start(bf16[128,256]{1,0:T(8,128)(2,1)S(1)} %get-tuple-element.36.refs_5_), channel_id=1, source_target_pairs={{0,2},{1,3},{2,0},{3,1},{4,6},{5,7},{6,4},{7,5},{8,10},{9,11},{10,... | collective-permute-start | bytes 196616 | tf_op jit(solution)/shard_map/ppermute | solution.py:165
  35.7 4.4 %collective-permute-start.17 = (bf16[128,256]{1,0:T(8,128)(2,1)S(1)}, bf16[128,256]{1,0:T(8,128)(2,1)S(1)}, u32[]{:S(2)}, u32[]{:S(2)}) collective-permute-start(bf16[128,256]{1,0:T(8,128)(2,1)S(1)} %get-tuple-element.37.refs_6_), channel_id=1, source_target_pairs={{0,3},{1,2},{2,1},{3,0},{4,7},{5,6},{6,5},{7,4},{8,11},{9,10},{10,... | collective-permute-start | bytes 196616 | tf_op jit(solution)/shard_map/ppermute | solution.py:165
  37.9 3.4 %collective-permute-start.20 = (bf16[64,256]{1,0:T(8,128)(2,1)S(1)}, bf16[64,256]{1,0:T(8,128)(2,1)S(1)}, u32[]{:S(2)}, u32[]{:S(2)}) collective-permute-start(bf16[64,256]{1,0:T(8,128)(2,1)S(1)} %grad_row.1.refs_0_), channel_id=1, source_target_pairs={{0,3},{1,2},{2,1},{3,0},{4,7},{5,6},{6,5},{7,4},{8,11},{9,10},{10,... | collective-permute-start | bytes 98312 | tf_op jit(solution)/shard_map/ppermute | solution.py:165
  38.0 4.3 %collective-permute-start.19 = (bf16[64,256]{1,0:T(8,128)(2,1)S(1)}, bf16[64,256]{1,0:T(8,128)(2,1)S(1)}, u32[]{:S(2)}, u32[]{:S(2)}) collective-permute-start(bf16[64,256]{1,0:T(8,128)(2,1)S(1)} %grad_row.1.refs_0_), channel_id=1, source_target_pairs={{0,2},{1,3},{2,0},{3,1},{4,6},{5,7},{6,4},{7,5},{8,10},{9,11},{10,... | collective-permute-start | bytes 98312 | tf_op jit(solution)/shard_map/ppermute | solution.py:165
  39.0 3.3 %collective-permute-start.18 = (bf16[64,256]{1,0:T(8,128)(2,1)S(1)}, bf16[64,256]{1,0:T(8,128)(2,1)S(1)}, u32[]{:S(2)}, u32[]{:S(2)}) collective-permute-start(bf16[64,256]{1,0:T(8,128)(2,1)S(1)} %grad_row.1.refs_0_), channel_id=1, source_target_pairs={{0,1},{1,0},{2,3},{3,2},{4,5},{5,4},{6,7},{7,6},{8,9},{9,8},{10,11... | collective-permute-start | bytes 98312 | tf_op jit(solution)/shard_map/ppermute | solution.py:165

commit v8 on v6

--- a/solution.py
+++ b/solution.py
@@ -254,10 +254,11 @@
         [VMEM] * col_devices + [ANY], (first, *fetch(pieces), column_send),
     )
     near_terms = exchange([grad_col] * half, "row")
-    row_got = fetch([chunks[0], *hold(chunks[1:], near_terms[3], "hold_chunks")])
+    held = hold(chunks[1:], near_terms[3], "hold_chunks")
+    row_got = fetch([chunks[0], *held])
     both = call(
         lambda *refs: near_kernel(*refs, terms=half), "grad_near", shape(slab + piece, width),
-        [VMEM] * (1 + half), (column_send, *near_terms),
+        [VMEM] * (1 + half) + [ANY] * len(held), (column_send, *near_terms, *held),
     )
     both_far = swap(both, "row", half)
     grad_row = call(

time: 42.8 us -> 43.8 us (1.023); the launches traced: 43.5 us -> 43.6 us
  no operation moved by 1% of the time
where the time goes in v8:
time: 43.8 us; the launch traced here: 43.6 us
  starting transfers between devices  21.9 us (50%)
  waiting for transfers between devices  13.7 us (31%)
  Pallas kernels  3.54 us (8%)
  local copies, waits for them, and re-layouts  2.33 us (5%)
  between operations  1.44 us (3%)
  other arithmetic  0.72 us (2%)
    ppermute x21, starting transfers between devices, swap(): return lax.ppermute(array, axis, pairs)  21.9 us
    ppermute x21, waiting for transfers between devices, swap(): return lax.ppermute(array, axis, pairs)  13.7 us
    pallas_call x13, Pallas kernels, call(): pl.pallas_call(kernel, out_shape=out_shape, in_specs=in_specs, out_specs=...  3.54 us
    unnamed x10, local copies, waits for them, and re-layouts  2.33 us
  transfers between devices with their start and end apart: 21, of which 10 were waited for; matrix products, arithmetic and copies ran while one was open for 0% of the time, Pallas kernels for 8%

profile of v8, /device:TPU:0, one launch (start us, length us, event | category | flops | bytes accessed | tf_op | source)
XLA Modules:
  0.0 43.6 jit_solution(8024432591153432714)
XLA Ops:
  0.6 3.0 %collective-permute-start = (bf16[128,256]{1,0:T(8,128)(2,1)}, bf16[128,256]{1,0:T(8,128)(2,1)S(1)}, u32[]{:S(2)}, u32[]{:S(2)}) collective-permute-start(bf16[128,256]{1,0:T(8,128)(2,1)} %bitcast.9), channel_id=1, source_target_pairs={{0,2},{1,3},{2,0},{3,1},{4,6},{5,7},{6,4},{7,5},{8,10},{9,11},{10,... | collective-permute-start | bytes 196616 | tf_op jit(solution)/shard_map/ppermute | solution.py:165
  3.7 2.6 %collective-permute-start.5 = (bf16[128,256]{1,0:T(8,128)(2,1)}, bf16[128,256]{1,0:T(8,128)(2,1)S(1)}, u32[]{:S(2)}, u32[]{:S(2)}) collective-permute-start(bf16[128,256]{1,0:T(8,128)(2,1)} %bitcast.11), channel_id=1, source_target_pairs={{0,16},{4,20},{8,24},{12,28},{16,0},{20,4},{24,8},{28,12},{1,17},{... | collective-permute-start | bytes 196616 | tf_op jit(solution)/shard_map/ppermute | solution.py:165
  6.9 0.8 %copy-done.2 = bf16[1,128,256]{2,1,0:T(8,128)(2,1)S(1)} copy-done((bf16[1,128,256]{2,1,0:T(8,128)(2,1)S(1)}, bf16[1,128,256]{2,1,0:T(8,128)(2,1)}, u32[]{:S(2)}) %copy-start.2) | copy-done | bytes 65560
  7.7 0.8 %copy-done.3 = bf16[1,128,256]{2,1,0:T(8,128)(2,1)S(1)} copy-done((bf16[1,128,256]{2,1,0:T(8,128)(2,1)S(1)}, bf16[1,128,256]{2,1,0:T(8,128)(2,1)}, u32[]{:S(2)}) %copy-start.3) | copy-done | bytes 65560
  8.6 0.0 collective-permute-done.refs_1_
  8.6 0.1 collective-permute-start.1
  8.7 0.6 %collective-permute-done.5.refs_1_ = bf16[128,256]{1,0:T(8,128)(2,1)S(1)} collective-permute-done((bf16[128,256]{1,0:T(8,128)(2,1)}, bf16[128,256]{1,0:T(8,128)(2,1)S(1)}, u32[]{:S(2)}, u32[]{:S(2)}) %collective-permute-start.5) | collective-permute-done | bytes 65568 | tf_op jit(solution)/shard_map/ppermute | solution.py:165
  9.4 2.3 %collective-permute-start.8 = (bf16[2,128,256]{2,1,0:T(8,128)(2,1)S(1)}, bf16[2,128,256]{2,1,0:T(8,128)(2,1)S(1)}, u32[]{:S(2)}, u32[]{:S(2)}) collective-permute-start(bf16[2,128,256]{2,1,0:T(8,128)(2,1)S(1)} %pair.1.refs_3_), channel_id=1, source_target_pairs={{0,12},{4,8},{8,4},{12,0},{16,28},{20,24},{24,20},{28,16},{1,13},{... | collective-permute-start | bytes 393224 | tf_op jit(solution)/shard_map/ppermute | solution.py:165
  11.6 0.7 %collective-permute-start.7 = (bf16[2,128,256]{2,1,0:T(8,128)(2,1)S(1)}, bf16[2,128,256]{2,1,0:T(8,128)(2,1)S(1)}, u32[]{:S(2)}, u32[]{:S(2)}) collective-permute-start(bf16[2,128,256]{2,1,0:T(8,128)(2,1)S(1)} %pair.1.refs_3_), channel_id=1, source_target_pairs={{0,8},{4,12},{8,0},{12,4},{16,24},{20,28},{24,16},{28,20},{1,9},{5... | collective-permute-start | bytes 393224 | tf_op jit(solution)/shard_map/ppermute | solution.py:165
  12.4 0.5 %collective-permute-start.6 = (bf16[2,128,256]{2,1,0:T(8,128)(2,1)S(1)}, bf16[2,128,256]{2,1,0:T(8,128)(2,1)S(1)}, u32[]{:S(2)}, u32[]{:S(2)}) collective-permute-start(bf16[2,128,256]{2,1,0:T(8,128)(2,1)S(1)} %pair.1.refs_3_), channel_id=1, source_target_pairs={{0,4},{4,0},{8,12},{12,8},{16,20},{20,16},{24,28},{28,24},{1,5},{5... | collective-permute-start | bytes 393224 | tf_op jit(solution)/shard_map/ppermute | solution.py:165
  12.9 0.7 %copy-done.4 = s32[1,1,32]{2,1,0:T(1,128)S(1)} copy-done((s32[1,1,32]{2,1,0:T(1,128)S(1)}, s32[1,1,32]{2,1,0:T(1,128)}, u32[]{:S(2)}) %copy-start.4) | copy-done | bytes 152
  13.6 1.2 %dense.1.adj_ref.refs_0_ = bf16[512,1024]{1,0:T(8,128)(2,1)S(1)} custom-call(s32[32]{0:T(128)S(1)} %bitcast.13, s32[1]{0:T(128)} %bitcast.7.count_ref, bf16[32,128,128]{2,1,0:T(8,128)(2,1)S(1)} %bitcast.8), custom_call_target="tpu_custom_call" | custom-call | tf_op jit(solution)/shard_map/dense/pallas_call | solution.py:183
  14.7 0.0 collective-permute-done.1.other_ref.refs_2_
  14.7 0.6 %backward.1 = (bf16[2,128,256]{2,1,0:T(8,128)(2,1)S(1)}, bf16[2,128,256]{2,1,0:T(8,128)(2,1)S(1)}, bf16[2,128,256]{2,1,0:T(8,128)(2,1)S(1)}, bf16[2,128,256]{2,1,0:T(8,128)(2,1)S(1)}) custom-call(bf16[512,1024]{1,0:T(8,128)(2,1)S(1)} %dense.1.adj_ref.refs_0_, bf16[2,128,256]{2,1,0:T(8,128)(2,1)S(1)} %cot_near.1.near_ref.refs_1_, ...), custom_call_target="tpu_custom_call" | custom-call | tf_op jit(solution)/shard_map/backward/pallas_call | solution.py:183
  15.3 2.1 %collective-permute-start.2 = (bf16[2,128,256]{2,1,0:T(8,128)(2,1)S(1)}, bf16[2,128,256]{2,1,0:T(8,128)(2,1)S(1)}, u32[]{:S(2)}, u32[]{:S(2)}) collective-permute-start(bf16[2,128,256]{2,1,0:T(8,128)(2,1)S(1)} %get-tuple-element.23), channel_id=1, source_target_pairs={{0,12},{4,8},{8,4},{12,0},{16,28},{20,24},{24,20},{28,16},{1,13},{... | collective-permute-start | bytes 393224 | tf_op jit(solution)/shard_map/ppermute | solution.py:165
  17.4 0.9 %collective-permute-start.3 = (bf16[2,128,256]{2,1,0:T(8,128)(2,1)S(1)}, bf16[2,128,256]{2,1,0:T(8,128)(2,1)S(1)}, u32[]{:S(2)}, u32[]{:S(2)}) collective-permute-start(bf16[2,128,256]{2,1,0:T(8,128)(2,1)S(1)} %get-tuple-element.24), channel_id=1, source_target_pairs={{0,8},{4,12},{8,0},{12,4},{16,24},{20,28},{24,16},{28,20},{1,9},{5... | collective-permute-start | bytes 393224 | tf_op jit(solution)/shard_map/ppermute | solution.py:165
  18.3 0.0 collective-permute-done.8.refs_6_
  18.3 0.6 %collective-permute-start.4 = (bf16[2,128,256]{2,1,0:T(8,128)(2,1)S(1)}, bf16[2,128,256]{2,1,0:T(8,128)(2,1)S(1)}, u32[]{:S(2)}, u32[]{:S(2)}) collective-permute-start(bf16[2,128,256]{2,1,0:T(8,128)(2,1)S(1)} %get-tuple-element.25), channel_id=1, source_target_pairs={{0,4},{4,0},{8,12},{12,8},{16,20},{20,16},{24,28},{28,24},{1,5},{5... | collective-permute-start | bytes 393224 | tf_op jit(solution)/shard_map/ppermute | solution.py:165
  18.9 0.2 collective-permute-done.7.refs_5_
  19.0 0.0 collective-permute-done.6.refs_4_
  19.0 0.8 %forward.1 = (bf16[128,256]{1,0:T(8,128)(2,1)S(1)}, bf16[128,256]{1,0:T(8,128)(2,1)S(1)}, bf16[128,256]{1,0:T(8,128)(2,1)S(1)}, bf16[64,256]{1,0:T(8,128)(2,1)S(...) custom-call(bf16[512,1024]{1,0:T(8,128)(2,1)S(1)} %dense.1.adj_ref.refs_0_, ...), custom_call_target="tpu_custom_call" | custom-call | tf_op jit(solution)/shard_map/forward/pallas_call | solution.py:183
  19.8 0.5 %collective-permute-start.10 = (bf16[64,256]{1,0:T(8,128)(2,1)S(1)}, bf16[64,256]{1,0:T(8,128)(2,1)S(1)}, u32[]{:S(2)}, u32[]{:S(2)}) collective-permute-start(bf16[64,256]{1,0:T(8,128)(2,1)S(1)} %get-tuple-element.32), channel_id=1, source_target_pairs={{0,2},{1,3},{2,0},{3,1},{4,6},{5,7},{6,4},{7,5},{8,10},{9,11},{10,... | collective-permute-start | bytes 98312 | tf_op jit(solution)/shard_map/ppermute | solution.py:165
  20.4 0.0 collective-permute-start.11
  20.4 2.3 %collective-permute-done.2.refs_0_ = bf16[2,128,256]{2,1,0:T(8,128)(2,1)S(1)} collective-permute-done((bf16[2,128,256]{2,1,0:T(8,128)(2,1)S(1)}, bf16[2,128,256]{2,1,0:T(8,128)(2,1)S(1)}, u32[]{:S(2)}, u32[]{:S(2)}) %collective-permute-start.2) | collective-permute-done | bytes 131104 | tf_op jit(solution)/shard_map/ppermute | solution.py:165
  22.6 0.0 collective-permute-start.9
  22.6 1.4 %collective-permute-done.3.refs_1_ = bf16[2,128,256]{2,1,0:T(8,128)(2,1)S(1)} collective-permute-done((bf16[2,128,256]{2,1,0:T(8,128)(2,1)S(1)}, bf16[2,128,256]{2,1,0:T(8,128)(2,1)S(1)}, u32[]{:S(2)}, u32[]{:S(2)}) %collective-permute-start.3) | collective-permute-done | bytes 131104 | tf_op jit(solution)/shard_map/ppermute | solution.py:165
  24.0 0.0 collective-permute-done.4.refs_2_
  24.0 0.1 pair_sum.1
  24.1 0.0 collective-permute-done.10.refs_2_
  24.1 0.0 collective-permute-done.11.refs_3_
  24.2 2.7 %collective-permute-start.14 = (bf16[64,256]{1,0:T(8,128)(2,1)S(1)}, bf16[64,256]{1,0:T(8,128)(2,1)S(1)}, u32[]{:S(2)}, u32[]{:S(2)}) collective-permute-start(bf16[64,256]{1,0:T(8,128)(2,1)S(1)} %grad_col.1.refs_1_), channel_id=1, source_target_pairs={{0,12},{4,8},{8,4},{12,0},{16,28},{20,24},{24,20},{28,16},{1,13},{... | collective-permute-start | bytes 98312 | tf_op jit(solution)/shard_map/ppermute | solution.py:165
  26.8 1.2 %collective-permute-start.13 = (bf16[64,256]{1,0:T(8,128)(2,1)S(1)}, bf16[64,256]{1,0:T(8,128)(2,1)S(1)}, u32[]{:S(2)}, u32[]{:S(2)}) collective-permute-start(bf16[64,256]{1,0:T(8,128)(2,1)S(1)} %grad_col.1.refs_1_), channel_id=1, source_target_pairs={{0,8},{4,12},{8,0},{12,4},{16,24},{20,28},{24,16},{28,20},{1,9},{5... | collective-permute-start | bytes 98312 | tf_op jit(solution)/shard_map/ppermute | solution.py:165
  28.1 0.0 collective-permute-start.12
  28.1 1.0 %collective-permute-done.14.refs_2_.refs_4_ = bf16[64,256]{1,0:T(8,128)(2,1)S(1)} collective-permute-done((bf16[64,256]{1,0:T(8,128)(2,1)S(1)}, bf16[64,256]{1,0:T(8,128)(2,1)S(1)}, u32[]{:S(2)}, u32[]{:S(2)}) %collective-permute-start.14) | collective-permute-done | bytes 32800 | tf_op jit(solution)/shard_map/ppermute | solution.py:165
  29.1 1.7 %collective-permute-done.13.refs_3_ = bf16[64,256]{1,0:T(8,128)(2,1)S(1)} collective-permute-done((bf16[64,256]{1,0:T(8,128)(2,1)S(1)}, bf16[64,256]{1,0:T(8,128)(2,1)S(1)}, u32[]{:S(2)}, u32[]{:S(2)}) %collective-permute-start.13) | collective-permute-done | bytes 32800 | tf_op jit(solution)/shard_map/ppermute | solution.py:165
  30.7 1.2 %collective-permute-done.12.refs_2_ = bf16[64,256]{1,0:T(8,128)(2,1)S(1)} collective-permute-done((bf16[64,256]{1,0:T(8,128)(2,1)S(1)}, bf16[64,256]{1,0:T(8,128)(2,1)S(1)}, u32[]{:S(2)}, u32[]{:S(2)}) %collective-permute-start.12) | collective-permute-done | bytes 32800 | tf_op jit(solution)/shard_map/ppermute | solution.py:165
  32.0 0.0 copy-start.1
  32.0 1.7 %collective-permute-start.15 = (bf16[192,256]{1,0:T(8,128)(2,1)S(1)}, bf16[192,256]{1,0:T(8,128)(2,1)S(1)}, u32[]{:S(2)}, u32[]{:S(2)}) collective-permute-start(bf16[192,256]{1,0:T(8,128)(2,1)S(1)} %grad_near.1.held_ref), channel_id=1, source_target_pairs={{0,16},{4,20},{8,24},{12,28},{16,0},{20,4},{24,8},{28,12},{1,17},{... | collective-permute-start | bytes 294920 | tf_op jit(solution)/shard_map/ppermute | solution.py:165
  33.8 1.0 %collective-permute-start.16 = (bf16[128,256]{1,0:T(8,128)(2,1)S(1)}, bf16[128,256]{1,0:T(8,128)(2,1)S(1)}, u32[]{:S(2)}, u32[]{:S(2)}) collective-permute-start(bf16[128,256]{1,0:T(8,128)(2,1)S(1)} %get-tuple-element.36.refs_5_), channel_id=1, source_target_pairs={{0,2},{1,3},{2,0},{3,1},{4,6},{5,7},{6,4},{7,5},{8,10},{9,11},{10,... | collective-permute-start | bytes 196616 | tf_op jit(solution)/shard_map/ppermute | solution.py:165
  34.7 0.0 collective-permute-start.17
  34.7 3.9 %collective-permute-done.15.far_ref.got_ref = bf16[192,256]{1,0:T(8,128)(2,1)S(1)} collective-permute-done((bf16[192,256]{1,0:T(8,128)(2,1)S(1)}, bf16[192,256]{1,0:T(8,128)(2,1)S(1)}, u32[]{:S(2)}, u32[]{:S(2)}) %collective-permute-start.15) | collective-permute-done | bytes 98336 | tf_op jit(solution)/shard_map/ppermute | solution.py:165
  38.7 0.1 collective-permute-start.20
  38.8 1.3 %collective-permute-start.19 = (bf16[64,256]{1,0:T(8,128)(2,1)S(1)}, bf16[64,256]{1,0:T(8,128)(2,1)S(1)}, u32[]{:S(2)}, u32[]{:S(2)}) collective-permute-start(bf16[64,256]{1,0:T(8,128)(2,1)S(1)} %grad_row.1.refs_0_), channel_id=1, source_target_pairs={{0,2},{1,3},{2,0},{3,1},{4,6},{5,7},{6,4},{7,5},{8,10},{9,11},{10,... | collective-permute-start | bytes 98312 | tf_op jit(solution)/shard_map/ppermute | solution.py:165
  40.0 0.6 %collective-permute-start.18 = (bf16[64,256]{1,0:T(8,128)(2,1)S(1)}, bf16[64,256]{1,0:T(8,128)(2,1)S(1)}, u32[]{:S(2)}, u32[]{:S(2)}) collective-permute-start(bf16[64,256]{1,0:T(8,128)(2,1)S(1)} %grad_row.1.refs_0_), channel_id=1, source_target_pairs={{0,1},{1,0},{2,3},{3,2},{4,5},{5,4},{6,7},{7,6},{8,9},{9,8},{10,11... | collective-permute-start | bytes 98312 | tf_op jit(solution)/shard_map/ppermute | solution.py:165
  40.6 0.8 %outputs.1 = (bf16[128,256]{1,0:T(8,128)(2,1)}, bf16[128,256]{1,0:T(8,128)(2,1)}) custom-call(bf16[256,256]{1,0:T(8,128)(2,1)S(1)} %copy-done.1, f32[128,256]{1,0:T(8,128)S(1)} %get-tuple-element.27.keep_ref, bf16[192,256]{1,0:T(8,128)(2,1)S(1)} %collective-permute-done.15.far_ref.got_ref, bf16[192,256]{1,0:T(8,128)(2,1)S(1)} %collective-permute-done.9.refs_0_.first_ref, ...), custom_call_target="tpu_custom_call" | custom-call | tf_op jit(solution)/shard_map/outputs/pallas_call | solution.py:183
  41.5 0.7 %collective-permute-done.20.refs_3_ = bf16[64,256]{1,0:T(8,128)(2,1)S(1)} collective-permute-done((bf16[64,256]{1,0:T(8,128)(2,1)S(1)}, bf16[64,256]{1,0:T(8,128)(2,1)S(1)}, u32[]{:S(2)}, u32[]{:S(2)}) %collective-permute-start.20) | collective-permute-done | bytes 32800 | tf_op jit(solution)/shard_map/ppermute | solution.py:165
  42.2 0.7 %collective-permute-done.19.refs_2_ = bf16[64,256]{1,0:T(8,128)(2,1)S(1)} collective-permute-done((bf16[64,256]{1,0:T(8,128)(2,1)S(1)}, bf16[64,256]{1,0:T(8,128)(2,1)S(1)}, u32[]{:S(2)}, u32[]{:S(2)}) %collective-permute-start.19) | collective-permute-done | bytes 32800 | tf_op jit(solution)/shard_map/ppermute | solution.py:165
  42.9 0.7 %convert_multiply_fusion = f32[256,256]{1,0:T(8,128)} fusion(bf16[256,256]{1,0:T(8,128)(2,1)S(1)} %weight_grad.1), kind=kLoop, calls=%fused_computation | loop fusion | flops 131072 | bytes 393216 | tf_op jit(solution)/shard_map/mul | solution.py:275
  (18 shorter events, 0.1 us)
Async XLA Ops:
  0.6 8.0 %collective-permute-start = (bf16[128,256]{1,0:T(8,128)(2,1)}, bf16[128,256]{1,0:T(8,128)(2,1)S(1)}, u32[]{:S(2)}, u32[]{:S(2)}) collective-permute-start(bf16[128,256]{1,0:T(8,128)(2,1)} %bitcast.9), channel_id=1, source_target_pairs={{0,2},{1,3},{2,0},{3,1},{4,6},{5,7},{6,4},{7,5},{8,10},{9,11},{10,... | collective-permute-start | bytes 196616 | tf_op jit(solution)/shard_map/ppermute | solution.py:165
  3.7 5.7 %collective-permute-start.5 = (bf16[128,256]{1,0:T(8,128)(2,1)}, bf16[128,256]{1,0:T(8,128)(2,1)S(1)}, u32[]{:S(2)}, u32[]{:S(2)}) collective-permute-start(bf16[128,256]{1,0:T(8,128)(2,1)} %bitcast.11), channel_id=1, source_target_pairs={{0,16},{4,20},{8,24},{12,28},{16,0},{20,4},{24,8},{28,12},{1,17},{... | collective-permute-start | bytes 196616 | tf_op jit(solution)/shard_map/ppermute | solution.py:165
  6.9 0.8 %copy-start.2 = (bf16[1,128,256]{2,1,0:T(8,128)(2,1)S(1)}, bf16[1,128,256]{2,1,0:T(8,128)(2,1)}, u32[]{:S(2)}) copy-start(bf16[1,128,256]{2,1,0:T(8,128)(2,1)} %param.11) | copy-start | bytes 196612
  7.7 0.8 %copy-start.3 = (bf16[1,128,256]{2,1,0:T(8,128)(2,1)S(1)}, bf16[1,128,256]{2,1,0:T(8,128)(2,1)}, u32[]{:S(2)}) copy-start(bf16[1,128,256]{2,1,0:T(8,128)(2,1)} %param.6) | copy-start | bytes 196612
  8.6 6.1 %collective-permute-start.1 = (bf16[2,128,256]{2,1,0:T(8,128)(2,1)S(1)}, bf16[2,128,256]{2,1,0:T(8,128)(2,1)S(1)}, u32[]{:S(2)}, u32[]{:S(2)}) collective-permute-start(bf16[2,128,256]{2,1,0:T(8,128)(2,1)S(1)} %cot_near.1.near_ref.refs_1_), channel_id=1, source_target_pairs={{0,1},{1,0},{2,3},{3,2},{4,5},{5,4},{6,7},{7,6},{8,9},{9,8},{10,11... | collective-permute-start | bytes 393224 | tf_op jit(solution)/shard_map/ppermute | solution.py:165
  9.3 3.6 %copy-start = (bf16[1,1,32,128,128]{4,3,2,1,0:T(8,128)(2,1)S(1)}, bf16[1,1,32,128,128]{4,3,2,1,0:T(8,128)(2,1)}, u32[]{:S(2)}) copy-start(bf16[1,1,32,128,128]{4,3,2,1,0:T(8,128)(2,1)} %param.8) | copy-start | bytes 3145732
  9.4 8.9 %collective-permute-start.8 = (bf16[2,128,256]{2,1,0:T(8,128)(2,1)S(1)}, bf16[2,128,256]{2,1,0:T(8,128)(2,1)S(1)}, u32[]{:S(2)}, u32[]{:S(2)}) collective-permute-start(bf16[2,128,256]{2,1,0:T(8,128)(2,1)S(1)} %pair.1.refs_3_), channel_id=1, source_target_pairs={{0,12},{4,8},{8,4},{12,0},{16,28},{20,24},{24,20},{28,16},{1,13},{... | collective-permute-start | bytes 393224 | tf_op jit(solution)/shard_map/ppermute | solution.py:165
  11.6 7.4 %collective-permute-start.7 = (bf16[2,128,256]{2,1,0:T(8,128)(2,1)S(1)}, bf16[2,128,256]{2,1,0:T(8,128)(2,1)S(1)}, u32[]{:S(2)}, u32[]{:S(2)}) collective-permute-start(bf16[2,128,256]{2,1,0:T(8,128)(2,1)S(1)} %pair.1.refs_3_), channel_id=1, source_target_pairs={{0,8},{4,12},{8,0},{12,4},{16,24},{20,28},{24,16},{28,20},{1,9},{5... | collective-permute-start | bytes 393224 | tf_op jit(solution)/shard_map/ppermute | solution.py:165
  12.4 6.7 %collective-permute-start.6 = (bf16[2,128,256]{2,1,0:T(8,128)(2,1)S(1)}, bf16[2,128,256]{2,1,0:T(8,128)(2,1)S(1)}, u32[]{:S(2)}, u32[]{:S(2)}) collective-permute-start(bf16[2,128,256]{2,1,0:T(8,128)(2,1)S(1)} %pair.1.refs_3_), channel_id=1, source_target_pairs={{0,4},{4,0},{8,12},{12,8},{16,20},{20,16},{24,28},{28,24},{1,5},{5... | collective-permute-start | bytes 393224 | tf_op jit(solution)/shard_map/ppermute | solution.py:165
  12.9 0.7 %copy-start.4 = (s32[1,1,32]{2,1,0:T(1,128)S(1)}, s32[1,1,32]{2,1,0:T(1,128)}, u32[]{:S(2)}) copy-start(s32[1,1,32]{2,1,0:T(1,128)} %param.9) | copy-start | bytes 388
  15.3 7.3 %collective-permute-start.2 = (bf16[2,128,256]{2,1,0:T(8,128)(2,1)S(1)}, bf16[2,128,256]{2,1,0:T(8,128)(2,1)S(1)}, u32[]{:S(2)}, u32[]{:S(2)}) collective-permute-start(bf16[2,128,256]{2,1,0:T(8,128)(2,1)S(1)} %get-tuple-element.23), channel_id=1, source_target_pairs={{0,12},{4,8},{8,4},{12,0},{16,28},{20,24},{24,20},{28,16},{1,13},{... | collective-permute-start | bytes 393224 | tf_op jit(solution)/shard_map/ppermute | solution.py:165
  17.4 6.6 %collective-permute-start.3 = (bf16[2,128,256]{2,1,0:T(8,128)(2,1)S(1)}, bf16[2,128,256]{2,1,0:T(8,128)(2,1)S(1)}, u32[]{:S(2)}, u32[]{:S(2)}) collective-permute-start(bf16[2,128,256]{2,1,0:T(8,128)(2,1)S(1)} %get-tuple-element.24), channel_id=1, source_target_pairs={{0,8},{4,12},{8,0},{12,4},{16,24},{20,28},{24,16},{28,20},{1,9},{5... | collective-permute-start | bytes 393224 | tf_op jit(solution)/shard_map/ppermute | solution.py:165
  18.3 5.8 %collective-permute-start.4 = (bf16[2,128,256]{2,1,0:T(8,128)(2,1)S(1)}, bf16[2,128,256]{2,1,0:T(8,128)(2,1)S(1)}, u32[]{:S(2)}, u32[]{:S(2)}) collective-permute-start(bf16[2,128,256]{2,1,0:T(8,128)(2,1)S(1)} %get-tuple-element.25), channel_id=1, source_target_pairs={{0,4},{4,0},{8,12},{12,8},{16,20},{20,16},{24,28},{28,24},{1,5},{5... | collective-permute-start | bytes 393224 | tf_op jit(solution)/shard_map/ppermute | solution.py:165
  19.8 4.3 %collective-permute-start.10 = (bf16[64,256]{1,0:T(8,128)(2,1)S(1)}, bf16[64,256]{1,0:T(8,128)(2,1)S(1)}, u32[]{:S(2)}, u32[]{:S(2)}) collective-permute-start(bf16[64,256]{1,0:T(8,128)(2,1)S(1)} %get-tuple-element.32), channel_id=1, source_target_pairs={{0,2},{1,3},{2,0},{3,1},{4,6},{5,7},{6,4},{7,5},{8,10},{9,11},{10,... | collective-permute-start | bytes 98312 | tf_op jit(solution)/shard_map/ppermute | solution.py:165
  20.4 3.8 %collective-permute-start.11 = (bf16[64,256]{1,0:T(8,128)(2,1)S(1)}, bf16[64,256]{1,0:T(8,128)(2,1)S(1)}, u32[]{:S(2)}, u32[]{:S(2)}) collective-permute-start(bf16[64,256]{1,0:T(8,128)(2,1)S(1)} %get-tuple-element.33), channel_id=1, source_target_pairs={{0,3},{1,2},{2,1},{3,0},{4,7},{5,6},{6,5},{7,4},{8,11},{9,10},{10,... | collective-permute-start | bytes 98312 | tf_op jit(solution)/shard_map/ppermute | solution.py:165
  22.6 1.5 %collective-permute-start.9 = (bf16[192,256]{1,0:T(8,128)(2,1)S(1)}, bf16[192,256]{1,0:T(8,128)(2,1)S(1)}, u32[]{:S(2)}, u32[]{:S(2)}) collective-permute-start(bf16[192,256]{1,0:T(8,128)(2,1)S(1)} %get-tuple-element.30), channel_id=1, source_target_pairs={{0,1},{1,0},{2,3},{3,2},{4,5},{5,4},{6,7},{7,6},{8,9},{9,8},{10,11... | collective-permute-start | bytes 294920 | tf_op jit(solution)/shard_map/ppermute | solution.py:165
  24.2 4.9 %collective-permute-start.14 = (bf16[64,256]{1,0:T(8,128)(2,1)S(1)}, bf16[64,256]{1,0:T(8,128)(2,1)S(1)}, u32[]{:S(2)}, u32[]{:S(2)}) collective-permute-start(bf16[64,256]{1,0:T(8,128)(2,1)S(1)} %grad_col.1.refs_1_), channel_id=1, source_target_pairs={{0,12},{4,8},{8,4},{12,0},{16,28},{20,24},{24,20},{28,16},{1,13},{... | collective-permute-start | bytes 98312 | tf_op jit(solution)/shard_map/ppermute | solution.py:165
  26.8 3.9 %collective-permute-start.13 = (bf16[64,256]{1,0:T(8,128)(2,1)S(1)}, bf16[64,256]{1,0:T(8,128)(2,1)S(1)}, u32[]{:S(2)}, u32[]{:S(2)}) collective-permute-start(bf16[64,256]{1,0:T(8,128)(2,1)S(1)} %grad_col.1.refs_1_), channel_id=1, source_target_pairs={{0,8},{4,12},{8,0},{12,4},{16,24},{20,28},{24,16},{28,20},{1,9},{5... | collective-permute-start | bytes 98312 | tf_op jit(solution)/shard_map/ppermute | solution.py:165
  28.1 3.9 %collective-permute-start.12 = (bf16[64,256]{1,0:T(8,128)(2,1)S(1)}, bf16[64,256]{1,0:T(8,128)(2,1)S(1)}, u32[]{:S(2)}, u32[]{:S(2)}) collective-permute-start(bf16[64,256]{1,0:T(8,128)(2,1)S(1)} %grad_col.1.refs_1_), channel_id=1, source_target_pairs={{0,4},{4,0},{8,12},{12,8},{16,20},{20,16},{24,28},{28,24},{1,5},{5... | collective-permute-start | bytes 98312 | tf_op jit(solution)/shard_map/ppermute | solution.py:165
  32.0 8.6 %copy-start.1 = (bf16[256,256]{1,0:T(8,128)(2,1)S(1)}, bf16[256,256]{1,0:T(8,128)(2,1)}, u32[]{:S(2)}) copy-start(bf16[256,256]{1,0:T(8,128)(2,1)} %weight_ref.1) | copy-start | bytes 393220
  32.0 6.6 %collective-permute-start.15 = (bf16[192,256]{1,0:T(8,128)(2,1)S(1)}, bf16[192,256]{1,0:T(8,128)(2,1)S(1)}, u32[]{:S(2)}, u32[]{:S(2)}) collective-permute-start(bf16[192,256]{1,0:T(8,128)(2,1)S(1)} %grad_near.1.held_ref), channel_id=1, source_target_pairs={{0,16},{4,20},{8,24},{12,28},{16,0},{20,4},{24,8},{28,12},{1,17},{... | collective-permute-start | bytes 294920 | tf_op jit(solution)/shard_map/ppermute | solution.py:165
  33.8 6.8 %collective-permute-start.16 = (bf16[128,256]{1,0:T(8,128)(2,1)S(1)}, bf16[128,256]{1,0:T(8,128)(2,1)S(1)}, u32[]{:S(2)}, u32[]{:S(2)}) collective-permute-start(bf16[128,256]{1,0:T(8,128)(2,1)S(1)} %get-tuple-element.36.refs_5_), channel_id=1, source_target_pairs={{0,2},{1,3},{2,0},{3,1},{4,6},{5,7},{6,4},{7,5},{8,10},{9,11},{10,... | collective-permute-start | bytes 196616 | tf_op jit(solution)/shard_map/ppermute | solution.py:165
  34.7 5.9 %collective-permute-start.17 = (bf16[128,256]{1,0:T(8,128)(2,1)S(1)}, bf16[128,256]{1,0:T(8,128)(2,1)S(1)}, u32[]{:S(2)}, u32[]{:S(2)}) collective-permute-start(bf16[128,256]{1,0:T(8,128)(2,1)S(1)} %get-tuple-element.37.refs_6_), channel_id=1, source_target_pairs={{0,3},{1,2},{2,1},{3,0},{4,7},{5,6},{6,5},{7,4},{8,11},{9,10},{10,... | collective-permute-start | bytes 196616 | tf_op jit(solution)/shard_map/ppermute | solution.py:165
  38.7 3.5 %collective-permute-start.20 = (bf16[64,256]{1,0:T(8,128)(2,1)S(1)}, bf16[64,256]{1,0:T(8,128)(2,1)S(1)}, u32[]{:S(2)}, u32[]{:S(2)}) collective-permute-start(bf16[64,256]{1,0:T(8,128)(2,1)S(1)} %grad_row.1.refs_0_), channel_id=1, source_target_pairs={{0,3},{1,2},{2,1},{3,0},{4,7},{5,6},{6,5},{7,4},{8,11},{9,10},{10,... | collective-permute-start | bytes 98312 | tf_op jit(solution)/shard_map/ppermute | solution.py:165
  38.8 4.1 %collective-permute-start.19 = (bf16[64,256]{1,0:T(8,128)(2,1)S(1)}, bf16[64,256]{1,0:T(8,128)(2,1)S(1)}, u32[]{:S(2)}, u32[]{:S(2)}) collective-permute-start(bf16[64,256]{1,0:T(8,128)(2,1)S(1)} %grad_row.1.refs_0_), channel_id=1, source_target_pairs={{0,2},{1,3},{2,0},{3,1},{4,6},{5,7},{6,4},{7,5},{8,10},{9,11},{10,... | collective-permute-start | bytes 98312 | tf_op jit(solution)/shard_map/ppermute | solution.py:165
  40.0 2.8 %collective-permute-start.18 = (bf16[64,256]{1,0:T(8,128)(2,1)S(1)}, bf16[64,256]{1,0:T(8,128)(2,1)S(1)}, u32[]{:S(2)}, u32[]{:S(2)}) collective-permute-start(bf16[64,256]{1,0:T(8,128)(2,1)S(1)} %grad_row.1.refs_0_), channel_id=1, source_target_pairs={{0,1},{1,0},{2,3},{3,2},{4,5},{5,4},{6,7},{7,6},{8,9},{9,8},{10,11... | collective-permute-start | bytes 98312 | tf_op jit(solution)/shard_map/ppermute | solution.py:165
